TPU v7x, 512 devices: a whole 4x4x16 slice. The times are simulated.
512 devices in a mesh: seq: 64 (over z_lo, y, core), head: 8 (over z_hi, x).
Axes of the slice: x: 4, y: 4, z: 16 (z_hi: 2, z_lo: 8; z = z_hi * 8 + z_lo), core: 2. Of those that a mesh axis runs over, the one named last changes fastest.
Arguments:
- queries: bfloat16 [65536, 2048], P('seq', 'head'), may hold values from -5 to 5
- keys: bfloat16 [65536, 2048], P('seq', 'head'), may hold values from -5 to 5
- values: bfloat16 [65536, 2048], P('seq', 'head'), may hold values from -6.5 to 6.5
- out_grad: bfloat16 [65536, 2048], P('seq', 'head'), may hold values from -6 to 6
Outputs:
- normed: bfloat16 [65536, 2048], P('seq', 'head')
- grad_queries: bfloat16 [65536, 2048], P('seq', 'head')
- grad_keys: bfloat16 [65536, 2048], P('seq', 'head')
- grad_values: bfloat16 [65536, 2048], P('seq', 'head')
- whole_level_grads: float32 [2, 512, 2048], P(None, 'seq', 'head')
All inputs are finite; a program needn't handle non-finite values.
Results may differ from a plain program's by a relative error of at most 0.03.
Values may be sent and summed in bfloat16 or wider, within the bound.
No kernel may reach another device: no remote copies, remote signals or barrier semaphores. Data moves between devices by JAX's collectives and lax.ppermute only.
A program may use at most 64 MiB of HBM per device.

v0:
```python
import jax
import jax.numpy as jnp
from jax import lax
from jax.sharding import PartitionSpec as P

H = 16
HD = 128
KEPT_PER_SEGMENT = 512
BLOCKS_PER_SPAN = 4


NEG = -1e30
EPS = 1e-05


def shifted(x, axis, by):
    size = lax.axis_size(axis)
    pairs = [(i, i + by) for i in range(size) if 0 <= i + by < size]
    return lax.ppermute(x, axis, pairs)


def level_forward(query_matrix, key_matrix, value_matrix, allowed):
    multiplier = HD ** (-0.5)
    attention_logits = (
        jnp.einsum("bqhd,bkhd->bhqk", query_matrix, key_matrix, preferred_element_type=jnp.float32)
        * multiplier
    )
    attention_logits = jnp.where(allowed, attention_logits, NEG)
    row_max = jnp.max(attention_logits, axis=-1)
    weight_tensors = jnp.exp(attention_logits - row_max[..., None])
    row_sum = jnp.sum(weight_tensors, axis=-1)
    blended_rows = jnp.einsum(
        "bhqk,bkhd->bqhd",
        weight_tensors.astype(jnp.bfloat16),
        value_matrix,
        preferred_element_type=jnp.float32,
    )
    return (row_max, row_sum, blended_rows)


def level_probs(
    query_matrix, key_matrix, value_matrix, row_gradients, log_total, delta_rows, allowed
):
    multiplier = HD ** (-0.5)
    attention_logits = (
        jnp.einsum("bqhd,bkhd->bhqk", query_matrix, key_matrix, preferred_element_type=jnp.float32)
        * multiplier
    )
    attention_logits = jnp.where(allowed, attention_logits, NEG)
    softmax_weights = jnp.exp(attention_logits - log_total[..., None])
    probability_gradient = jnp.einsum(
        "bqhd,bkhd->bhqk", row_gradients, value_matrix, preferred_element_type=jnp.float32
    )
    logit_gradient = softmax_weights * (probability_gradient - delta_rows[..., None])
    return (softmax_weights.astype(jnp.bfloat16), logit_gradient.astype(jnp.bfloat16))


def level_backward(
    query_matrix, key_matrix, value_matrix, row_gradients, log_total, delta_rows, allowed
):
    multiplier = HD ** (-0.5)
    softmax_weights, logit_gradient = level_probs(
        query_matrix, key_matrix, value_matrix, row_gradients, log_total, delta_rows, allowed
    )
    query_gradient = (
        jnp.einsum(
            "bhqk,bkhd->bqhd", logit_gradient, key_matrix, preferred_element_type=jnp.float32
        )
        * multiplier
    )
    key_gradient = (
        jnp.einsum(
            "bhqk,bqhd->bkhd", logit_gradient, query_matrix, preferred_element_type=jnp.float32
        )
        * multiplier
    )
    value_gradient = jnp.einsum(
        "bhqk,bqhd->bkhd", softmax_weights, row_gradients, preferred_element_type=jnp.float32
    )
    return (query_gradient, key_gradient, value_gradient)


def pick_rows(row_block, chosen):
    spacing_step = chosen.shape[0]
    grouped = row_block.reshape(
        row_block.shape[0] // spacing_step, spacing_step, row_block.shape[1], row_block.shape[2]
    )
    picked = jnp.einsum(
        "rjhd,jh->rhd", grouped, chosen.astype(row_block.dtype), preferred_element_type=jnp.float32
    )
    return picked.astype(row_block.dtype)


def pick_stat(statistic, chosen):
    spacing_step = chosen.shape[0]
    grouped = statistic.reshape(
        statistic.shape[0] // spacing_step, spacing_step, statistic.shape[1]
    )
    return jnp.sum(jnp.where(chosen[None], grouped, 0.0), axis=1)


def spread_rows(row_block, chosen):
    spacing_step = chosen.shape[0]
    widened = row_block[:, None] * chosen.astype(jnp.float32)[None, :, :, None]
    return widened.reshape(
        row_block.shape[0] * spacing_step, row_block.shape[1], row_block.shape[2]
    )


def spread_stat(statistic, chosen, filler):
    widened = jnp.where(chosen[None], statistic[:, None, :], filler)
    return widened.reshape(statistic.shape[0] * chosen.shape[0], statistic.shape[1])


def row_totals(first_sum, second_sum):
    return lax.psum((first_sum, second_sum), "head")


def local(queries, keys, values, out_grad):
    sequence_count = lax.axis_size("seq")
    seq_index = lax.axis_index("seq")
    head_index = lax.axis_index("head")
    token_inputs = queries.shape[0]
    local_heads = queries.shape[1] // HD
    model_width = H * HD
    multiplier = HD ** (-0.5)
    blocks = token_inputs // KEPT_PER_SEGMENT
    central_spacing = BLOCKS_PER_SPAN * token_inputs // KEPT_PER_SEGMENT
    distant_spacing = token_inputs * sequence_count // KEPT_PER_SEGMENT
    rows_mid = KEPT_PER_SEGMENT // BLOCKS_PER_SPAN
    rows_far = KEPT_PER_SEGMENT // sequence_count
    query_all = queries.reshape(token_inputs, local_heads, HD)
    key_all = keys.reshape(token_inputs, local_heads, HD)
    value_all = values.reshape(token_inputs, local_heads, HD)
    head_numbers = head_index * local_heads + jnp.arange(local_heads, dtype=jnp.int32)
    picked_central = (
        jnp.arange(central_spacing, dtype=jnp.int32)[:, None]
        == (head_numbers % central_spacing)[None, :]
    )
    picked_distant = (
        jnp.arange(distant_spacing, dtype=jnp.int32)[:, None]
        == (head_numbers % distant_spacing)[None, :]
    )
    causal = jnp.arange(KEPT_PER_SEGMENT)[:, None] >= jnp.arange(KEPT_PER_SEGMENT)[None, :]
    near_shape = (blocks, KEPT_PER_SEGMENT, local_heads, HD)
    near_query = query_all.reshape(near_shape)
    near_key = key_all.reshape(near_shape)
    near_value = value_all.reshape(near_shape)
    near_max, near_sum, near_out = level_forward(
        near_query, near_key, near_value, causal[None, None]
    )
    near_max = near_max.transpose(0, 2, 1).reshape(token_inputs, local_heads)
    near_sum = near_sum.transpose(0, 2, 1).reshape(token_inputs, local_heads)
    near_out = near_out.reshape(token_inputs, local_heads, HD)
    mid_query = pick_rows(query_all, picked_central)
    mid_key = pick_rows(key_all, picked_central)
    mid_value = pick_rows(value_all, picked_central)
    earlier_keys = []
    earlier_values = []
    for distance in range(BLOCKS_PER_SPAN - 1, 0, -1):
        moved_pair = shifted((mid_key, mid_value), "seq", distance)
        earlier_keys.append(moved_pair[0])
        earlier_values.append(moved_pair[1])
    mid_keys = jnp.concatenate(earlier_keys + [mid_key], 0)
    mid_values = jnp.concatenate(earlier_values + [mid_value], 0)
    key_slot = jnp.arange(KEPT_PER_SEGMENT, dtype=jnp.int32)
    key_source = seq_index - (BLOCKS_PER_SPAN - 1) + key_slot // rows_mid
    key_place = (seq_index - (BLOCKS_PER_SPAN - 1)) * rows_mid + key_slot
    query_place = seq_index * rows_mid + jnp.arange(rows_mid, dtype=jnp.int32)
    mid_allowed = (key_source >= seq_index // BLOCKS_PER_SPAN * BLOCKS_PER_SPAN)[None, :] & (
        key_place[None, :] <= query_place[:, None]
    )
    mid_max, mid_sum, mid_out = level_forward(
        mid_query[None], mid_keys[None], mid_values[None], mid_allowed[None, None]
    )
    mid_max = spread_stat(mid_max[0].T, picked_central, NEG)
    mid_sum = spread_stat(mid_sum[0].T, picked_central, 0.0)
    mid_out = spread_rows(mid_out[0], picked_central)
    far_query = pick_rows(query_all, picked_distant)
    far_key = pick_rows(key_all, picked_distant)
    far_value = pick_rows(value_all, picked_distant)
    far_keys, far_values = (
        lax.all_gather(far_key, "seq", axis=0, tiled=True),
        lax.all_gather(far_value, "seq", axis=0, tiled=True),
    )
    far_place = seq_index * rows_far + jnp.arange(rows_far, dtype=jnp.int32)
    far_allowed = jnp.arange(KEPT_PER_SEGMENT, dtype=jnp.int32)[None, :] <= far_place[:, None]
    far_max, far_sum, far_out = level_forward(
        far_query[None], far_keys[None], far_values[None], far_allowed[None, None]
    )
    far_max = spread_stat(far_max[0].T, picked_distant, NEG)
    far_sum = spread_stat(far_sum[0].T, picked_distant, 0.0)
    far_out = spread_rows(far_out[0], picked_distant)
    overall_max = jnp.maximum(jnp.maximum(near_max, mid_max), far_max)
    near_scale = jnp.exp(near_max - overall_max)
    mid_scale = jnp.exp(mid_max - overall_max)
    far_scale = jnp.exp(far_max - overall_max)
    denominator = near_scale * near_sum + mid_scale * mid_sum + far_scale * far_sum
    merged = (
        near_scale[..., None] * near_out
        + mid_scale[..., None] * mid_out
        + far_scale[..., None] * far_out
    ) / denominator[..., None]
    log_total = overall_max + jnp.log(denominator)
    attention = merged.astype(jnp.bfloat16)
    attention_flat = attention.reshape(token_inputs, local_heads * HD).astype(jnp.float32)
    row_sum_all, row_square_all = row_totals(
        jnp.sum(attention_flat, axis=1), jnp.sum(attention_flat * attention_flat, axis=1)
    )
    row_mean = row_sum_all / model_width
    row_var = row_square_all / model_width - row_mean * row_mean
    row_scale = lax.rsqrt(row_var + EPS)
    centred = (attention_flat - row_mean[:, None]) * row_scale[:, None]
    normed = centred.astype(jnp.bfloat16)
    upstream = out_grad.astype(jnp.float32)
    grad_total, grad_cross = row_totals(
        jnp.sum(upstream, axis=1), jnp.sum(upstream * centred, axis=1)
    )
    grad_attention = (
        row_scale[:, None]
        * (
            upstream
            - grad_total[:, None] / model_width
            - centred * grad_cross[:, None] / model_width
        )
    ).astype(jnp.bfloat16)
    grad_attention = grad_attention.reshape(token_inputs, local_heads, HD)
    delta_rows = jnp.einsum(
        "thd,thd->th", grad_attention, attention, preferred_element_type=jnp.float32
    )
    near_lse = log_total.reshape(blocks, KEPT_PER_SEGMENT, local_heads).transpose(0, 2, 1)
    near_delta = delta_rows.reshape(blocks, KEPT_PER_SEGMENT, local_heads).transpose(0, 2, 1)
    near_dq, near_dk, near_dv = level_backward(
        near_query,
        near_key,
        near_value,
        grad_attention.reshape(near_shape),
        near_lse,
        near_delta,
        causal[None, None],
    )
    mid_grad = pick_rows(grad_attention, picked_central)
    mid_lse = pick_stat(log_total, picked_central).T[None]
    mid_delta = pick_stat(delta_rows, picked_central).T[None]
    mid_dq, mid_dk, mid_dv = level_backward(
        mid_query[None],
        mid_keys[None],
        mid_values[None],
        mid_grad[None],
        mid_lse,
        mid_delta,
        mid_allowed[None, None],
    )
    own_dk = mid_dk[0, KEPT_PER_SEGMENT - rows_mid :]
    own_dv = mid_dv[0, KEPT_PER_SEGMENT - rows_mid :]
    for distance in range(1, BLOCKS_PER_SPAN):
        first_row = (BLOCKS_PER_SPAN - 1 - distance) * rows_mid
        returned = shifted(
            (
                mid_dk[0, first_row : first_row + rows_mid],
                mid_dv[0, first_row : first_row + rows_mid],
            ),
            "seq",
            -distance,
        )
        own_dk = own_dk + returned[0]
        own_dv = own_dv + returned[1]
    far_grad = pick_rows(grad_attention, picked_distant)
    far_lse = pick_stat(log_total, picked_distant)
    far_delta = pick_stat(delta_rows, picked_distant)
    far_probs, far_scores = level_probs(
        far_query[None],
        far_keys[None],
        far_values[None],
        far_grad[None],
        far_lse.T[None],
        far_delta.T[None],
        far_allowed[None, None],
    )
    far_dq = (
        jnp.einsum(
            "bhqk,bkhd->bqhd", far_scores, far_keys[None], preferred_element_type=jnp.float32
        )[0]
        * multiplier
    )
    score_part = far_scores[0]
    prob_part = far_probs[0]
    key_part = (
        jnp.einsum("hqk,qhd->khd", score_part, far_query, preferred_element_type=jnp.float32)
        * multiplier
    )
    value_part = jnp.einsum("hqk,qhd->khd", prob_part, far_grad, preferred_element_type=jnp.float32)
    own_terms = lax.psum_scatter(
        jnp.stack([key_part, value_part], 1).reshape(
            rows_far * lax.axis_size("seq"), 2, local_heads * HD
        ),
        "seq",
        scatter_dimension=0,
        tiled=True,
    )
    far_dk = own_terms[:, 0].reshape(rows_far, local_heads, HD)
    far_dv = own_terms[:, 1].reshape(rows_far, local_heads, HD)
    whole_level_grads = jnp.stack(
        [far_dk.reshape(rows_far, local_heads * HD), far_dv.reshape(rows_far, local_heads * HD)], 0
    )
    grad_queries = (
        near_dq.reshape(token_inputs, local_heads, HD)
        + spread_rows(mid_dq[0], picked_central)
        + spread_rows(far_dq, picked_distant)
    )
    grad_keys = (
        near_dk.reshape(token_inputs, local_heads, HD)
        + spread_rows(own_dk, picked_central)
        + spread_rows(far_dk, picked_distant)
    )
    grad_values = (
        near_dv.reshape(token_inputs, local_heads, HD)
        + spread_rows(own_dv, picked_central)
        + spread_rows(far_dv, picked_distant)
    )
    flat_shape = (token_inputs, local_heads * HD)
    return (
        normed,
        grad_queries.reshape(flat_shape).astype(jnp.bfloat16),
        grad_keys.reshape(flat_shape).astype(jnp.bfloat16),
        grad_values.reshape(flat_shape).astype(jnp.bfloat16),
        whole_level_grads,
    )


def solution(mesh):
    return jax.shard_map(
        local,
        mesh=mesh,
        in_specs=(P("seq", "head"), P("seq", "head"), P("seq", "head"), P("seq", "head")),
        out_specs=(
            P("seq", "head"),
            P("seq", "head"),
            P("seq", "head"),
            P("seq", "head"),
            P(None, "seq", "head"),
        ),
        check_vma=False,
    )
```

profile of v0, /device:TPU:1, one launch (start us, length us, event | category | flops | bytes accessed | tf_op | source)
XLA Modules:
  0.0 860.9 jit_solution(9227576665790016787)
XLA Ops:
  9.9 6.8 collective-permute-start
  16.7 2.3 collective-permute-start.1
  19.0 1.9 collective-permute-start.2
  23.0 5.2 collective-permute-start.3
  28.2 3.2 collective-permute-start.4
  38.8 115.6 %all_gather.6 = bf16[512,2,128]{2,0,1:T(8,128)(2,1)S(1)} all-gather(bf16[8,2,128]{2,0,1:T(8,128)(2,1)S(1)} %convert_bitcast_fusion.2), channel_id=1, replica_groups=mesh['seq'=64,'head'=8] {'seq'}, dimensions={0}, use_global_device_ids=true | all-gather | bytes 266240 | tf_op jit(solution)/shard_map/all_gather | solution.py:183
  154.9 113.1 %all_gather.7 = bf16[512,2,128]{2,0,1:T(8,128)(2,1)S(1)} all-gather(bf16[8,2,128]{2,0,1:T(8,128)(2,1)S(1)} %convert_bitcast_fusion.1), channel_id=1, replica_groups=mesh['seq'=64,'head'=8] {'seq'}, dimensions={0}, use_global_device_ids=true | all-gather | bytes 266240 | tf_op jit(solution)/shard_map/all_gather | solution.py:184
  268.6 1.9 fusion.3
  270.6 2.0 copy-done.3
  283.2 3.4 collective-permute-start.5
  292.6 6.2 convert_reduce_fusion.1
  307.7 43.5 %all-reduce.1 = (f32[1024]{0:T(1024)}, f32[1024]{0:T(1024)}) all-reduce(f32[1024]{0:T(1024)} %bitcast.469, f32[1024]{0:T(1024)} %bitcast.468), channel_id=1, replica_groups=mesh['seq'=64,'head'=8] {'head'}, use_global_device_ids=true, to_apply=%region_9.10 | all-reduce | flops 2048 | bytes 16384 | tf_op jit(solution)/shard_map/psum | solution.py:116
  352.0 2.2 mul.433.clone
  360.8 2.6 convert_reduce_fusion
  363.5 30.3 %all-reduce = (f32[1024]{0:T(1024)S(1)}, f32[1024]{0:T(1024)S(1)}) all-reduce(f32[1024]{0:T(1024)} %get-tuple-element.6, f32[1024]{0:T(1024)} %get-tuple-element.5), channel_id=1, replica_groups=mesh['seq'=64,'head'=8] {'head'}, use_global_device_ids=true, to_apply=%region_13.14 | all-reduce | flops 2048 | bytes 16384 | tf_op jit(solution)/shard_map/psum | solution.py:116
  393.7 2.9 fusion.36
  399.9 2.0 copy.246
  401.9 3.9 multiply_reduce_fusion
  405.9 4.0 multiply_convert_fusion
  410.0 1.9 fusion.23
  420.0 2.0 copy.243
  423.1 2.3 pad_maximum_fusion
  428.6 2.0 copy.222
  430.6 3.0 copy.241
  435.5 8.9 %collective-permute-start.6 = (f32[128,2,128]{0,2,1:T(8,128)}, f32[128,2,128]{0,2,1:T(8,128)}, u32[]{:S(2)}, u32[]{:S(2)}) collective-permute-start(f32[128,2,128]{0,2,1:T(8,128)} %get-tuple-element.35), channel_id=1, source_target_pairs={{8,0},{16,8},{24,16},{32,24},{40,32},{48,40},{56,48},{64,56},{72,6... | collective-permute-start | bytes 393224 | tf_op jit(solution)/shard_map/ppermute | solution.py:19
  447.0 1.9 fusion.28
  455.5 4.6 fusion.19
  460.1 2.3 copy.248
  462.6 1.9 collective-permute-start.9
  465.8 4.5 collective-permute-done.9
  473.1 375.2 %reduce-scatter.2.cloned.1.call-done = f32[8,2,256]{2,0,1:T(8,128)} async-done(((f32[512,2,256]{2,0,1:T(8,128)}), f32[8,2,256]{2,0,1:T(8,128)}) %reduce-scatter.2.cloned.1.call-update) | async-done | bytes 16400 | tf_op jit(solution)/shard_map/reduce_scatter | solution.py:293
  850.4 3.6 fusion.39
  (265 shorter events, 78.3 us)
Async XLA Ops:
  7.2 28.9 %copy-start.1 = (bf16[1024,256]{1,0:T(8,128)(2,1)S(1)}, bf16[1024,256]{1,0:T(8,128)(2,1)}, u32[]{:S(2)}) copy-start(bf16[1024,256]{1,0:T(8,128)(2,1)} %param.5) | copy-start | bytes 1572868
  7.2 29.0 %copy-start.2 = (bf16[1024,256]{1,0:T(8,128)(2,1)S(1)}, bf16[1024,256]{1,0:T(8,128)(2,1)}, u32[]{:S(2)}) copy-start(bf16[1024,256]{1,0:T(8,128)(2,1)} %param.6) | copy-start | bytes 1572868
  7.2 28.7 %copy-start = (bf16[1024,256]{1,0:T(8,128)(2,1)S(1)}, bf16[1024,256]{1,0:T(8,128)(2,1)}, u32[]{:S(2)}) copy-start(bf16[1024,256]{1,0:T(8,128)(2,1)} %param.4) | copy-start | bytes 1572868
  7.2 841.1 %reduce-scatter.2.cloned.1.call-start = ((), (), s32[]{:S(2)}) async-start(), calls=%async_computation.1 | async-start | bytes 1064960 | tf_op jit(solution)/shard_map/reduce_scatter | solution.py:293
  7.9 30.9 %copy-start.32 = (pred[8,2,1,1]{0,1,2,3:T(4,128)(4,1)}, pred[8,2,1,1]{0,1,2,3:T(4,128)(4,1)S(1)}, u32[]{:S(2)}) copy-start(pred[8,2,1,1]{0,1,2,3:T(4,128)(4,1)S(1)} %get-tuple-element.51) | copy-start | bytes 52
  9.9 273.3 %collective-permute-start = (bf16[128,2,128]{2,0,1:T(8,128)(2,1)}, bf16[128,2,128]{2,0,1:T(8,128)(2,1)}, u32[]{:S(2)}, u32[]{:S(2)}) collective-permute-start(bf16[128,2,128]{2,0,1:T(8,128)(2,1)} %convert_bitcast_fusion), channel_id=1, source_target_pairs={{0,24},{8,32},{16,40},{24,48},{32,56},{40,64},{48,72},{56,80},{64,... | collective-permute-start | bytes 196616 | tf_op jit(solution)/shard_map/ppermute | solution.py:19
  16.7 269.9 %collective-permute-start.1 = (bf16[128,2,128]{2,0,1:T(8,128)(2,1)}, bf16[128,2,128]{2,0,1:T(8,128)(2,1)}, u32[]{:S(2)}, u32[]{:S(2)}) collective-permute-start(bf16[128,2,128]{2,0,1:T(8,128)(2,1)} %convert_bitcast_fusion), channel_id=1, source_target_pairs={{0,16},{8,24},{16,32},{24,40},{32,48},{40,56},{48,64},{56,72},{64,... | collective-permute-start | bytes 196616 | tf_op jit(solution)/shard_map/ppermute | solution.py:19
  19.0 267.6 %collective-permute-start.2 = (bf16[128,2,128]{2,0,1:T(8,128)(2,1)}, bf16[128,2,128]{2,0,1:T(8,128)(2,1)}, u32[]{:S(2)}, u32[]{:S(2)}) collective-permute-start(bf16[128,2,128]{2,0,1:T(8,128)(2,1)} %convert_bitcast_fusion), channel_id=1, source_target_pairs={{0,8},{8,16},{16,24},{24,32},{32,40},{40,48},{48,56},{56,64},{64,7... | collective-permute-start | bytes 196616 | tf_op jit(solution)/shard_map/ppermute | solution.py:19
  23.0 266.0 %collective-permute-start.3 = (bf16[128,2,128]{0,2,1:T(8,128)(2,1)}, bf16[128,2,128]{0,2,1:T(8,128)(2,1)}, u32[]{:S(2)}, u32[]{:S(2)}) collective-permute-start(bf16[128,2,128]{0,2,1:T(8,128)(2,1)} %fusion.99), channel_id=1, source_target_pairs={{0,24},{8,32},{16,40},{24,48},{32,56},{40,64},{48,72},{56,80},{64,... | collective-permute-start | bytes 196616 | tf_op jit(solution)/shard_map/ppermute | solution.py:19
  28.2 260.8 %collective-permute-start.4 = (bf16[128,2,128]{0,2,1:T(8,128)(2,1)}, bf16[128,2,128]{0,2,1:T(8,128)(2,1)}, u32[]{:S(2)}, u32[]{:S(2)}) collective-permute-start(bf16[128,2,128]{0,2,1:T(8,128)(2,1)} %fusion.99), channel_id=1, source_target_pairs={{0,16},{8,24},{16,32},{24,40},{32,48},{40,56},{48,64},{56,72},{64,... | collective-permute-start | bytes 196616 | tf_op jit(solution)/shard_map/ppermute | solution.py:19
  36.1 234.5 %copy-start.4 = (bf16[2,512,2,128]{3,2,1,0:T(2,128)(2,1)}, bf16[2,512,2,128]{3,2,1,0:T(2,128)(2,1)S(1)}, u32[]{:S(2)}) copy-start(bf16[2,512,2,128]{3,2,1,0:T(2,128)(2,1)S(1)} %reshape_reshape.36) | copy-start | bytes 1572868
  36.2 234.4 %copy-start.6 = (bf16[2,512,2,128]{3,2,1,0:T(2,128)(2,1)}, bf16[2,512,2,128]{3,2,1,0:T(2,128)(2,1)S(1)}, u32[]{:S(2)}) copy-start(bf16[2,512,2,128]{3,2,1,0:T(2,128)(2,1)S(1)} %reshape_reshape.37) | copy-start | bytes 1572868
  38.6 229.6 %copy-start.34 = (pred[128,2,1,1]{0,1,2,3:T(4,128)(4,1)}, pred[128,2,1,1]{0,1,2,3:T(4,128)(4,1)S(1)}, u32[]{:S(2)}) copy-start(pred[128,2,1,1]{0,1,2,3:T(4,128)(4,1)S(1)} %get-tuple-element.54) | copy-start | bytes 772
  38.8 233.7 %copy-start.14 = (pred[512,512]{0,1:T(8,128)(4,1)S(1)}, pred[512,512]{0,1:T(8,128)(4,1)}, u32[]{:S(2)}) copy-start(pred[512,512]{0,1:T(8,128)(4,1)} %iota_compare_fusion) | copy-start | bytes 786436
  268.2 12.8 %copy-start.38 = (f32[2,8]{1,0:T(2,128)}, f32[2,8]{1,0:T(2,128)S(1)}, u32[]{:S(2)}) copy-start(f32[2,8]{1,0:T(2,128)S(1)} %get-tuple-element.58) | copy-start | bytes 196
  268.4 11.3 %copy-start.46 = (f32[2,8]{1,0:T(2,128)}, f32[2,8]{1,0:T(2,128)S(1)}, u32[]{:S(2)}) copy-start(f32[2,8]{1,0:T(2,128)S(1)} %fusion.105) | copy-start | bytes 196
  272.6 15.6 %copy-start.54 = (pred[8,2]{0,1:T(4,128)(4,1)S(1)}, pred[8,2]{0,1:T(4,128)(4,1)}, u32[]{:S(2)}) copy-start(pred[8,2]{0,1:T(4,128)(4,1)} %get-tuple-element.52) | copy-start | bytes 52
  276.5 11.7 %copy-start.21 = (bf16[2,1,128,128]{2,3,0,1:T(8,128)(2,1)}, bf16[2,1,128,128]{2,3,0,1:T(8,128)(2,1)S(1)}, u32[]{:S(2)}) copy-start(bf16[2,1,128,128]{2,3,0,1:T(8,128)(2,1)S(1)} %copy.253) | copy-start | bytes 196612
  283.2 5.9 collective-permute-start.5
  287.9 10.9 %copy-start.10 = (f32[2,128,512]{2,1,0:T(8,128)}, f32[2,128,512]{2,1,0:T(8,128)S(1)}, u32[]{:S(2)}) copy-start(f32[2,128,512]{2,1,0:T(8,128)S(1)} %get-tuple-element.61) | copy-start | bytes 1572868
  352.0 8.8 %copy-start.36 = (f32[1024]{0:T(1024)}, f32[1024]{0:T(1024)S(1)}, u32[]{:S(2)}) copy-start(f32[1024]{0:T(1024)S(1)} %get-tuple-element.42) | copy-start | bytes 12292
  352.0 8.8 %copy-start.37 = (f32[1024]{0:T(1024)}, f32[1024]{0:T(1024)S(1)}, u32[]{:S(2)}) copy-start(f32[1024]{0:T(1024)S(1)} %get-tuple-element.43) | copy-start | bytes 12292
  352.0 7.5 copy-start.8
  413.6 12.8 %copy-start.41 = (f32[128,8,2]{0,1,2:T(8,128)S(1)}, f32[128,8,2]{0,1,2:T(8,128)}, u32[]{:S(2)}) copy-start(f32[128,8,2]{0,1,2:T(8,128)} %copy.228) | copy-start | bytes 24580
  415.1 12.3 %copy-start.11 = (f32[2,128,512]{2,1,0:T(8,128)S(1)}, f32[2,128,512]{2,1,0:T(8,128)}, u32[]{:S(2)}) copy-start(f32[2,128,512]{2,1,0:T(8,128)} %copy-done.10) | copy-start | bytes 1572868
  435.5 27.1 %collective-permute-start.6 = (f32[128,2,128]{0,2,1:T(8,128)}, f32[128,2,128]{0,2,1:T(8,128)}, u32[]{:S(2)}, u32[]{:S(2)}) collective-permute-start(f32[128,2,128]{0,2,1:T(8,128)} %get-tuple-element.35), channel_id=1, source_target_pairs={{8,0},{16,8},{24,16},{32,24},{40,32},{48,40},{56,48},{64,56},{72,6... | collective-permute-start | bytes 393224 | tf_op jit(solution)/shard_map/ppermute | solution.py:19
  444.4 20.1 %collective-permute-start.7 = (f32[128,2,128]{0,2,1:T(8,128)}, f32[128,2,128]{0,2,1:T(8,128)}, u32[]{:S(2)}, u32[]{:S(2)}) collective-permute-start(f32[128,2,128]{0,2,1:T(8,128)} %get-tuple-element.37), channel_id=1, source_target_pairs={{16,0},{24,8},{32,16},{40,24},{48,32},{56,40},{64,48},{72,56},{80,... | collective-permute-start | bytes 393224 | tf_op jit(solution)/shard_map/ppermute | solution.py:19
  445.7 18.8 %collective-permute-start.8 = (f32[128,2,128]{0,2,1:T(8,128)}, f32[128,2,128]{0,2,1:T(8,128)}, u32[]{:S(2)}, u32[]{:S(2)}) collective-permute-start(f32[128,2,128]{0,2,1:T(8,128)} %get-tuple-element.36), channel_id=1, source_target_pairs={{24,0},{32,8},{40,16},{48,24},{56,32},{64,40},{72,48},{80,56},{88,... | collective-permute-start | bytes 393224 | tf_op jit(solution)/shard_map/ppermute | solution.py:19
  452.9 12.9 %collective-permute-start.10 = (f32[128,2,128]{0,2,1:T(8,128)}, f32[128,2,128]{0,2,1:T(8,128)}, u32[]{:S(2)}, u32[]{:S(2)}) collective-permute-start(f32[128,2,128]{0,2,1:T(8,128)} %get-tuple-element.34), channel_id=1, source_target_pairs={{16,0},{24,8},{32,16},{40,24},{48,32},{56,40},{64,48},{72,56},{80,... | collective-permute-start | bytes 393224 | tf_op jit(solution)/shard_map/ppermute | solution.py:19
  454.2 8.2 copy-start.31
  454.2 11.6 %collective-permute-start.11 = (f32[128,2,128]{0,2,1:T(8,128)}, f32[128,2,128]{0,2,1:T(8,128)}, u32[]{:S(2)}, u32[]{:S(2)}) collective-permute-start(f32[128,2,128]{0,2,1:T(8,128)} %get-tuple-element.33), channel_id=1, source_target_pairs={{24,0},{32,8},{40,16},{48,24},{56,32},{64,40},{72,48},{80,56},{88,... | collective-permute-start | bytes 393224 | tf_op jit(solution)/shard_map/ppermute | solution.py:19
  462.6 7.7 collective-permute-start.9
  (40 other events, 187.5 us)
Sparse Core Ops, SparseCore 0:
  425.5 422.7 reduce-scatter.1
where the time goes:
time: 872 us; the launch traced here: 861 us
  waiting for transfers between devices  380 us (44%)
  blocking collectives  302 us (35%)
  local copies, waits for them, and re-layouts  58 us (7%)
  starting transfers between devices  38.9 us (4%)
  matrix products  37.5 us (4%)
  other arithmetic  29.2 us (3%)
  between operations  15.2 us (2%)
    reduce_scatter x1, waiting for transfers between devices, local(): lax.psum_scatter(jnp.stack([key_part, value_part], 1).reshape(rows_far *...  375 us
    all_gather x1, blocking collectives, local(): lax.all_gather(far_key, 'seq', axis=0, tiled=True)  116 us
    all_gather x1, blocking collectives, local(): lax.all_gather(far_value, 'seq', axis=0, tiled=True)  113 us
    psum x2, blocking collectives, row_totals(): return lax.psum((first_sum, second_sum), 'head')  73.8 us
    ppermute x12, starting transfers between devices, shifted(): return lax.ppermute(x, axis, pairs)  38.9 us
  transfers between devices with their start and end apart: 13, of which 2 were waited for; matrix products, arithmetic and copies ran while one was open for 6% of the time, Pallas kernels for 0%

commit v1 on v0

v1 whole, which is shorter than its diff:
```python
import jax
import jax.numpy as jnp
from jax import lax
from jax.experimental import pallas as pl
from jax.experimental.pallas import tpu as pltpu
from jax.sharding import PartitionSpec as P

H = 16
HD = 128
D = H * HD
TOK = 1024
SEG = 512
NEG = -1e30
EPS = 1e-05
SCALE = HD ** (-0.5)
BF = jnp.bfloat16
F32 = jnp.float32
VMEM = pl.BlockSpec(memory_space=pltpu.VMEM)
SMEM = pl.BlockSpec(memory_space=pltpu.SMEM)
PARAMS = pltpu.CompilerParams(vmem_limit_bytes=16 * 1024 * 1024)


def dot_nt(a, b):
    return lax.dot_general(a, b, (((1,), (1,)), ((), ())), preferred_element_type=F32)


def dot_nn(a, b):
    return lax.dot_general(a, b, (((1,), (0,)), ((), ())), preferred_element_type=F32)


def dot_tn(a, b):
    return lax.dot_general(a, b, (((0,), (0,)), ((), ())), preferred_element_type=F32)


def iota(shape, axis):
    return lax.broadcasted_iota(jnp.int32, shape, axis)


def cost(flops, bytes_accessed, transcendentals=0):
    return pl.CostEstimate(
        flops=flops, bytes_accessed=bytes_accessed, transcendentals=transcendentals
    )


def split3(x):
    hi = x.astype(BF)
    rest = x - hi.astype(F32)
    mid = rest.astype(BF)
    low = (rest - mid.astype(F32)).astype(BF)
    return hi.astype(F32), mid.astype(F32), low.astype(F32)


def select_kernel(idx, q_ref, k_ref, v_ref, mid_ref, far_ref, wide):
    far = []
    for j in range(2):
        head = idx[1] * 2 + j
        for a, ref in enumerate((k_ref, v_ref, q_ref)):
            slot = wide.at[j * 3 + a]
            slot[...] = ref[:, j * HD : (j + 1) * HD].astype(F32)
            mid = slot[pl.ds(lax.rem(head, 8), 128, stride=8), :]
            mid_ref[j * 128 : (j + 1) * 128, a * HD : (a + 1) * HD] = mid.astype(BF)
            far.append(slot[pl.ds(head, 8, stride=128), :])
    for a in range(3):
        both = jnp.concatenate([far[a], far[3 + a]], 0)
        far_ref[:, a * HD : (a + 1) * HD] = both.astype(BF)


def near_forward_kernel(q_ref, k_ref, v_ref, o_ref, lse_ref):
    for c in range(2):
        rows = slice(c * 256, (c + 1) * 256)
        n = (c + 1) * 256
        s = dot_nt(q_ref[rows, :], k_ref[:n, :]) * SCALE
        keep = iota((256, n), 1) <= iota((256, n), 0) + c * 256
        s = jnp.where(keep, s, NEG)
        top = jnp.max(s, axis=1, keepdims=True)
        p = jnp.exp(s - top)
        total = jnp.sum(p, axis=1, keepdims=True)
        o = dot_nn(p.astype(BF), v_ref[:n, :])
        o_ref[0, rows, :] = o / total
        lse_ref[0, rows, :] = jnp.broadcast_to(top + jnp.log(total), (256, HD))


def mid_slots(s, shape, axis):
    n = iota(shape, axis)
    pos = n // 128
    other = s ^ ((pos & 1) * 2 + (pos >> 1))
    return (other & 3) * 128 + (n & 127)


def mid_forward_kernel(idx, mid_ref, o_ref, lse_ref):
    s_idx = idx[0]
    key_slot = mid_slots(s_idx, (128, SEG), 1)
    query_slot = (s_idx & 3) * 128 + iota((128, SEG), 0)
    keep = key_slot <= query_slot
    for j in range(2):
        q = mid_ref[j * 128 : (j + 1) * 128, 2 * HD :]
        k = jnp.concatenate(
            [mid_ref[p * 256 + j * 128 : p * 256 + (j + 1) * 128, :HD] for p in range(4)], 0
        )
        v = jnp.concatenate(
            [mid_ref[p * 256 + j * 128 : p * 256 + (j + 1) * 128, HD : 2 * HD] for p in range(4)], 0
        )
        s = jnp.where(keep, dot_nt(q, k) * SCALE, NEG)
        top = jnp.max(s, axis=1, keepdims=True)
        p = jnp.exp(s - top)
        total = jnp.sum(p, axis=1, keepdims=True)
        o = dot_nn(p.astype(BF), v)
        o_ref[j * 128 : (j + 1) * 128, :] = o / total
        lse_ref[j * 128 : (j + 1) * 128, :] = jnp.broadcast_to(top + jnp.log(total), (128, HD))


def far_places(s):
    n, row = iota((16, 1024), 1), iota((16, 1024), 0)
    pos = n // 16
    flips = (pos & 1) * 32 + (pos & 2) * 8 + (pos & 4) * 2 + ((pos >> 3) & 3) * 2 + (pos >> 5)
    place = (s ^ flips) * 8 + (n & 7)
    return ((n >> 3) & 1) == (row >> 3), place, s * 8 + (row & 7)


def far_keep_forward(s):
    same_head, place, mine = far_places(s)
    return same_head & (place <= mine)


def far_keep_backward(s):
    same_head, place, mine = far_places(s)
    return same_head & (place >= mine)


def pre_kernel(
    idx, o0, lse0, o1, lse1, mid_o, mid_lse, g_ref, att_ref, lse_ref, stat_ref, far_ref, out_scr
):
    for j in range(2):
        head = idx[1] * 2 + j
        picked = pl.ds(lax.rem(head, 8), 128, stride=8)
        distant = pl.ds(head, 8, stride=128)
        own = slice(j * 128, (j + 1) * 128)
        so, sl = out_scr.at[j], lse_ref.at[j]
        so[:SEG, :], so[SEG:, :] = o0[j], o1[j]
        sl[:SEG, :], sl[SEG:, :] = lse0[j], lse1[j]
        l1, l2 = sl[picked, :], mid_lse[own, :]
        peak = jnp.maximum(l1, l2)
        e1, e2 = jnp.exp(l1 - peak), jnp.exp(l2 - peak)
        den = e1 + e2
        so[picked, :] = (e1 * so[picked, :] + e2 * mid_o[own, :]) / den
        sl[picked, :] = peak + jnp.log(den)
        far_ref[0, j * 8 : (j + 1) * 8, :] = so[distant, :]
        far_ref[1, j * 8 : (j + 1) * 8, :] = sl[distant, :]
    lane = iota((128, HD), 1)
    row = iota((128, HD), 0)
    for b in range(8):
        rows = slice(b * 128, (b + 1) * 128)
        at, g = [], []
        for j in range(2):
            a16 = out_scr[j, rows, :].astype(BF)
            att_ref[rows, j * HD : (j + 1) * HD] = a16
            at.append(jnp.where(row == idx[1] * 2 + j, 0.0, a16.astype(F32)))
            g.append(g_ref[rows, j * HD : (j + 1) * HD].astype(F32))
            out_scr[j, rows, :] = g[j]
        sums = (
            at[0] + at[1],
            at[0] * at[0] + at[1] * at[1],
            g[0] * at[0] + g[1] * at[1],
            g[0] + g[1],
        )
        block = jnp.zeros((128, HD), F32)
        for i, term in enumerate(sums):
            block = jnp.where(lane == i, jnp.sum(term, axis=1, keepdims=True), block)
        stat_ref[:, rows] = block.T[:4, :]
    for j in range(2):
        distant = pl.ds(idx[1] * 2 + j, 8, stride=128)
        far_ref[2, j * 8 : (j + 1) * 8, :] = out_scr.at[j][distant, :]


def norm_terms(total, squares, cross, g_total):
    mean = total / D
    rstd = lax.rsqrt(squares / D - mean * mean + EPS)
    return mean, rstd, g_total / D, rstd * (cross - mean * g_total) / D


def stat_pack(lse, delta, lane):
    pack = jnp.zeros(lane.shape, F32)
    for i, term in enumerate(split3(lse) + split3(delta)):
        pack = jnp.where(lane == i, term, pack)
    return pack


def far_forward_kernel(idx, far_all, far_in, stat_in, patch_ref, stat_ref, own_scr):
    s_idx = idx[0]
    q = far_all[:16, 2 * HD :]
    s = jnp.where(far_keep_forward(s_idx), dot_nt(q, far_all[:, :HD]) * SCALE, NEG)
    top = jnp.max(s, axis=1, keepdims=True)
    p = jnp.exp(s - top)
    total = jnp.sum(p, axis=1, keepdims=True)
    o3 = dot_nn(p.astype(BF), far_all[:, HD : 2 * HD]) / total
    l3 = top + jnp.log(total)
    o12, l12, g = far_in[0], far_in[1], far_in[2]
    peak = jnp.maximum(l12, l3)
    e12, e3 = jnp.exp(l12 - peak), jnp.exp(l3 - peak)
    den = e12 + e3
    at = ((e12 * o12 + e3 * o3) / den).astype(BF).astype(F32)
    patch_ref[0] = at
    patch_ref[1] = peak + jnp.log(den)
    lane, row = iota((16, HD), 1), iota((16, HD), 0)
    slot = (row & 7) * 16 + idx[1] * 2 + (row >> 3)
    for k, term in enumerate((at, at * at, g * at)):
        mine = jnp.sum(term, axis=1, keepdims=True)
        own_scr[k : k + 1, :] = jnp.sum(jnp.where(lane == slot, mine, 0.0), axis=0, keepdims=True)
    own_scr[3:4, :] = jnp.zeros((1, HD), F32)
    own = own_scr[...]
    for i in range(8):
        cols = slice(i * 128, (i + 1) * 128)
        mine = jnp.concatenate([own[:, i * 16 : (i + 1) * 16], jnp.zeros((4, HD - 16), F32)], 1)
        stat_ref[:, cols] = stat_in[:, cols] + mine


def far_grad_kernel(idx, stat_ref, far_in, patch_ref, pack_ref, tall_scr, col_scr):
    for i in range(8):
        tall_scr[i * 4 : (i + 1) * 4, :] = stat_ref[:, i * 128 : (i + 1) * 128]
    lane32 = iota((32, HD), 1)
    sums = [[], [], [], []]
    for j in range(2):
        cs = col_scr.at[j]
        chosen = jnp.where(lane32 == idx[1] * 2 + j, tall_scr[...], 0.0)
        cs[...] = jnp.broadcast_to(jnp.sum(chosen, axis=1, keepdims=True), (32, HD))
        for k in range(4):
            sums[k].append(cs[pl.ds(k, 8, stride=4), :])
    mean, rstd, sg, sgx = norm_terms(*(jnp.concatenate(pair, 0) for pair in sums))
    at = patch_ref[0]
    x = (at - mean) * rstd
    grad = (rstd * (far_in[2] - sg - x * sgx)).astype(BF)
    delta = jnp.sum(grad.astype(F32) * at, axis=1, keepdims=True)
    pack_ref[:, :HD] = grad
    delta = jnp.broadcast_to(delta, (16, HD))
    pack_ref[:, HD:] = stat_pack(patch_ref[1], delta, iota((16, HD), 1)).astype(BF)


def norm_kernel(
    idx,
    stat_ref,
    att_ref,
    g_ref,
    lse_in,
    patch_ref,
    normed_ref,
    grad_ref,
    delta_ref,
    lse_ref,
    mid_ref,
    att_scr,
    pack_scr,
):
    for j in range(2):
        distant = pl.ds(idx[1] * 2 + j, 8, stride=128)
        own = slice(j * 8, (j + 1) * 8)
        at, lse = att_scr.at[j], lse_ref.at[j]
        at[...] = att_ref[:, j * HD : (j + 1) * HD].astype(F32)
        at[distant, :] = patch_ref[0, own, :]
        lse[...] = lse_in[j]
        lse[distant, :] = patch_ref[1, own, :]
    lane = iota((128, HD), 1)
    for b in range(8):
        rows = slice(b * 128, (b + 1) * 128)
        stats = stat_ref[:, rows]
        terms = norm_terms(stats[0:1], stats[1:2], stats[2:3], stats[3:4])
        cols = jnp.concatenate(list(terms) + [jnp.zeros((124, HD), F32)], 0).T
        mean, rstd, sg, sgx = (cols[:, i : i + 1] for i in range(4))
        for j in range(2):
            at = att_scr[j, rows, :]
            x = (at - mean) * rstd
            normed_ref[rows, j * HD : (j + 1) * HD] = x.astype(BF)
            g = g_ref[rows, j * HD : (j + 1) * HD].astype(F32)
            grad = (rstd * (g - sg - x * sgx)).astype(BF)
            grad_ref[rows, j * HD : (j + 1) * HD] = grad
            grad = grad.astype(F32)
            delta = jnp.broadcast_to(jnp.sum(grad * at, axis=1, keepdims=True), (128, HD))
            delta_ref[j, rows, :] = delta
            att_scr[j, rows, :] = grad
            pack_scr[j, rows, :] = stat_pack(lse_ref[j, rows, :], delta, lane)
    for j in range(2):
        picked = pl.ds(lax.rem(idx[1] * 2 + j, 8), 128, stride=8)
        mid_ref[j * 128 : (j + 1) * 128, :HD] = att_scr.at[j][picked, :].astype(BF)
        mid_ref[j * 128 : (j + 1) * 128, HD:] = pack_scr.at[j][picked, :].astype(BF)


def near_backward_kernel(
    q_ref, k_ref, v_ref, g_ref, lse_ref, delta_ref, dq_ref, dk_ref, dv_ref
):
    for c in range(2):
        keys = slice(c * 256, (c + 1) * 256)
        rows = slice(c * 256, 512)
        n = 512 - c * 256
        q, g = q_ref[rows, :], g_ref[rows, :]
        k, v = k_ref[keys, :], v_ref[keys, :]
        lse = jnp.concatenate([lse_ref[0, rows, :]] * 2, 1)
        delta = jnp.concatenate([delta_ref[0, rows, :]] * 2, 1)
        s = dot_nt(q, k) * SCALE
        keep = iota((n, 256), 1) <= iota((n, 256), 0)
        p = jnp.exp(jnp.where(keep, s, NEG) - lse)
        ds = (p * (dot_nt(g, v) - delta)).astype(BF)
        p = p.astype(BF)
        dv_ref[0, keys, :] = dot_tn(p, g)
        dk_ref[0, keys, :] = dot_tn(ds, q) * SCALE
        dq = dot_nn(ds, k) * SCALE
        if c == 0:
            dq_ref[0, :, :] = dq
        else:
            dq_ref[0, rows, :] += dq


def query_grad_kernel(idx, dq0, dq1, mid_ref, far_ref, mid_g, far_g, out_ref, scr, far_scr):
    s_idx = idx[0]

    def stat_cols(pack):
        pack = pack.astype(F32)
        lse = pack[:, 0:1] + pack[:, 1:2] + pack[:, 2:3]
        delta = pack[:, 3:4] + pack[:, 4:5] + pack[:, 5:6]
        return lse, delta

    k_all, v_all = far_ref[:, :HD], far_ref[:, HD : 2 * HD]
    lse, delta = stat_cols(far_g[:, HD:])
    s = jnp.where(
        far_keep_forward(s_idx), dot_nt(far_ref[:16, 2 * HD :], k_all) * SCALE, NEG
    )
    p = jnp.exp(s - lse)
    ds = (p * (dot_nt(far_g[:, :HD], v_all) - delta)).astype(BF)
    far_dq = dot_nn(ds, k_all) * SCALE

    key_slot = mid_slots(s_idx, (128, SEG), 1)
    query_slot = (s_idx & 3) * 128 + iota((128, SEG), 0)
    keep = key_slot <= query_slot
    for j in range(2):
        head = idx[1] * 2 + j
        own = slice(j * 128, (j + 1) * 128)
        q = mid_ref[own, 2 * HD :]
        g = mid_g[own, :HD]
        lse, delta = stat_cols(mid_g[own, HD:])
        k = jnp.concatenate(
            [mid_ref[p * 256 + j * 128 : p * 256 + (j + 1) * 128, :HD] for p in range(4)], 0
        )
        v = jnp.concatenate(
            [mid_ref[p * 256 + j * 128 : p * 256 + (j + 1) * 128, HD : 2 * HD] for p in range(4)], 0
        )
        s = jnp.where(keep, dot_nt(q, k) * SCALE, NEG)
        p = jnp.exp(s - lse)
        ds = (p * (dot_nt(g, v) - delta)).astype(BF)
        fs = far_scr.at[j]
        fs[...] = dot_nn(ds, k) * SCALE
        spread = pl.ds(head // 8, 8, stride=16)
        fs[spread, :] = fs[spread, :] + far_dq[j * 8 : (j + 1) * 8]
        picked = pl.ds(lax.rem(head, 8), 128, stride=8)
        sc = scr.at[j]
        sc[:SEG, :], sc[SEG:, :] = dq0[j], dq1[j]
        sc[picked, :] = sc[picked, :] + fs[...]
        out_ref[:, j * HD : (j + 1) * HD] = sc[...].astype(BF)


def key_grad_kernel(
    idx,
    dk0,
    dk1,
    dv0,
    dv1,
    mid_ref,
    far_all,
    grads,
    dk_out,
    dv_out,
    whole_ref,
    scr,
    far_scr,
):
    s_idx = idx[0]
    lane = iota((8, HD), 1)
    row = iota((8, HD), 0)
    pick = ((row == lane // 3) & (lane < 6)).astype(F32).astype(BF)

    far_g = jnp.concatenate([grads[:512, :], grads[1024:1536, :]], 0)
    mid_g = jnp.concatenate([grads[512:1024, :], grads[1536:, :]], 0)
    stats = dot_nt(pick, far_g[:, HD:])
    lse, delta = stats[0:1], stats[1:2]
    keep = far_keep_backward(s_idx)
    k, v = far_all[:16, :HD], far_all[:16, HD : 2 * HD]
    q_all, g_all = far_all[:, 2 * HD :], far_g[:, :HD]
    s = jnp.where(keep, dot_nt(k, q_all) * SCALE, NEG)
    p = jnp.exp(s - lse)
    ds = (p * (dot_nt(v, g_all) - delta)).astype(BF)
    far_dk = dot_nn(ds, q_all) * SCALE
    far_dv = dot_nn(p.astype(BF), g_all)
    for j in range(2):
        whole_ref[0, :, j * HD : (j + 1) * HD] = far_dk[j * 8 : (j + 1) * 8]
        whole_ref[1, :, j * HD : (j + 1) * HD] = far_dv[j * 8 : (j + 1) * 8]

    stats = dot_nt(pick, mid_g[:, HD:])
    query_slot = mid_slots(s_idx, (128, SEG), 1)
    key_slot = (s_idx & 3) * 128 + iota((128, SEG), 0)
    keep = key_slot <= query_slot
    for j in range(2):
        head = idx[1] * 2 + j
        own = slice(j * 128, (j + 1) * 128)
        places = [slice(p * 256 + j * 128, p * 256 + (j + 1) * 128) for p in range(4)]
        k, v = mid_ref[own, :HD], mid_ref[own, HD : 2 * HD]
        q = jnp.concatenate([mid_ref[r, 2 * HD :] for r in places], 0)
        g = jnp.concatenate([mid_g[r, :HD] for r in places], 0)
        lse = jnp.concatenate([stats[0:1, r] for r in places], 1)
        delta = jnp.concatenate([stats[1:2, r] for r in places], 1)
        s = jnp.where(keep, dot_nt(k, q) * SCALE, NEG)
        p = jnp.exp(s - lse)
        ds = (p * (dot_nt(v, g) - delta)).astype(BF)
        mid_dk = dot_nn(ds, q) * SCALE
        mid_dv = dot_nn(p.astype(BF), g)
        spread = pl.ds(head // 8, 8, stride=16)
        picked = pl.ds(lax.rem(head, 8), 128, stride=8)
        for a, (mid, far, near0, near1, out) in enumerate(
            ((mid_dk, far_dk, dk0, dk1, dk_out), (mid_dv, far_dv, dv0, dv1, dv_out))
        ):
            fs, sc = far_scr.at[j * 2 + a], scr.at[j * 2 + a]
            fs[...] = mid
            fs[spread, :] = fs[spread, :] + far[j * 8 : (j + 1) * 8]
            sc[:SEG, :], sc[SEG:, :] = near0[j], near1[j]
            sc[picked, :] = sc[picked, :] + fs[...]
            out[:, j * HD : (j + 1) * HD] = sc[...].astype(BF)


def exchange(x, bit):
    return lax.ppermute(x, "seq", [(i, i ^ bit) for i in range(64)])


def head_exchange(x, bit):
    return lax.ppermute(x, "head", [(i, i ^ bit) for i in range(8)])


def round_of_y(x, to_pair):
    from_far = exchange(x, 4)
    from_pair = exchange(to_pair, 2)
    from_next = exchange(x, 6)
    return from_pair, from_far, from_next


def joined(a, b):
    return jnp.concatenate([a, b], 0)


def after(arrays):
    return lax.optimization_barrier(arrays)


def sds(shape, dtype):
    return jax.ShapeDtypeStruct(shape, dtype)


def local(queries, keys, values, out_grad):
    seq_index = lax.axis_index("seq")
    head_index = lax.axis_index("head")
    idx = jnp.stack([seq_index, head_index]).astype(jnp.int32)

    mid0, far0 = pl.pallas_call(
        select_kernel,
        out_shape=(sds((256, 384), BF), sds((16, 384), BF)),
        in_specs=[SMEM, VMEM, VMEM, VMEM],
        out_specs=(VMEM, VMEM),
        scratch_shapes=[pltpu.VMEM((6, TOK, HD), F32)],
        compiler_params=PARAMS,
        cost_estimate=cost(10**6, 2 * 10**6),
        name="select",
    )(idx, queries, keys, values)

    unit = pl.BlockSpec((SEG, HD), lambda b, j: (b, j))
    by_head = pl.BlockSpec((1, SEG, HD), lambda b, j: (j, b, 0))
    by_head_shape = sds((2, TOK, HD), F32)
    half = pl.BlockSpec((1, SEG, HD), lambda j: (j, 0, 0))
    half_shape = sds((2, SEG, HD), F32)

    def near_forward(block):
        part = pl.BlockSpec((SEG, HD), lambda j: (block, j))
        return pl.pallas_call(
            near_forward_kernel,
            grid=(2,),
            out_shape=(half_shape, half_shape),
            in_specs=[part, part, part],
            out_specs=(half, half),
            compiler_params=PARAMS,
            cost_estimate=cost(4 * 10**8, 2 * 10**6, 10**6),
            name=f"near_forward_{block}",
        )(queries, keys, values)

    mid1 = exchange(mid0, 2)
    far1 = exchange(far0, 32)
    near0 = near_forward(0)
    mid_two, far_two, near0 = after((joined(mid0, mid1), joined(far0, far1), near0))
    mid2 = exchange(mid_two, 1)
    far2 = exchange(far_two, 16)
    near1 = near_forward(1)
    far_four, near1 = after((joined(far_two, far2), near1))
    far4 = exchange(far_four, 8)
    mid_all = joined(mid_two, mid2)
    mid_o, mid_lse = pl.pallas_call(
        mid_forward_kernel,
        out_shape=(sds((256, HD), F32), sds((256, HD), F32)),
        in_specs=[SMEM, VMEM],
        out_specs=(VMEM, VMEM),
        compiler_params=PARAMS,
        cost_estimate=cost(2 * 10**8, 10**6, 10**5),
        name="mid_forward",
    )(idx, mid_all)

    att, lse12, stats, far_in = pl.pallas_call(
        pre_kernel,
        out_shape=(
            sds((TOK, 256), BF),
            by_head_shape,
            sds((4, TOK), F32),
            sds((3, 16, HD), F32),
        ),
        in_specs=[SMEM] + [VMEM] * 7,
        out_specs=(VMEM,) * 4,
        scratch_shapes=[pltpu.VMEM((2, TOK, HD), F32)],
        compiler_params=PARAMS,
        cost_estimate=cost(10**7, 4 * 10**6, 10**5),
        name="pre",
    )(idx, *near0, *near1, mid_o, mid_lse, out_grad)

    far_eight, mid_o = after((joined(far_four, far4), mid_o))
    far_y = [far_eight] + list(round_of_y(far_eight, far_eight))
    far_y, stats = after((jnp.concatenate(far_y, 0), stats))
    far_all = joined(far_y, exchange(far_y, 1))

    patch, stats = pl.pallas_call(
        far_forward_kernel,
        out_shape=(sds((2, 16, HD), F32), sds((4, TOK), F32)),
        in_specs=[SMEM] + [VMEM] * 3,
        out_specs=(VMEM,) * 2,
        scratch_shapes=[pltpu.VMEM((4, HD), F32)],
        compiler_params=PARAMS,
        cost_estimate=cost(10**7, 10**6, 10**5),
        name="far_forward",
    )(idx, far_all, far_in, stats)

    for bit in (2, 1, 4):
        stats = stats + head_exchange(stats, bit)

    far_g = pl.pallas_call(
        far_grad_kernel,
        out_shape=sds((16, 256), BF),
        in_specs=[SMEM] + [VMEM] * 3,
        out_specs=VMEM,
        scratch_shapes=[pltpu.VMEM((32, HD), F32), pltpu.VMEM((2, 32, HD), F32)],
        compiler_params=PARAMS,
        cost_estimate=cost(10**6, 10**5),
        name="far_grad",
    )(idx, stats, far_in, patch)

    stats, far_g = after((stats, far_g))
    part1 = exchange(far_g, 32)
    normed, grad, delta, lse, mid_g = pl.pallas_call(
        norm_kernel,
        out_shape=(
            sds((TOK, 256), BF),
            sds((TOK, 256), BF),
            by_head_shape,
            by_head_shape,
            sds((256, 256), BF),
        ),
        in_specs=[SMEM] + [VMEM] * 5,
        out_specs=(VMEM,) * 5,
        scratch_shapes=[pltpu.VMEM((2, TOK, HD), F32), pltpu.VMEM((2, TOK, HD), F32)],
        compiler_params=PARAMS,
        cost_estimate=cost(10**7, 4 * 10**6),
        name="norm",
    )(idx, stats, att, out_grad, lse12, patch)

    def near_backward(block):
        part = pl.BlockSpec((SEG, HD), lambda j: (block, j))
        stat = pl.BlockSpec((1, SEG, HD), lambda j: (j, block, 0))
        return pl.pallas_call(
            near_backward_kernel,
            grid=(2,),
            out_shape=(half_shape,) * 3,
            in_specs=[part] * 4 + [stat] * 2,
            out_specs=(half,) * 3,
            compiler_params=PARAMS,
            cost_estimate=cost(10**9, 4 * 10**6, 10**6),
            name=f"near_backward_{block}",
        )(queries, keys, values, grad, lse, delta)

    part_a, mid_g = after((joined(far_g, part1), mid_g))
    part2 = exchange(part_a, 16)
    dq0, dk0, dv0 = near_backward(0)
    part_b, dq0 = after((joined(part_a, part2), dq0))
    part3 = exchange(part_b, 8)
    dq1, dk1, dv1 = near_backward(1)
    part_c, dq1 = after((joined(part_b, part3), dq1))
    sent2, sent4, sent6 = round_of_y(part_c, joined(part_c, mid_g))

    grad_queries = pl.pallas_call(
        query_grad_kernel,
        out_shape=sds((TOK, 256), BF),
        in_specs=[SMEM] + [VMEM] * 6,
        out_specs=VMEM,
        scratch_shapes=[pltpu.VMEM((2, TOK, HD), F32), pltpu.VMEM((2, 128, HD), F32)],
        compiler_params=PARAMS,
        cost_estimate=cost(2 * 10**8, 3 * 10**6, 10**5),
        name="query_grad",
    )(idx, dq0, dq1, mid_all, far_all, mid_g, far_g)

    sent = jnp.concatenate([part_c, sent2[:128], sent4, sent6, mid_g, sent2[128:]], 0)
    sent, grad_queries = after((sent, grad_queries))
    grads = joined(sent, exchange(sent, 1))

    grad_keys, grad_values, whole = pl.pallas_call(
        key_grad_kernel,
        out_shape=(sds((TOK, 256), BF), sds((TOK, 256), BF), sds((2, 8, 256), F32)),
        in_specs=[SMEM] + [VMEM] * 7,
        out_specs=(VMEM,) * 3,
        scratch_shapes=[pltpu.VMEM((4, TOK, HD), F32), pltpu.VMEM((4, 128, HD), F32)],
        compiler_params=PARAMS,
        cost_estimate=cost(2 * 10**8, 4 * 10**6, 10**5),
        name="key_grad",
    )(idx, dk0, dk1, dv0, dv1, mid_all, far_all, grads)

    return normed, grad_queries, grad_keys, grad_values, whole


def solution(mesh):
    spec = P("seq", "head")
    return jax.shard_map(
        local,
        mesh=mesh,
        in_specs=(spec,) * 4,
        out_specs=(spec,) * 4 + (P(None, "seq", "head"),),
        check_vma=False,
    )
```

time: 872 us -> 130 us (0.15); the launches traced: 861 us -> 129 us
  waiting for transfers between devices: 380 us -> 12.1 us
  blocking collectives: 302 us -> 0 us
  local copies, waits for them, and re-layouts: 58 us -> 3.4 us
  starting transfers between devices: 38.9 us -> 90.2 us
  matrix products: 37.5 us -> 0 us
  other arithmetic: 29.2 us -> 0.3 us
  Pallas kernels: 0 us -> 21.9 us
  between operations: 15.2 us -> 1.05 us
    reduce_scatter x1 -> x0, waiting for transfers between devices: 375 us -> none  [local(): lax.psum_scatter(jnp.stack([key_part, value_part], 1).reshape(rows_far *...]
    all_gather x2 -> x0, blocking collectives: 229 us -> none  [the longest x1 116 us: local(): lax.all_gather(far_key, 'seq', axis=0, tiled=True)]
    psum x2 -> x0, blocking collectives: 73.8 us -> none  [row_totals(): return lax.psum((first_sum, second_sum), 'head')]
    ppermute x12 -> x19, starting transfers between devices: 38.9 us -> 90.2 us  [the longest x16 69.7 us: exchange(): return lax.ppermute(x, 'seq', [(i, i ^ bit) for i in range(64)])]
    dot_general x26 -> x0, matrix products: 37.5 us -> none  [the longest x3 7.66 us: level_forward(): jnp.einsum('bhqk,bkhd->bqhd', weight_tensors.astype(jnp.bfloat16), value_...]
    pallas_call x0 -> x12, Pallas kernels: none -> 21.9 us  [the longest x2 4.26 us: near_backward(): pl.pallas_call(near_backward_kernel, grid=(2,), out_shape=(half_shape,) *...]
    mul x25 -> x0, local copies, waits for them, and re-layouts: 16.1 us -> none  [the longest x19 6.27 us: spread_rows(): widened = row_block[:, None] * chosen.astype(jnp.float32)[None, :, :, None]]
    another operation x12 -> x0, local copies, waits for them, and re-layouts: 11.2 us -> none  [the longest x4 3.37 us: pick_rows(): row_block.reshape(row_block.shape[0] // spacing_step, spacing_step, row_b...]
  transfers between devices with their start and end apart: 13 -> 19, of which waited for: 2 -> 8; matrix products, arithmetic and copies ran while one was open for 6% -> 0% of each run, Pallas kernels for 0% -> 12%
where the time goes in v1:
time: 130 us; the launch traced here: 129 us
  starting transfers between devices  90.2 us (69%)
  Pallas kernels  21.9 us (17%)
  waiting for transfers between devices  12.1 us (9%)
  local copies, waits for them, and re-layouts  3.4 us (3%)
    ppermute x16, starting transfers between devices, exchange(): return lax.ppermute(x, 'seq', [(i, i ^ bit) for i in range(64)])  69.7 us
    ppermute x3, starting transfers between devices, head_exchange(): return lax.ppermute(x, 'head', [(i, i ^ bit) for i in range(8)])  20.5 us
    ppermute x16, waiting for transfers between devices, exchange(): return lax.ppermute(x, 'seq', [(i, i ^ bit) for i in range(64)])  7.41 us
    ppermute x3, waiting for transfers between devices, head_exchange(): return lax.ppermute(x, 'head', [(i, i ^ bit) for i in range(8)])  4.69 us
    pallas_call x2, Pallas kernels, near_backward(): pl.pallas_call(near_backward_kernel, grid=(2,), out_shape=(half_shape,) *...  4.26 us
    pallas_call x2, Pallas kernels, near_forward(): pl.pallas_call(near_forward_kernel, grid=(2,), out_shape=(half_shape, hal...  3.43 us
    unnamed x21, local copies, waits for them, and re-layouts  3.26 us
    pallas_call x1, Pallas kernels, local(): pl.pallas_call(norm_kernel, out_shape=(sds((TOK, 256), BF), sds((TOK, 256...  3.22 us
  transfers between devices with their start and end apart: 19, of which 8 were waited for; matrix products, arithmetic and copies ran while one was open for 0% of the time, Pallas kernels for 12%

profile of v1, /device:TPU:1, one launch (start us, length us, event | category | flops | bytes accessed | tf_op | source)
XLA Modules:
  0.0 128.9 jit_solution(12978915162014365876)
XLA Ops:
  4.7 4.0 %collective-permute-start = (bf16[256,384]{1,0:T(8,128)(2,1)S(1)}, bf16[256,384]{1,0:T(8,128)(2,1)S(1)}, u32[]{:S(2)}, u32[]{:S(2)}) collective-permute-start(bf16[256,384]{1,0:T(8,128)(2,1)S(1)} %get-tuple-element.53), channel_id=1, source_target_pairs={{0,16},{8,24},{16,0},{24,8},{32,48},{40,56},{48,32},{56,40},{64,80... | collective-permute-start | bytes 589832 | tf_op jit(solution)/shard_map/ppermute | solution.py:426
  8.8 8.8 %collective-permute-start.1 = (bf16[16,384]{1,0:T(8,128)(2,1)S(1)}, bf16[16,384]{1,0:T(8,128)(2,1)S(1)}, u32[]{:S(2)}, u32[]{:S(2)}) collective-permute-start(bf16[16,384]{1,0:T(8,128)(2,1)S(1)} %get-tuple-element.54), channel_id=1, source_target_pairs={{0,256},{8,264},{16,272},{24,280},{32,288},{40,296},{48,304},{56,3... | collective-permute-start | bytes 36872 | tf_op jit(solution)/shard_map/ppermute | solution.py:426
  17.6 1.7 %near_forward_0.1 = (f32[2,512,128]{2,1,0:T(8,128)S(1)}, f32[2,512,128]{2,1,0:T(8,128)S(1)}) custom-call(bf16[1024,256]{1,0:T(8,128)(2,1)S(1)} %copy-done.1, bf16[1024,256]{1,0:T(8,128)(2,1)S(1)} %copy-done.3, bf16[1024,256]{1,0:T(8,128)(2,1)S(1)} %copy-done.5), custom_call_target="tpu_custom_call" | custom-call | flops 400000000 | bytes 2000000 | tf_op jit(solution)/shard_map/near_forward_0/pallas_call | solution.py:476
  19.4 5.6 %collective-permute-start.4 = (bf16[512,384]{1,0:T(8,128)(2,1)S(1)}, bf16[512,384]{1,0:T(8,128)(2,1)S(1)}, u32[]{:S(2)}, u32[]{:S(2)}) collective-permute-start(bf16[512,384]{1,0:T(8,128)(2,1)S(1)} %pad_maximum_fusion.1), channel_id=1, source_target_pairs={{0,8},{8,0},{16,24},{24,16},{32,40},{40,32},{48,56},{56,48},{64,72... | collective-permute-start | bytes 1179656 | tf_op jit(solution)/shard_map/ppermute | solution.py:426
  25.0 2.5 %collective-permute-start.2 = (bf16[32,384]{1,0:T(8,128)(2,1)S(1)}, bf16[32,384]{1,0:T(8,128)(2,1)S(1)}, u32[]{:S(2)}, u32[]{:S(2)}) collective-permute-start(bf16[32,384]{1,0:T(8,128)(2,1)S(1)} %pad_maximum_fusion.8), channel_id=1, source_target_pairs={{0,128},{8,136},{16,144},{24,152},{32,160},{40,168},{48,176},{56,1... | collective-permute-start | bytes 73736 | tf_op jit(solution)/shard_map/ppermute | solution.py:426
  27.5 1.7 %near_forward_1.1 = (f32[2,512,128]{2,1,0:T(8,128)S(1)}, f32[2,512,128]{2,1,0:T(8,128)S(1)}) custom-call(bf16[1024,256]{1,0:T(8,128)(2,1)S(1)} %copy-done.1, bf16[1024,256]{1,0:T(8,128)(2,1)S(1)} %copy-done.3, bf16[1024,256]{1,0:T(8,128)(2,1)S(1)} %copy-done.5), custom_call_target="tpu_custom_call" | custom-call | flops 400000000 | bytes 2000000 | tf_op jit(solution)/shard_map/near_forward_1/pallas_call | solution.py:476
  29.2 1.4 %collective-permute-done.2 = bf16[32,384]{1,0:T(8,128)(2,1)S(1)} collective-permute-done((bf16[32,384]{1,0:T(8,128)(2,1)S(1)}, bf16[32,384]{1,0:T(8,128)(2,1)S(1)}, u32[]{:S(2)}, u32[]{:S(2)}) %collective-permute-start.2) | collective-permute-done | bytes 24608 | tf_op jit(solution)/shard_map/ppermute | solution.py:426
  30.6 2.2 %collective-permute-start.3 = (bf16[64,384]{1,0:T(8,128)(2,1)S(1)}, bf16[64,384]{1,0:T(8,128)(2,1)S(1)}, u32[]{:S(2)}, u32[]{:S(2)}) collective-permute-start(bf16[64,384]{1,0:T(8,128)(2,1)S(1)} %pad_maximum_fusion.6), channel_id=1, source_target_pairs={{0,64},{8,72},{16,80},{24,88},{32,96},{40,104},{48,112},{56,120},{... | collective-permute-start | bytes 147464 | tf_op jit(solution)/shard_map/ppermute | solution.py:426
  32.9 2.5 %collective-permute-done.3 = bf16[64,384]{1,0:T(8,128)(2,1)S(1)} collective-permute-done((bf16[64,384]{1,0:T(8,128)(2,1)S(1)}, bf16[64,384]{1,0:T(8,128)(2,1)S(1)}, u32[]{:S(2)}, u32[]{:S(2)}) %collective-permute-start.3) | collective-permute-done | bytes 49184 | tf_op jit(solution)/shard_map/ppermute | solution.py:426
  36.7 3.6 %collective-permute-start.5 = (bf16[128,384]{1,0:T(8,128)(2,1)S(1)}, bf16[128,384]{1,0:T(8,128)(2,1)S(1)}, u32[]{:S(2)}, u32[]{:S(2)}) collective-permute-start(bf16[128,384]{1,0:T(8,128)(2,1)S(1)} %pad_maximum_fusion.4), channel_id=1, source_target_pairs={{0,16},{8,24},{16,0},{24,8},{32,48},{40,56},{48,32},{56,40},{64,80... | collective-permute-start | bytes 294920 | tf_op jit(solution)/shard_map/ppermute | solution.py:426
  40.4 2.1 %collective-permute-start.6 = (bf16[128,384]{1,0:T(8,128)(2,1)S(1)}, bf16[128,384]{1,0:T(8,128)(2,1)S(1)}, u32[]{:S(2)}, u32[]{:S(2)}) collective-permute-start(bf16[128,384]{1,0:T(8,128)(2,1)S(1)} %pad_maximum_fusion.4), channel_id=1, source_target_pairs={{0,32},{8,40},{16,48},{24,56},{32,0},{40,8},{48,16},{56,24},{64,96... | collective-permute-start | bytes 294920 | tf_op jit(solution)/shard_map/ppermute | solution.py:426
  42.5 4.1 %collective-permute-start.7 = (bf16[128,384]{1,0:T(8,128)(2,1)S(1)}, bf16[128,384]{1,0:T(8,128)(2,1)S(1)}, u32[]{:S(2)}, u32[]{:S(2)}) collective-permute-start(bf16[128,384]{1,0:T(8,128)(2,1)S(1)} %pad_maximum_fusion.4), channel_id=1, source_target_pairs={{0,48},{8,56},{16,32},{24,40},{32,16},{40,24},{48,0},{56,8},{64,11... | collective-permute-start | bytes 294920 | tf_op jit(solution)/shard_map/ppermute | solution.py:426
  46.6 1.8 %pre.1 = (bf16[1024,256]{1,0:T(8,128)(2,1)S(1)}, f32[2,1024,128]{2,1,0:T(8,128)S(1)}, f32[4,1024]{1,0:T(4,128)S(1)}, f32[3,16,128]{2,1,0:T(8,128)S(1)}) custom-call(s32[2]{0:T(128)S(1)} %pad_add_fusion.idx, f32[2,512,128]{2,1,0:T(8,128)S(1)} %get-tuple-element.64.o0, f32[2,512,128]{2,1,0:T(8,128)S(1)} %get-tuple-element.65.lse0, ...), custom_call_target="tpu_custom_call" | custom-call | flops 10000000 | bytes 4000000 | tf_op jit(solution)/shard_map/pre/pallas_call | solution.py:507
  49.1 5.4 %collective-permute-start.8 = (bf16[512,384]{1,0:T(8,128)(2,1)S(1)}, bf16[512,384]{1,0:T(8,128)(2,1)S(1)}, u32[]{:S(2)}, u32[]{:S(2)}) collective-permute-start(bf16[512,384]{1,0:T(8,128)(2,1)S(1)} %pad_maximum_fusion.2), channel_id=1, source_target_pairs={{0,8},{8,0},{16,24},{24,16},{32,40},{40,32},{48,56},{56,48},{64,72... | collective-permute-start | bytes 1179656 | tf_op jit(solution)/shard_map/ppermute | solution.py:426
  57.1 4.2 %collective-permute-start.9 = (f32[4,1024]{1,0:T(4,128)S(1)}, f32[4,1024]{1,0:T(4,128)S(1)}, u32[]{:S(2)}, u32[]{:S(2)}) collective-permute-start(f32[4,1024]{1,0:T(4,128)S(1)} %get-tuple-element.73), channel_id=1, source_target_pairs={{0,2},{1,3},{2,0},{3,1},{4,6},{5,7},{6,4},{7,5},{8,10},{9,11},{10,... | collective-permute-start | bytes 49160 | tf_op jit(solution)/shard_map/ppermute | solution.py:430
  61.3 1.8 %collective-permute-done.9 = f32[4,1024]{1,0:T(4,128)S(1)} collective-permute-done((f32[4,1024]{1,0:T(4,128)S(1)}, f32[4,1024]{1,0:T(4,128)S(1)}, u32[]{:S(2)}, u32[]{:S(2)}) %collective-permute-start.9) | collective-permute-done | bytes 16416 | tf_op jit(solution)/shard_map/ppermute | solution.py:430
  63.1 2.7 %collective-permute-start.10 = (f32[4,1024]{1,0:T(4,128)S(1)}, f32[4,1024]{1,0:T(4,128)S(1)}, u32[]{:S(2)}, u32[]{:S(2)}) collective-permute-start(f32[4,1024]{1,0:T(4,128)S(1)} %add.9), channel_id=1, source_target_pairs={{0,1},{1,0},{2,3},{3,2},{4,5},{5,4},{6,7},{7,6},{8,9},{9,8},{10,11... | collective-permute-start | bytes 49160 | tf_op jit(solution)/shard_map/ppermute | solution.py:430
  65.7 1.8 %collective-permute-done.10 = f32[4,1024]{1,0:T(4,128)S(1)} collective-permute-done((f32[4,1024]{1,0:T(4,128)S(1)}, f32[4,1024]{1,0:T(4,128)S(1)}, u32[]{:S(2)}, u32[]{:S(2)}) %collective-permute-start.10) | collective-permute-done | bytes 16416 | tf_op jit(solution)/shard_map/ppermute | solution.py:430
  67.6 13.7 %collective-permute-start.11 = (f32[4,1024]{1,0:T(4,128)S(1)}, f32[4,1024]{1,0:T(4,128)S(1)}, u32[]{:S(2)}, u32[]{:S(2)}) collective-permute-start(f32[4,1024]{1,0:T(4,128)S(1)} %add.10), channel_id=1, source_target_pairs={{0,4},{1,5},{2,6},{3,7},{4,0},{5,1},{6,2},{7,3},{8,12},{9,13},{10,... | collective-permute-start | bytes 49160 | tf_op jit(solution)/shard_map/ppermute | solution.py:430
  83.1 5.4 %collective-permute-start.12 = (bf16[16,256]{1,0:T(8,128)(2,1)S(1)}, bf16[16,256]{1,0:T(8,128)(2,1)S(1)}, u32[]{:S(2)}, u32[]{:S(2)}) collective-permute-start(bf16[16,256]{1,0:T(8,128)(2,1)S(1)} %far_grad.1.far_g), channel_id=1, source_target_pairs={{0,256},{8,264},{16,272},{24,280},{32,288},{40,296},{48,304},{56,3... | collective-permute-start | bytes 24584 | tf_op jit(solution)/shard_map/ppermute | solution.py:426
  88.4 3.2 %norm.1 = (bf16[1024,256]{1,0:T(8,128)(2,1)}, bf16[1024,256]{1,0:T(8,128)(2,1)S(1)}, f32[2,1024,128]{2,1,0:T(8,128)S(1)}, f32[2,1024,128]{2,1,0:T(8,128)S(1)}, bf16[256,256]{1,0:T(8,128)(2,1)S(1)}) custom-call(s32[2]{0:T(128)S(1)} %pad_add_fusion.idx, f32[4,1024]{1,0:T(4,128)S(1)} %add.11.stat_ref, bf16[1024,256]{1,0:T(8,128)(2,1)S(1)} %get-tuple-element.76.att_ref, ...), custom_call_target="tpu_custom_call" | custom-call | flops 10000000 | bytes 4000000 | tf_op jit(solution)/shard_map/norm/pallas_call | solution.py:555
  91.7 4.7 %collective-permute-start.13 = (bf16[32,256]{1,0:T(8,128)(2,1)S(1)}, bf16[32,256]{1,0:T(8,128)(2,1)S(1)}, u32[]{:S(2)}, u32[]{:S(2)}) collective-permute-start(bf16[32,256]{1,0:T(8,128)(2,1)S(1)} %pad_maximum_fusion.9), channel_id=1, source_target_pairs={{0,128},{8,136},{16,144},{24,152},{32,160},{40,168},{48,176},{56,1... | collective-permute-start | bytes 49160 | tf_op jit(solution)/shard_map/ppermute | solution.py:426
  96.3 2.1 %near_backward_0.1 = (f32[2,512,128]{2,1,0:T(8,128)S(1)}, f32[2,512,128]{2,1,0:T(8,128)S(1)}, f32[2,512,128]{2,1,0:T(8,128)S(1)}) custom-call(bf16[1024,256]{1,0:T(8,128)(2,1)S(1)} %copy-done.1, bf16[1024,256]{1,0:T(8,128)(2,1)S(1)} %copy-done.3, bf16[1024,256]{1,0:T(8,128)(2,1)S(1)} %copy-done.5, bf16[1024,256]{1,0:T(8,128)(2,1)S(1)} %get-tuple-element.82.g_ref, ...), custom_call_target="tpu_custom_call" | custom-call | flops 1000000000 | bytes 4000000 | tf_op jit(solution)/shard_map/near_backward_0/pallas_call | solution.py:575
  98.5 3.4 %collective-permute-start.14 = (bf16[64,256]{1,0:T(8,128)(2,1)S(1)}, bf16[64,256]{1,0:T(8,128)(2,1)S(1)}, u32[]{:S(2)}, u32[]{:S(2)}) collective-permute-start(bf16[64,256]{1,0:T(8,128)(2,1)S(1)} %pad_maximum_fusion.7), channel_id=1, source_target_pairs={{0,64},{8,72},{16,80},{24,88},{32,96},{40,104},{48,112},{56,120},{... | collective-permute-start | bytes 98312 | tf_op jit(solution)/shard_map/ppermute | solution.py:426
  101.9 2.1 %near_backward_1.1 = (f32[2,512,128]{2,1,0:T(8,128)S(1)}, f32[2,512,128]{2,1,0:T(8,128)S(1)}, f32[2,512,128]{2,1,0:T(8,128)S(1)}) custom-call(bf16[1024,256]{1,0:T(8,128)(2,1)S(1)} %copy-done.1, bf16[1024,256]{1,0:T(8,128)(2,1)S(1)} %copy-done.3, bf16[1024,256]{1,0:T(8,128)(2,1)S(1)} %copy-done.5, bf16[1024,256]{1,0:T(8,128)(2,1)S(1)} %get-tuple-element.82.g_ref, ...), custom_call_target="tpu_custom_call" | custom-call | flops 1000000000 | bytes 4000000 | tf_op jit(solution)/shard_map/near_backward_1/pallas_call | solution.py:575
  104.1 1.9 %collective-permute-start.15 = (bf16[384,256]{1,0:T(8,128)(2,1)S(1)}, bf16[384,256]{1,0:T(8,128)(2,1)S(1)}, u32[]{:S(2)}, u32[]{:S(2)}) collective-permute-start(bf16[384,256]{1,0:T(8,128)(2,1)S(1)} %pad_maximum_fusion.3), channel_id=1, source_target_pairs={{0,16},{8,24},{16,0},{24,8},{32,48},{40,56},{48,32},{56,40},{64,80... | collective-permute-start | bytes 589832 | tf_op jit(solution)/shard_map/ppermute | solution.py:426
  106.0 3.9 %collective-permute-start.16 = (bf16[128,256]{1,0:T(8,128)(2,1)S(1)}, bf16[128,256]{1,0:T(8,128)(2,1)S(1)}, u32[]{:S(2)}, u32[]{:S(2)}) collective-permute-start(bf16[128,256]{1,0:T(8,128)(2,1)S(1)} %pad_maximum_fusion.5), channel_id=1, source_target_pairs={{0,32},{8,40},{16,48},{24,56},{32,0},{40,8},{48,16},{56,24},{64,96... | collective-permute-start | bytes 196616 | tf_op jit(solution)/shard_map/ppermute | solution.py:426
  109.9 3.8 %collective-permute-start.17 = (bf16[128,256]{1,0:T(8,128)(2,1)S(1)}, bf16[128,256]{1,0:T(8,128)(2,1)S(1)}, u32[]{:S(2)}, u32[]{:S(2)}) collective-permute-start(bf16[128,256]{1,0:T(8,128)(2,1)S(1)} %pad_maximum_fusion.5), channel_id=1, source_target_pairs={{0,48},{8,56},{16,32},{24,40},{32,16},{40,24},{48,0},{56,8},{64,11... | collective-permute-start | bytes 196616 | tf_op jit(solution)/shard_map/ppermute | solution.py:426
  113.7 2.3 %query_grad.1 = bf16[1024,256]{1,0:T(8,128)(2,1)} custom-call(s32[2]{0:T(128)S(1)} %pad_add_fusion.idx, f32[2,512,128]{2,1,0:T(8,128)S(1)} %get-tuple-element.90.dq0, f32[2,512,128]{2,1,0:T(8,128)S(1)} %get-tuple-element.91.dq1, bf16[1024,384]{1,0:T(8,128)(2,1)S(1)} %constant_dynamic-update-slice_fusion.mid_ref, ...), custom_call_target="tpu_custom_call" | custom-call | flops 200000000 | bytes 3000000 | tf_op jit(solution)/shard_map/query_grad/pallas_call | solution.py:595
  116.2 8.3 %collective-permute-start.18 = (bf16[1024,256]{1,0:T(8,128)(2,1)S(1)}, bf16[1024,256]{1,0:T(8,128)(2,1)S(1)}, u32[]{:S(2)}, u32[]{:S(2)}) collective-permute-start(bf16[1024,256]{1,0:T(8,128)(2,1)S(1)} %slice_dynamic-update-slice_fusion), channel_id=1, source_target_pairs={{0,8},{8,0},{16,24},{24,16},{32,40},{40,32},{48,56},{56,48},{64,72... | collective-permute-start | bytes 1572872 | tf_op jit(solution)/shard_map/ppermute | solution.py:426
  124.4 1.5 %collective-permute-done.18 = bf16[1024,256]{1,0:T(8,128)(2,1)S(1)} collective-permute-done((bf16[1024,256]{1,0:T(8,128)(2,1)S(1)}, bf16[1024,256]{1,0:T(8,128)(2,1)S(1)}, u32[]{:S(2)}, u32[]{:S(2)}) %collective-permute-start.18) | collective-permute-done | bytes 524320 | tf_op jit(solution)/shard_map/ppermute | solution.py:426
  126.0 2.9 %key_grad.1 = (bf16[1024,256]{1,0:T(8,128)(2,1)}, bf16[1024,256]{1,0:T(8,128)(2,1)}, f32[2,8,256]{2,1,0:T(8,128)}) custom-call(s32[2]{0:T(128)S(1)} %pad_add_fusion.idx, f32[2,512,128]{2,1,0:T(8,128)S(1)} %get-tuple-element.93.dk0, f32[2,512,128]{2,1,0:T(8,128)S(1)} %get-tuple-element.94.dk1, f32[2,512,128]{2,1,0:T(8,128)S(1)} %get-tuple-element.95.dv0, ...), custom_call_target="tpu_custom_call" | custom-call | flops 200000000 | bytes 4000000 | tf_op jit(solution)/shard_map/key_grad/pallas_call | solution.py:610
  (56 shorter events, 10.7 us)
Async XLA Ops:
  0.7 1.0 copy-start
  1.8 1.0 copy-start.2
  2.8 1.0 copy-start.4
  3.8 13.8 %copy-start.1 = (bf16[1024,256]{1,0:T(8,128)(2,1)S(1)}, bf16[1024,256]{1,0:T(8,128)(2,1)}, u32[]{:S(2)}) copy-start(bf16[1024,256]{1,0:T(8,128)(2,1)} %q_ref.9) | copy-start | bytes 1572868
  3.8 13.8 %copy-start.3 = (bf16[1024,256]{1,0:T(8,128)(2,1)S(1)}, bf16[1024,256]{1,0:T(8,128)(2,1)}, u32[]{:S(2)}) copy-start(bf16[1024,256]{1,0:T(8,128)(2,1)} %k_ref.9) | copy-start | bytes 1572868
  3.8 13.8 %copy-start.5 = (bf16[1024,256]{1,0:T(8,128)(2,1)S(1)}, bf16[1024,256]{1,0:T(8,128)(2,1)}, u32[]{:S(2)}) copy-start(bf16[1024,256]{1,0:T(8,128)(2,1)} %v_ref.9) | copy-start | bytes 1572868
  4.7 14.6 %collective-permute-start = (bf16[256,384]{1,0:T(8,128)(2,1)S(1)}, bf16[256,384]{1,0:T(8,128)(2,1)S(1)}, u32[]{:S(2)}, u32[]{:S(2)}) collective-permute-start(bf16[256,384]{1,0:T(8,128)(2,1)S(1)} %get-tuple-element.53), channel_id=1, source_target_pairs={{0,16},{8,24},{16,0},{24,8},{32,48},{40,56},{48,32},{56,40},{64,80... | collective-permute-start | bytes 589832 | tf_op jit(solution)/shard_map/ppermute | solution.py:426
  8.8 10.6 %collective-permute-start.1 = (bf16[16,384]{1,0:T(8,128)(2,1)S(1)}, bf16[16,384]{1,0:T(8,128)(2,1)S(1)}, u32[]{:S(2)}, u32[]{:S(2)}) collective-permute-start(bf16[16,384]{1,0:T(8,128)(2,1)S(1)} %get-tuple-element.54), channel_id=1, source_target_pairs={{0,256},{8,264},{16,272},{24,280},{32,288},{40,296},{48,304},{56,3... | collective-permute-start | bytes 36872 | tf_op jit(solution)/shard_map/ppermute | solution.py:426
  19.4 16.0 %collective-permute-start.4 = (bf16[512,384]{1,0:T(8,128)(2,1)S(1)}, bf16[512,384]{1,0:T(8,128)(2,1)S(1)}, u32[]{:S(2)}, u32[]{:S(2)}) collective-permute-start(bf16[512,384]{1,0:T(8,128)(2,1)S(1)} %pad_maximum_fusion.1), channel_id=1, source_target_pairs={{0,8},{8,0},{16,24},{24,16},{32,40},{40,32},{48,56},{56,48},{64,72... | collective-permute-start | bytes 1179656 | tf_op jit(solution)/shard_map/ppermute | solution.py:426
  25.0 5.6 %collective-permute-start.2 = (bf16[32,384]{1,0:T(8,128)(2,1)S(1)}, bf16[32,384]{1,0:T(8,128)(2,1)S(1)}, u32[]{:S(2)}, u32[]{:S(2)}) collective-permute-start(bf16[32,384]{1,0:T(8,128)(2,1)S(1)} %pad_maximum_fusion.8), channel_id=1, source_target_pairs={{0,128},{8,136},{16,144},{24,152},{32,160},{40,168},{48,176},{56,1... | collective-permute-start | bytes 73736 | tf_op jit(solution)/shard_map/ppermute | solution.py:426
  30.6 4.8 %collective-permute-start.3 = (bf16[64,384]{1,0:T(8,128)(2,1)S(1)}, bf16[64,384]{1,0:T(8,128)(2,1)S(1)}, u32[]{:S(2)}, u32[]{:S(2)}) collective-permute-start(bf16[64,384]{1,0:T(8,128)(2,1)S(1)} %pad_maximum_fusion.6), channel_id=1, source_target_pairs={{0,64},{8,72},{16,80},{24,88},{32,96},{40,104},{48,112},{56,120},{... | collective-permute-start | bytes 147464 | tf_op jit(solution)/shard_map/ppermute | solution.py:426
  32.9 13.7 %copy-start.6 = (bf16[1024,256]{1,0:T(8,128)(2,1)S(1)}, bf16[1024,256]{1,0:T(8,128)(2,1)}, u32[]{:S(2)}) copy-start(bf16[1024,256]{1,0:T(8,128)(2,1)} %g_ref.3) | copy-start | bytes 1572868
  36.7 11.7 %collective-permute-start.5 = (bf16[128,384]{1,0:T(8,128)(2,1)S(1)}, bf16[128,384]{1,0:T(8,128)(2,1)S(1)}, u32[]{:S(2)}, u32[]{:S(2)}) collective-permute-start(bf16[128,384]{1,0:T(8,128)(2,1)S(1)} %pad_maximum_fusion.4), channel_id=1, source_target_pairs={{0,16},{8,24},{16,0},{24,8},{32,48},{40,56},{48,32},{56,40},{64,80... | collective-permute-start | bytes 294920 | tf_op jit(solution)/shard_map/ppermute | solution.py:426
  40.4 8.0 %collective-permute-start.6 = (bf16[128,384]{1,0:T(8,128)(2,1)S(1)}, bf16[128,384]{1,0:T(8,128)(2,1)S(1)}, u32[]{:S(2)}, u32[]{:S(2)}) collective-permute-start(bf16[128,384]{1,0:T(8,128)(2,1)S(1)} %pad_maximum_fusion.4), channel_id=1, source_target_pairs={{0,32},{8,40},{16,48},{24,56},{32,0},{40,8},{48,16},{56,24},{64,96... | collective-permute-start | bytes 294920 | tf_op jit(solution)/shard_map/ppermute | solution.py:426
  42.5 6.6 %collective-permute-start.7 = (bf16[128,384]{1,0:T(8,128)(2,1)S(1)}, bf16[128,384]{1,0:T(8,128)(2,1)S(1)}, u32[]{:S(2)}, u32[]{:S(2)}) collective-permute-start(bf16[128,384]{1,0:T(8,128)(2,1)S(1)} %pad_maximum_fusion.4), channel_id=1, source_target_pairs={{0,48},{8,56},{16,32},{24,40},{32,16},{40,24},{48,0},{56,8},{64,11... | collective-permute-start | bytes 294920 | tf_op jit(solution)/shard_map/ppermute | solution.py:426
  49.1 6.8 %collective-permute-start.8 = (bf16[512,384]{1,0:T(8,128)(2,1)S(1)}, bf16[512,384]{1,0:T(8,128)(2,1)S(1)}, u32[]{:S(2)}, u32[]{:S(2)}) collective-permute-start(bf16[512,384]{1,0:T(8,128)(2,1)S(1)} %pad_maximum_fusion.2), channel_id=1, source_target_pairs={{0,8},{8,0},{16,24},{24,16},{32,40},{40,32},{48,56},{56,48},{64,72... | collective-permute-start | bytes 1179656 | tf_op jit(solution)/shard_map/ppermute | solution.py:426
  57.1 6.0 %collective-permute-start.9 = (f32[4,1024]{1,0:T(4,128)S(1)}, f32[4,1024]{1,0:T(4,128)S(1)}, u32[]{:S(2)}, u32[]{:S(2)}) collective-permute-start(f32[4,1024]{1,0:T(4,128)S(1)} %get-tuple-element.73), channel_id=1, source_target_pairs={{0,2},{1,3},{2,0},{3,1},{4,6},{5,7},{6,4},{7,5},{8,10},{9,11},{10,... | collective-permute-start | bytes 49160 | tf_op jit(solution)/shard_map/ppermute | solution.py:430
  63.1 4.5 %collective-permute-start.10 = (f32[4,1024]{1,0:T(4,128)S(1)}, f32[4,1024]{1,0:T(4,128)S(1)}, u32[]{:S(2)}, u32[]{:S(2)}) collective-permute-start(f32[4,1024]{1,0:T(4,128)S(1)} %add.9), channel_id=1, source_target_pairs={{0,1},{1,0},{2,3},{3,2},{4,5},{5,4},{6,7},{7,6},{8,9},{9,8},{10,11... | collective-permute-start | bytes 49160 | tf_op jit(solution)/shard_map/ppermute | solution.py:430
  67.6 14.8 %collective-permute-start.11 = (f32[4,1024]{1,0:T(4,128)S(1)}, f32[4,1024]{1,0:T(4,128)S(1)}, u32[]{:S(2)}, u32[]{:S(2)}) collective-permute-start(f32[4,1024]{1,0:T(4,128)S(1)} %add.10), channel_id=1, source_target_pairs={{0,4},{1,5},{2,6},{3,7},{4,0},{5,1},{6,2},{7,3},{8,12},{9,13},{10,... | collective-permute-start | bytes 49160 | tf_op jit(solution)/shard_map/ppermute | solution.py:430
  83.1 8.6 %collective-permute-start.12 = (bf16[16,256]{1,0:T(8,128)(2,1)S(1)}, bf16[16,256]{1,0:T(8,128)(2,1)S(1)}, u32[]{:S(2)}, u32[]{:S(2)}) collective-permute-start(bf16[16,256]{1,0:T(8,128)(2,1)S(1)} %far_grad.1.far_g), channel_id=1, source_target_pairs={{0,256},{8,264},{16,272},{24,280},{32,288},{40,296},{48,304},{56,3... | collective-permute-start | bytes 24584 | tf_op jit(solution)/shard_map/ppermute | solution.py:426
  91.7 6.8 %collective-permute-start.13 = (bf16[32,256]{1,0:T(8,128)(2,1)S(1)}, bf16[32,256]{1,0:T(8,128)(2,1)S(1)}, u32[]{:S(2)}, u32[]{:S(2)}) collective-permute-start(bf16[32,256]{1,0:T(8,128)(2,1)S(1)} %pad_maximum_fusion.9), channel_id=1, source_target_pairs={{0,128},{8,136},{16,144},{24,152},{32,160},{40,168},{48,176},{56,1... | collective-permute-start | bytes 49160 | tf_op jit(solution)/shard_map/ppermute | solution.py:426
  98.5 5.5 %collective-permute-start.14 = (bf16[64,256]{1,0:T(8,128)(2,1)S(1)}, bf16[64,256]{1,0:T(8,128)(2,1)S(1)}, u32[]{:S(2)}, u32[]{:S(2)}) collective-permute-start(bf16[64,256]{1,0:T(8,128)(2,1)S(1)} %pad_maximum_fusion.7), channel_id=1, source_target_pairs={{0,64},{8,72},{16,80},{24,88},{32,96},{40,104},{48,112},{56,120},{... | collective-permute-start | bytes 98312 | tf_op jit(solution)/shard_map/ppermute | solution.py:426
  104.1 12.0 %collective-permute-start.15 = (bf16[384,256]{1,0:T(8,128)(2,1)S(1)}, bf16[384,256]{1,0:T(8,128)(2,1)S(1)}, u32[]{:S(2)}, u32[]{:S(2)}) collective-permute-start(bf16[384,256]{1,0:T(8,128)(2,1)S(1)} %pad_maximum_fusion.3), channel_id=1, source_target_pairs={{0,16},{8,24},{16,0},{24,8},{32,48},{40,56},{48,32},{56,40},{64,80... | collective-permute-start | bytes 589832 | tf_op jit(solution)/shard_map/ppermute | solution.py:426
  106.0 10.1 %collective-permute-start.16 = (bf16[128,256]{1,0:T(8,128)(2,1)S(1)}, bf16[128,256]{1,0:T(8,128)(2,1)S(1)}, u32[]{:S(2)}, u32[]{:S(2)}) collective-permute-start(bf16[128,256]{1,0:T(8,128)(2,1)S(1)} %pad_maximum_fusion.5), channel_id=1, source_target_pairs={{0,32},{8,40},{16,48},{24,56},{32,0},{40,8},{48,16},{56,24},{64,96... | collective-permute-start | bytes 196616 | tf_op jit(solution)/shard_map/ppermute | solution.py:426
  109.9 6.2 %collective-permute-start.17 = (bf16[128,256]{1,0:T(8,128)(2,1)S(1)}, bf16[128,256]{1,0:T(8,128)(2,1)S(1)}, u32[]{:S(2)}, u32[]{:S(2)}) collective-permute-start(bf16[128,256]{1,0:T(8,128)(2,1)S(1)} %pad_maximum_fusion.5), channel_id=1, source_target_pairs={{0,48},{8,56},{16,32},{24,40},{32,16},{40,24},{48,0},{56,8},{64,11... | collective-permute-start | bytes 196616 | tf_op jit(solution)/shard_map/ppermute | solution.py:426
  116.2 9.8 %collective-permute-start.18 = (bf16[1024,256]{1,0:T(8,128)(2,1)S(1)}, bf16[1024,256]{1,0:T(8,128)(2,1)S(1)}, u32[]{:S(2)}, u32[]{:S(2)}) collective-permute-start(bf16[1024,256]{1,0:T(8,128)(2,1)S(1)} %slice_dynamic-update-slice_fusion), channel_id=1, source_target_pairs={{0,8},{8,0},{16,24},{24,16},{32,40},{40,32},{48,56},{56,48},{64,72... | collective-permute-start | bytes 1572872 | tf_op jit(solution)/shard_map/ppermute | solution.py:426

commit v2 on v1

--- a/solution.py
+++ b/solution.py
@@ -110,11 +110,17 @@
 
 
 def far_places(s):
-    n, row = iota((16, 1024), 1), iota((16, 1024), 0)
-    pos = n // 16
-    flips = (pos & 1) * 32 + (pos & 2) * 8 + (pos & 4) * 2 + ((pos >> 3) & 3) * 2 + (pos >> 5)
-    place = (s ^ flips) * 8 + (n & 7)
-    return ((n >> 3) & 1) == (row >> 3), place, s * 8 + (row & 7)
+    n, row = iota((32, 1024), 1), iota((32, 1024), 0)
+    pos = n // 32
+    flips = (pos & 1) * 32 + (pos & 2) * 8 + (pos & 4) * 2 + ((pos & 8) >> 1) + ((pos & 16) >> 3)
+    place = (s ^ flips ^ ((n >> 4) & 1)) * 8 + (n & 7)
+    mine = (s ^ (row >> 4)) * 8 + (row & 7)
+    return ((n >> 3) & 1) == ((row >> 3) & 1), place, mine
+
+
+def own_share(idx, keep_ref, reply_ref):
+    odd = (iota(keep_ref.shape, 0) * 0 + (idx[0] & 1)) == 1
+    return jnp.where(odd, keep_ref[...], reply_ref[...])
 
 
 def far_keep_forward(s):
@@ -128,7 +134,7 @@
 
 
 def pre_kernel(
-    idx, o0, lse0, o1, lse1, mid_o, mid_lse, g_ref, att_ref, lse_ref, stat_ref, far_ref, out_scr
+    idx, o0, lse0, o1, lse1, mid_o, mid_lse, g_ref, att_ref, lse_ref, far_ref, out_scr
 ):
     for j in range(2):
         head = idx[1] * 2 + j
@@ -144,8 +150,8 @@
         den = e1 + e2
         so[picked, :] = (e1 * so[picked, :] + e2 * mid_o[own, :]) / den
         sl[picked, :] = peak + jnp.log(den)
-        far_ref[0, j * 8 : (j + 1) * 8, :] = so[distant, :]
-        far_ref[1, j * 8 : (j + 1) * 8, :] = sl[distant, :]
+        far_ref[j * 8 : (j + 1) * 8, :] = so[distant, :]
+        far_ref[16 + j * 8 : 24 + j * 8, :] = sl[distant, :]
     lane = iota((128, HD), 1)
     row = iota((128, HD), 0)
     for b in range(8):
@@ -166,10 +172,10 @@
         block = jnp.zeros((128, HD), F32)
         for i, term in enumerate(sums):
             block = jnp.where(lane == i, jnp.sum(term, axis=1, keepdims=True), block)
-        stat_ref[:, rows] = block.T[:4, :]
+        far_ref[48 + b * 4 : 52 + b * 4, :] = block.T[:4, :]
     for j in range(2):
         distant = pl.ds(idx[1] * 2 + j, 8, stride=128)
-        far_ref[2, j * 8 : (j + 1) * 8, :] = out_scr.at[j][distant, :]
+        far_ref[32 + j * 8 : 40 + j * 8, :] = out_scr.at[j][distant, :]
 
 
 def norm_terms(total, squares, cross, g_total):
@@ -185,63 +191,85 @@
     return pack
 
 
-def far_forward_kernel(idx, far_all, far_in, stat_in, patch_ref, stat_ref, own_scr):
-    s_idx = idx[0]
-    q = far_all[:16, 2 * HD :]
-    s = jnp.where(far_keep_forward(s_idx), dot_nt(q, far_all[:, :HD]) * SCALE, NEG)
+def far_forward_kernel(idx, far_all, own_ref, mate_ref, patch_ref, stat_ref):
+    q = far_all[:32, 2 * HD :]
+    s = jnp.where(far_keep_forward(idx[0]), dot_nt(q, far_all[:, :HD]) * SCALE, NEG)
     top = jnp.max(s, axis=1, keepdims=True)
     p = jnp.exp(s - top)
     total = jnp.sum(p, axis=1, keepdims=True)
     o3 = dot_nn(p.astype(BF), far_all[:, HD : 2 * HD]) / total
     l3 = top + jnp.log(total)
-    o12, l12, g = far_in[0], far_in[1], far_in[2]
+    o12 = jnp.concatenate([own_ref[:16], mate_ref[:16]], 0)
+    l12 = jnp.concatenate([own_ref[16:32], mate_ref[16:32]], 0)
+    g = jnp.concatenate([own_ref[32:48], mate_ref[32:48]], 0)
     peak = jnp.maximum(l12, l3)
     e12, e3 = jnp.exp(l12 - peak), jnp.exp(l3 - peak)
     den = e12 + e3
     at = ((e12 * o12 + e3 * o3) / den).astype(BF).astype(F32)
-    patch_ref[0] = at
-    patch_ref[1] = peak + jnp.log(den)
-    lane, row = iota((16, HD), 1), iota((16, HD), 0)
-    slot = (row & 7) * 16 + idx[1] * 2 + (row >> 3)
+    patch_ref[:32] = at
+    patch_ref[32:] = peak + jnp.log(den)
+    stat_ref[:32, :] = own_ref[48:]
+    stat_ref[32:, :] = mate_ref[48:]
+    lane, row = iota((32, HD), 1), iota((32, HD), 0)
+    here = lane == idx[1] * 2 + ((row >> 3) & 1)
     for k, term in enumerate((at, at * at, g * at)):
-        mine = jnp.sum(term, axis=1, keepdims=True)
-        own_scr[k : k + 1, :] = jnp.sum(jnp.where(lane == slot, mine, 0.0), axis=0, keepdims=True)
-    own_scr[3:4, :] = jnp.zeros((1, HD), F32)
-    own = own_scr[...]
-    for i in range(8):
-        cols = slice(i * 128, (i + 1) * 128)
-        mine = jnp.concatenate([own[:, i * 16 : (i + 1) * 16], jnp.zeros((4, HD - 16), F32)], 1)
-        stat_ref[:, cols] = stat_in[:, cols] + mine
-
-
-def far_grad_kernel(idx, stat_ref, far_in, patch_ref, pack_ref, tall_scr, col_scr):
-    for i in range(8):
-        tall_scr[i * 4 : (i + 1) * 4, :] = stat_ref[:, i * 128 : (i + 1) * 128]
-    lane32 = iota((32, HD), 1)
+        mine = jnp.where(here, jnp.sum(term, axis=1, keepdims=True), 0.0)
+        for half in range(2):
+            both = mine[half * 16 : half * 16 + 8] + mine[half * 16 + 8 : half * 16 + 16]
+            rows = pl.ds(half * 32 + k, 8, stride=4)
+            stat_ref[rows, :] = stat_ref[rows, :] + both
+
+
+def far_grad_kernel(idx, stat_ref, own_ref, mate_ref, patch_ref, pack_ref, col_scr):
+    lane64 = iota((64, HD), 1)
     sums = [[], [], [], []]
-    for j in range(2):
-        cs = col_scr.at[j]
-        chosen = jnp.where(lane32 == idx[1] * 2 + j, tall_scr[...], 0.0)
-        cs[...] = jnp.broadcast_to(jnp.sum(chosen, axis=1, keepdims=True), (32, HD))
-        for k in range(4):
-            sums[k].append(cs[pl.ds(k, 8, stride=4), :])
-    mean, rstd, sg, sgx = norm_terms(*(jnp.concatenate(pair, 0) for pair in sums))
-    at = patch_ref[0]
+    for half in range(2):
+        for j in range(2):
+            cs = col_scr.at[half * 2 + j]
+            chosen = jnp.where(lane64 == idx[1] * 2 + j, stat_ref[...], 0.0)
+            cs[...] = jnp.broadcast_to(jnp.sum(chosen, axis=1, keepdims=True), (64, HD))
+            for k in range(4):
+                sums[k].append(cs[pl.ds(half * 32 + k, 8, stride=4), :])
+    mean, rstd, sg, sgx = norm_terms(*(jnp.concatenate(part, 0) for part in sums))
+    at = patch_ref[:32]
+    g = jnp.concatenate([own_ref[32:48], mate_ref[32:48]], 0)
     x = (at - mean) * rstd
-    grad = (rstd * (far_in[2] - sg - x * sgx)).astype(BF)
+    grad = (rstd * (g - sg - x * sgx)).astype(BF)
     delta = jnp.sum(grad.astype(F32) * at, axis=1, keepdims=True)
     pack_ref[:, :HD] = grad
-    delta = jnp.broadcast_to(delta, (16, HD))
-    pack_ref[:, HD:] = stat_pack(patch_ref[1], delta, iota((16, HD), 1)).astype(BF)
+    delta = jnp.broadcast_to(delta, (32, HD))
+    pack_ref[:, HD:] = stat_pack(patch_ref[32:], delta, iota((32, HD), 1)).astype(BF)
+
+
+def stat_cols(pack):
+    pack = pack.astype(F32)
+    lse = pack[:, 0:1] + pack[:, 1:2] + pack[:, 2:3]
+    delta = pack[:, 3:4] + pack[:, 4:5] + pack[:, 5:6]
+    return lse, delta
+
+
+def far_query_kernel(idx, far_all, pack_ref, stat_ref, patch_ref, keep_ref, reply_ref):
+    k_all, v_all = far_all[:, :HD], far_all[:, HD : 2 * HD]
+    lse, delta = stat_cols(pack_ref[:, HD:])
+    keep = far_keep_forward(idx[0])
+    s = jnp.where(keep, dot_nt(far_all[:32, 2 * HD :], k_all) * SCALE, NEG)
+    p = jnp.exp(s - lse)
+    ds = (p * (dot_nt(pack_ref[:, :HD], v_all) - delta)).astype(BF)
+    dq = dot_nn(ds, k_all) * SCALE
+    for half, out in enumerate((keep_ref, reply_ref)):
+        out[:32, :] = stat_ref[half * 32 : half * 32 + 32, :]
+        out[32:48, :] = patch_ref[half * 16 : half * 16 + 16, :]
+        out[48:64, :] = patch_ref[32 + half * 16 : 48 + half * 16, :]
+        out[64:80, :] = dq[half * 16 : half * 16 + 16]
 
 
 def norm_kernel(
     idx,
-    stat_ref,
+    keep_in,
+    reply_in,
     att_ref,
     g_ref,
     lse_in,
-    patch_ref,
     normed_ref,
     grad_ref,
     delta_ref,
@@ -250,18 +278,18 @@
     att_scr,
     pack_scr,
 ):
+    share = own_share(idx, keep_in, reply_in)
     for j in range(2):
         distant = pl.ds(idx[1] * 2 + j, 8, stride=128)
-        own = slice(j * 8, (j + 1) * 8)
         at, lse = att_scr.at[j], lse_ref.at[j]
         at[...] = att_ref[:, j * HD : (j + 1) * HD].astype(F32)
-        at[distant, :] = patch_ref[0, own, :]
+        at[distant, :] = share[32 + j * 8 : 40 + j * 8]
         lse[...] = lse_in[j]
-        lse[distant, :] = patch_ref[1, own, :]
+        lse[distant, :] = share[48 + j * 8 : 56 + j * 8]
     lane = iota((128, HD), 1)
     for b in range(8):
         rows = slice(b * 128, (b + 1) * 128)
-        stats = stat_ref[:, rows]
+        stats = share[b * 4 : b * 4 + 4]
         terms = norm_terms(stats[0:1], stats[1:2], stats[2:3], stats[3:4])
         cols = jnp.concatenate(list(terms) + [jnp.zeros((124, HD), F32)], 0).T
         mean, rstd, sg, sgx = (cols[:, i : i + 1] for i in range(4))
@@ -308,24 +336,9 @@
             dq_ref[0, rows, :] += dq
 
 
-def query_grad_kernel(idx, dq0, dq1, mid_ref, far_ref, mid_g, far_g, out_ref, scr, far_scr):
+def query_grad_kernel(idx, dq0, dq1, mid_ref, mid_g, keep_in, reply_in, out_ref, scr, far_scr):
     s_idx = idx[0]
-
-    def stat_cols(pack):
-        pack = pack.astype(F32)
-        lse = pack[:, 0:1] + pack[:, 1:2] + pack[:, 2:3]
-        delta = pack[:, 3:4] + pack[:, 4:5] + pack[:, 5:6]
-        return lse, delta
-
-    k_all, v_all = far_ref[:, :HD], far_ref[:, HD : 2 * HD]
-    lse, delta = stat_cols(far_g[:, HD:])
-    s = jnp.where(
-        far_keep_forward(s_idx), dot_nt(far_ref[:16, 2 * HD :], k_all) * SCALE, NEG
-    )
-    p = jnp.exp(s - lse)
-    ds = (p * (dot_nt(far_g[:, :HD], v_all) - delta)).astype(BF)
-    far_dq = dot_nn(ds, k_all) * SCALE
-
+    far_dq = own_share(idx, keep_in, reply_in)[64:80]
     key_slot = mid_slots(s_idx, (128, SEG), 1)
     query_slot = (s_idx & 3) * 128 + iota((128, SEG), 0)
     keep = key_slot <= query_slot
@@ -355,70 +368,64 @@
         out_ref[:, j * HD : (j + 1) * HD] = sc[...].astype(BF)
 
 
-def key_grad_kernel(
-    idx,
-    dk0,
-    dk1,
-    dv0,
-    dv1,
-    mid_ref,
-    far_all,
-    grads,
-    dk_out,
-    dv_out,
-    whole_ref,
-    scr,
-    far_scr,
-):
-    s_idx = idx[0]
-    lane = iota((8, HD), 1)
-    row = iota((8, HD), 0)
+def stat_rows(packs):
+    lane, row = iota((8, HD), 1), iota((8, HD), 0)
     pick = ((row == lane // 3) & (lane < 6)).astype(F32).astype(BF)
-
-    far_g = jnp.concatenate([grads[:512, :], grads[1024:1536, :]], 0)
-    mid_g = jnp.concatenate([grads[512:1024, :], grads[1536:, :]], 0)
-    stats = dot_nt(pick, far_g[:, HD:])
-    lse, delta = stats[0:1], stats[1:2]
-    keep = far_keep_backward(s_idx)
-    k, v = far_all[:16, :HD], far_all[:16, HD : 2 * HD]
-    q_all, g_all = far_all[:, 2 * HD :], far_g[:, :HD]
-    s = jnp.where(keep, dot_nt(k, q_all) * SCALE, NEG)
+    stats = dot_nt(pick, packs)
+    return stats[0:1], stats[1:2]
+
+
+def far_key_kernel(idx, far_all, grads, keep_ref, reply_ref):
+    lse, delta = stat_rows(grads[:, HD:])
+    k, v = far_all[:32, :HD], far_all[:32, HD : 2 * HD]
+    q_all, g_all = far_all[:, 2 * HD :], grads[:, :HD]
+    s = jnp.where(far_keep_backward(idx[0]), dot_nt(k, q_all) * SCALE, NEG)
     p = jnp.exp(s - lse)
     ds = (p * (dot_nt(v, g_all) - delta)).astype(BF)
-    far_dk = dot_nn(ds, q_all) * SCALE
-    far_dv = dot_nn(p.astype(BF), g_all)
-    for j in range(2):
-        whole_ref[0, :, j * HD : (j + 1) * HD] = far_dk[j * 8 : (j + 1) * 8]
-        whole_ref[1, :, j * HD : (j + 1) * HD] = far_dv[j * 8 : (j + 1) * 8]
-
-    stats = dot_nt(pick, mid_g[:, HD:])
+    dk = dot_nn(ds, q_all) * SCALE
+    dv = dot_nn(p.astype(BF), g_all)
+    for half, out in enumerate((keep_ref, reply_ref)):
+        out[:16, :] = dk[half * 16 : half * 16 + 16]
+        out[16:, :] = dv[half * 16 : half * 16 + 16]
+
+
+def mid_key_kernel(idx, dk0, dk1, dv0, dv1, mid_ref, grads, dk_ref, dv_ref):
+    s_idx = idx[0]
+    all_lse, all_delta = stat_rows(grads[:, HD:])
     query_slot = mid_slots(s_idx, (128, SEG), 1)
     key_slot = (s_idx & 3) * 128 + iota((128, SEG), 0)
     keep = key_slot <= query_slot
     for j in range(2):
-        head = idx[1] * 2 + j
         own = slice(j * 128, (j + 1) * 128)
         places = [slice(p * 256 + j * 128, p * 256 + (j + 1) * 128) for p in range(4)]
         k, v = mid_ref[own, :HD], mid_ref[own, HD : 2 * HD]
         q = jnp.concatenate([mid_ref[r, 2 * HD :] for r in places], 0)
-        g = jnp.concatenate([mid_g[r, :HD] for r in places], 0)
-        lse = jnp.concatenate([stats[0:1, r] for r in places], 1)
-        delta = jnp.concatenate([stats[1:2, r] for r in places], 1)
+        g = jnp.concatenate([grads[r, :HD] for r in places], 0)
+        lse = jnp.concatenate([all_lse[:, r] for r in places], 1)
+        delta = jnp.concatenate([all_delta[:, r] for r in places], 1)
         s = jnp.where(keep, dot_nt(k, q) * SCALE, NEG)
         p = jnp.exp(s - lse)
         ds = (p * (dot_nt(v, g) - delta)).astype(BF)
-        mid_dk = dot_nn(ds, q) * SCALE
-        mid_dv = dot_nn(p.astype(BF), g)
-        spread = pl.ds(head // 8, 8, stride=16)
-        picked = pl.ds(lax.rem(head, 8), 128, stride=8)
-        for a, (mid, far, near0, near1, out) in enumerate(
-            ((mid_dk, far_dk, dk0, dk1, dk_out), (mid_dv, far_dv, dv0, dv1, dv_out))
+        picked = pl.ds(lax.rem(idx[1] * 2 + j, 8), 128, stride=8)
+        for near0, near1, mid, out_ref in (
+            (dk0, dk1, dot_nn(ds, q) * SCALE, dk_ref),
+            (dv0, dv1, dot_nn(p.astype(BF), g), dv_ref),
         ):
-            fs, sc = far_scr.at[j * 2 + a], scr.at[j * 2 + a]
-            fs[...] = mid
-            fs[spread, :] = fs[spread, :] + far[j * 8 : (j + 1) * 8]
-            sc[:SEG, :], sc[SEG:, :] = near0[j], near1[j]
-            sc[picked, :] = sc[picked, :] + fs[...]
+            out = out_ref.at[j]
+            out[:SEG, :], out[SEG:, :] = near0[j], near1[j]
+            out[picked, :] = out[picked, :] + mid
+
+
+def key_grad_kernel(idx, dk_in, dv_in, keep_in, reply_in, dk_out, dv_out, whole_ref, scr):
+    share = own_share(idx, keep_in, reply_in)
+    for j in range(2):
+        distant = pl.ds(idx[1] * 2 + j, 8, stride=128)
+        for a, (near, out) in enumerate(((dk_in, dk_out), (dv_in, dv_out))):
+            far = share[a * 16 + j * 8 : a * 16 + j * 8 + 8]
+            whole_ref[a, :, j * HD : (j + 1) * HD] = far
+            sc = scr.at[j * 2 + a]
+            sc[...] = near[j]
+            sc[distant, :] = sc[distant, :] + far
             out[:, j * HD : (j + 1) * HD] = sc[...].astype(BF)
 
 
@@ -426,15 +433,21 @@
     return lax.ppermute(x, "seq", [(i, i ^ bit) for i in range(64)])
 
 
-def head_exchange(x, bit):
-    return lax.ppermute(x, "head", [(i, i ^ bit) for i in range(8)])
-
-
-def round_of_y(x, to_pair):
-    from_far = exchange(x, 4)
-    from_pair = exchange(to_pair, 2)
-    from_next = exchange(x, 6)
-    return from_pair, from_far, from_next
+def odd_exchange(x, bit):
+    return lax.ppermute(x, "seq", [(i, i ^ bit) for i in range(1, 64, 2)])
+
+
+def odd_head_exchange(x, bit):
+    pairs = [(s * 8 + h, s * 8 + (h ^ bit)) for s in range(1, 64, 2) for h in range(8)]
+    return lax.ppermute(x, ("seq", "head"), pairs)
+
+
+def to_odd(x):
+    return lax.ppermute(x, "seq", [(i, i + 1) for i in range(0, 64, 2)])
+
+
+def to_even(x):
+    return lax.ppermute(x, "seq", [(i + 1, i) for i in range(0, 64, 2)])
 
 
 def joined(a, b):
@@ -484,15 +497,17 @@
             name=f"near_forward_{block}",
         )(queries, keys, values)
 
+    mate_far = to_odd(far0)
     mid1 = exchange(mid0, 2)
-    far1 = exchange(far0, 32)
+    far1 = joined(far0, mate_far)
+    from1 = odd_exchange(far1, 32)
     near0 = near_forward(0)
-    mid_two, far_two, near0 = after((joined(mid0, mid1), joined(far0, far1), near0))
+    mid_two, far2, near0 = after((joined(mid0, mid1), joined(far1, from1), near0))
     mid2 = exchange(mid_two, 1)
-    far2 = exchange(far_two, 16)
+    from2 = odd_exchange(far2, 16)
     near1 = near_forward(1)
-    far_four, near1 = after((joined(far_two, far2), near1))
-    far4 = exchange(far_four, 8)
+    far4, near1 = after((joined(far2, from2), near1))
+    from4 = odd_exchange(far4, 8)
     mid_all = joined(mid_two, mid2)
     mid_o, mid_lse = pl.pallas_call(
         mid_forward_kernel,
@@ -504,54 +519,58 @@
         name="mid_forward",
     )(idx, mid_all)
 
-    att, lse12, stats, far_in = pl.pallas_call(
+    far8, mid_o = after((joined(far4, from4), mid_o))
+    from8 = odd_exchange(far8, 4)
+    att, lse12, bundle = pl.pallas_call(
         pre_kernel,
-        out_shape=(
-            sds((TOK, 256), BF),
-            by_head_shape,
-            sds((4, TOK), F32),
-            sds((3, 16, HD), F32),
-        ),
+        out_shape=(sds((TOK, 256), BF), by_head_shape, sds((80, HD), F32)),
         in_specs=[SMEM] + [VMEM] * 7,
-        out_specs=(VMEM,) * 4,
+        out_specs=(VMEM,) * 3,
         scratch_shapes=[pltpu.VMEM((2, TOK, HD), F32)],
         compiler_params=PARAMS,
         cost_estimate=cost(10**7, 4 * 10**6, 10**5),
         name="pre",
     )(idx, *near0, *near1, mid_o, mid_lse, out_grad)
-
-    far_eight, mid_o = after((joined(far_four, far4), mid_o))
-    far_y = [far_eight] + list(round_of_y(far_eight, far_eight))
-    far_y, stats = after((jnp.concatenate(far_y, 0), stats))
-    far_all = joined(far_y, exchange(far_y, 1))
+    far16, bundle = after((joined(far8, from8), bundle))
+    from16 = odd_exchange(far16, 2)
+    mate_bundle = to_odd(bundle)
+    far_all = joined(far16, from16)
 
     patch, stats = pl.pallas_call(
         far_forward_kernel,
-        out_shape=(sds((2, 16, HD), F32), sds((4, TOK), F32)),
+        out_shape=(sds((64, HD), F32), sds((64, HD), F32)),
         in_specs=[SMEM] + [VMEM] * 3,
         out_specs=(VMEM,) * 2,
-        scratch_shapes=[pltpu.VMEM((4, HD), F32)],
         compiler_params=PARAMS,
         cost_estimate=cost(10**7, 10**6, 10**5),
         name="far_forward",
-    )(idx, far_all, far_in, stats)
+    )(idx, far_all, bundle, mate_bundle)
 
     for bit in (2, 1, 4):
-        stats = stats + head_exchange(stats, bit)
+        stats = stats + odd_head_exchange(stats, bit)
 
     far_g = pl.pallas_call(
         far_grad_kernel,
-        out_shape=sds((16, 256), BF),
-        in_specs=[SMEM] + [VMEM] * 3,
+        out_shape=sds((32, 256), BF),
+        in_specs=[SMEM] + [VMEM] * 4,
         out_specs=VMEM,
-        scratch_shapes=[pltpu.VMEM((32, HD), F32), pltpu.VMEM((2, 32, HD), F32)],
+        scratch_shapes=[pltpu.VMEM((4, 64, HD), F32)],
         compiler_params=PARAMS,
         cost_estimate=cost(10**6, 10**5),
         name="far_grad",
-    )(idx, stats, far_in, patch)
-
-    stats, far_g = after((stats, far_g))
-    part1 = exchange(far_g, 32)
+    )(idx, stats, bundle, mate_bundle, patch)
+
+    part1 = odd_exchange(far_g, 32)
+    keep, reply = pl.pallas_call(
+        far_query_kernel,
+        out_shape=(sds((80, HD), F32), sds((80, HD), F32)),
+        in_specs=[SMEM] + [VMEM] * 4,
+        out_specs=(VMEM,) * 2,
+        compiler_params=PARAMS,
+        cost_estimate=cost(10**7, 10**6, 10**5),
+        name="far_query",
+    )(idx, far_all, far_g, stats, patch)
+    reply = to_even(reply)
     normed, grad, delta, lse, mid_g = pl.pallas_call(
         norm_kernel,
         out_shape=(
@@ -567,7 +586,7 @@
         compiler_params=PARAMS,
         cost_estimate=cost(10**7, 4 * 10**6),
         name="norm",
-    )(idx, stats, att, out_grad, lse12, patch)
+    )(idx, keep, reply, att, out_grad, lse12)
 
     def near_backward(block):
         part = pl.BlockSpec((SEG, HD), lambda j: (block, j))
@@ -584,13 +603,15 @@
         )(queries, keys, values, grad, lse, delta)
 
     part_a, mid_g = after((joined(far_g, part1), mid_g))
-    part2 = exchange(part_a, 16)
+    part2 = odd_exchange(part_a, 16)
+    mid_g1 = exchange(mid_g, 2)
     dq0, dk0, dv0 = near_backward(0)
     part_b, dq0 = after((joined(part_a, part2), dq0))
-    part3 = exchange(part_b, 8)
+    part3 = odd_exchange(part_b, 8)
     dq1, dk1, dv1 = near_backward(1)
-    part_c, dq1 = after((joined(part_b, part3), dq1))
-    sent2, sent4, sent6 = round_of_y(part_c, joined(part_c, mid_g))
+    part_c, mid_gs, dq1 = after((joined(part_b, part3), joined(mid_g, mid_g1), dq1))
+    part4 = odd_exchange(part_c, 4)
+    mid_g2 = exchange(mid_gs, 1)
 
     grad_queries = pl.pallas_call(
         query_grad_kernel,
@@ -601,22 +622,41 @@
         compiler_params=PARAMS,
         cost_estimate=cost(2 * 10**8, 3 * 10**6, 10**5),
         name="query_grad",
-    )(idx, dq0, dq1, mid_all, far_all, mid_g, far_g)
-
-    sent = jnp.concatenate([part_c, sent2[:128], sent4, sent6, mid_g, sent2[128:]], 0)
-    sent, grad_queries = after((sent, grad_queries))
-    grads = joined(sent, exchange(sent, 1))
+    )(idx, dq0, dq1, mid_all, mid_g, keep, reply)
+
+    part_d, grad_queries = after((joined(part_c, part4), grad_queries))
+    part5 = odd_exchange(part_d, 2)
+    dk, dv = pl.pallas_call(
+        mid_key_kernel,
+        out_shape=(by_head_shape, by_head_shape),
+        in_specs=[SMEM] + [VMEM] * 6,
+        out_specs=(VMEM,) * 2,
+        compiler_params=PARAMS,
+        cost_estimate=cost(2 * 10**8, 4 * 10**6, 10**5),
+        name="mid_key",
+    )(idx, dk0, dk1, dv0, dv1, mid_all, joined(mid_gs, mid_g2))
+    far_gs, dk = after((joined(part_d, part5), dk))
+
+    keep, reply = pl.pallas_call(
+        far_key_kernel,
+        out_shape=(sds((32, HD), F32), sds((32, HD), F32)),
+        in_specs=[SMEM] + [VMEM] * 2,
+        out_specs=(VMEM,) * 2,
+        compiler_params=PARAMS,
+        cost_estimate=cost(10**7, 10**6, 10**5),
+        name="far_key",
+    )(idx, far_all, far_gs)
 
     grad_keys, grad_values, whole = pl.pallas_call(
         key_grad_kernel,
         out_shape=(sds((TOK, 256), BF), sds((TOK, 256), BF), sds((2, 8, 256), F32)),
-        in_specs=[SMEM] + [VMEM] * 7,
+        in_specs=[SMEM] + [VMEM] * 4,
         out_specs=(VMEM,) * 3,
-        scratch_shapes=[pltpu.VMEM((4, TOK, HD), F32), pltpu.VMEM((4, 128, HD), F32)],
-        compiler_params=PARAMS,
-        cost_estimate=cost(2 * 10**8, 4 * 10**6, 10**5),
+        scratch_shapes=[pltpu.VMEM((4, TOK, HD), F32)],
+        compiler_params=PARAMS,
+        cost_estimate=cost(10**6, 4 * 10**6),
         name="key_grad",
-    )(idx, dk0, dk1, dv0, dv1, mid_all, far_all, grads)
+    )(idx, dk, dv, keep, to_even(reply))
 
     return normed, grad_queries, grad_keys, grad_values, whole
 

time: 130 us -> 127 us (0.977)
  starting transfers between devices: 90.2 us -> 72.7 us
  waiting for transfers between devices: 12.1 us -> 24.9 us
  Pallas kernels: 21.9 us -> 23.9 us
    ppermute x16 -> x4, starting transfers between devices: 69.7 us -> 9.95 us  [exchange(): return lax.ppermute(x, 'seq', [(i, i ^ bit) for i in range(64)])]
    ppermute x3 -> x17, starting transfers between devices: 20.5 us -> 62.8 us  [the longest x10 38.5 us: odd_exchange(): return lax.ppermute(x, 'seq', [(i, i ^ bit) for i in range(1, 64, 2)])]
    ppermute x3 -> x17, waiting for transfers between devices: 4.69 us -> 24.9 us  [the longest x10 14.7 us: odd_exchange(): return lax.ppermute(x, 'seq', [(i, i ^ bit) for i in range(1, 64, 2)])]
    ppermute x16 -> x4, waiting for transfers between devices: 7.41 us -> 0.01 us  [exchange(): return lax.ppermute(x, 'seq', [(i, i ^ bit) for i in range(64)])]
    pallas_call x2 -> x5, Pallas kernels: 1.85 us -> 5.2 us  [the longest x1 1.4 us: local(): pl.pallas_call(mid_key_kernel, out_shape=(by_head_shape, by_head_shape),...]
    unnamed x21 -> x16, local copies, waits for them, and re-layouts: 3.26 us -> 3.22 us
  transfers between devices with their start and end apart: 19 -> 21, of which waited for: 8 -> 12; matrix products, arithmetic and copies ran while one was open for 0% -> 0% of each run, Pallas kernels for 12% -> 11%
where the time goes in v2:
time: 127 us; the launch traced here: 126 us
  starting transfers between devices  72.7 us (57%)
  waiting for transfers between devices  24.9 us (20%)
  Pallas kernels  23.9 us (19%)
  local copies, waits for them, and re-layouts  3.35 us (3%)
    ppermute x10, starting transfers between devices, odd_exchange(): return lax.ppermute(x, 'seq', [(i, i ^ bit) for i in range(1, 64, 2)])  38.5 us
    ppermute x3, starting transfers between devices, odd_head_exchange(): return lax.ppermute(x, ('seq', 'head'), pairs)  19.1 us
    ppermute x10, waiting for transfers between devices, odd_exchange(): return lax.ppermute(x, 'seq', [(i, i ^ bit) for i in range(1, 64, 2)])  14.7 us
    ppermute x4, starting transfers between devices, exchange(): return lax.ppermute(x, 'seq', [(i, i ^ bit) for i in range(64)])  9.95 us
    ppermute x3, waiting for transfers between devices, odd_head_exchange(): return lax.ppermute(x, ('seq', 'head'), pairs)  5.08 us
    pallas_call x2, Pallas kernels, near_backward(): pl.pallas_call(near_backward_kernel, grid=(2,), out_shape=(half_shape,) *...  4.25 us
    ppermute x2, waiting for transfers between devices, to_odd(): return lax.ppermute(x, 'seq', [(i, i + 1) for i in range(0, 64, 2)])  3.49 us
    pallas_call x2, Pallas kernels, near_forward(): pl.pallas_call(near_forward_kernel, grid=(2,), out_shape=(half_shape, hal...  3.43 us
  transfers between devices with their start and end apart: 21, of which 12 were waited for; matrix products, arithmetic and copies ran while one was open for 0% of the time, Pallas kernels for 11%

profile of v2, /device:TPU:1, one launch (start us, length us, event | category | flops | bytes accessed | tf_op | source)
XLA Modules:
  0.0 126.4 jit_solution(10657568888695265148)
XLA Ops:
  6.0 4.0 %collective-permute-start = (bf16[256,384]{1,0:T(8,128)(2,1)S(1)}, bf16[256,384]{1,0:T(8,128)(2,1)S(1)}, u32[]{:S(2)}, u32[]{:S(2)}) collective-permute-start(bf16[256,384]{1,0:T(8,128)(2,1)S(1)} %get-tuple-element.60), channel_id=1, source_target_pairs={{0,16},{8,24},{16,0},{24,8},{32,48},{40,56},{48,32},{56,40},{64,80... | collective-permute-start | bytes 589832 | tf_op jit(solution)/shard_map/ppermute | solution.py:433
  10.1 3.5 %collective-permute-done.1 = bf16[16,384]{1,0:T(8,128)(2,1)S(1)} collective-permute-done((bf16[16,384]{1,0:T(8,128)(2,1)S(1)}, bf16[16,384]{1,0:T(8,128)(2,1)S(1)}, u32[]{:S(2)}, u32[]{:S(2)}) %collective-permute-start.1) | collective-permute-done | bytes 12320 | tf_op jit(solution)/shard_map/ppermute | solution.py:446
  13.6 5.4 %collective-permute-start.2 = (bf16[32,384]{1,0:T(8,128)(2,1)S(1)}, bf16[32,384]{1,0:T(8,128)(2,1)S(1)}, u32[]{:S(2)}, u32[]{:S(2)}) collective-permute-start(bf16[32,384]{1,0:T(8,128)(2,1)S(1)} %pad_maximum_fusion.12), channel_id=1, source_target_pairs={{8,264},{24,280},{40,296},{56,312},{72,328},{88,344},{104,360},{12... | collective-permute-start | bytes 73736 | tf_op jit(solution)/shard_map/ppermute | solution.py:437
  19.0 1.7 %near_forward_0.1 = (f32[2,512,128]{2,1,0:T(8,128)S(1)}, f32[2,512,128]{2,1,0:T(8,128)S(1)}) custom-call(bf16[1024,256]{1,0:T(8,128)(2,1)S(1)} %copy-done.1, bf16[1024,256]{1,0:T(8,128)(2,1)S(1)} %copy-done.3, bf16[1024,256]{1,0:T(8,128)(2,1)S(1)} %copy-done.5), custom_call_target="tpu_custom_call" | custom-call | flops 400000000 | bytes 2000000 | tf_op jit(solution)/shard_map/near_forward_0/pallas_call | solution.py:489
  22.1 3.6 %collective-permute-start.3 = (bf16[64,384]{1,0:T(8,128)(2,1)S(1)}, bf16[64,384]{1,0:T(8,128)(2,1)S(1)}, u32[]{:S(2)}, u32[]{:S(2)}) collective-permute-start(bf16[64,384]{1,0:T(8,128)(2,1)S(1)} %pad_maximum_fusion.10), channel_id=1, source_target_pairs={{8,136},{24,152},{40,168},{56,184},{72,200},{88,216},{104,232},{12... | collective-permute-start | bytes 147464 | tf_op jit(solution)/shard_map/ppermute | solution.py:437
  25.7 1.9 %collective-permute-start.5 = (bf16[512,384]{1,0:T(8,128)(2,1)S(1)}, bf16[512,384]{1,0:T(8,128)(2,1)S(1)}, u32[]{:S(2)}, u32[]{:S(2)}) collective-permute-start(bf16[512,384]{1,0:T(8,128)(2,1)S(1)} %pad_maximum_fusion.2), channel_id=1, source_target_pairs={{0,8},{8,0},{16,24},{24,16},{32,40},{40,32},{48,56},{56,48},{64,72... | collective-permute-start | bytes 1179656 | tf_op jit(solution)/shard_map/ppermute | solution.py:433
  27.6 1.7 %near_forward_1.1 = (f32[2,512,128]{2,1,0:T(8,128)S(1)}, f32[2,512,128]{2,1,0:T(8,128)S(1)}) custom-call(bf16[1024,256]{1,0:T(8,128)(2,1)S(1)} %copy-done.1, bf16[1024,256]{1,0:T(8,128)(2,1)S(1)} %copy-done.3, bf16[1024,256]{1,0:T(8,128)(2,1)S(1)} %copy-done.5), custom_call_target="tpu_custom_call" | custom-call | flops 400000000 | bytes 2000000 | tf_op jit(solution)/shard_map/near_forward_1/pallas_call | solution.py:489
  29.4 3.5 %collective-permute-start.4 = (bf16[128,384]{1,0:T(8,128)(2,1)S(1)}, bf16[128,384]{1,0:T(8,128)(2,1)S(1)}, u32[]{:S(2)}, u32[]{:S(2)}) collective-permute-start(bf16[128,384]{1,0:T(8,128)(2,1)S(1)} %pad_maximum_fusion.8), channel_id=1, source_target_pairs={{8,72},{24,88},{40,104},{56,120},{72,8},{88,24},{104,40},{120,56},... | collective-permute-start | bytes 294920 | tf_op jit(solution)/shard_map/ppermute | solution.py:437
  33.0 1.9 %collective-permute-done.4 = bf16[128,384]{1,0:T(8,128)(2,1)S(1)} collective-permute-done((bf16[128,384]{1,0:T(8,128)(2,1)S(1)}, bf16[128,384]{1,0:T(8,128)(2,1)S(1)}, u32[]{:S(2)}, u32[]{:S(2)}) %collective-permute-start.4) | collective-permute-done | bytes 98336 | tf_op jit(solution)/shard_map/ppermute | solution.py:437
  36.2 4.5 %collective-permute-start.6 = (bf16[256,384]{1,0:T(8,128)(2,1)S(1)}, bf16[256,384]{1,0:T(8,128)(2,1)S(1)}, u32[]{:S(2)}, u32[]{:S(2)}) collective-permute-start(bf16[256,384]{1,0:T(8,128)(2,1)S(1)} %pad_maximum_fusion.6), channel_id=1, source_target_pairs={{8,40},{24,56},{40,8},{56,24},{72,104},{88,120},{104,72},{120,88},... | collective-permute-start | bytes 589832 | tf_op jit(solution)/shard_map/ppermute | solution.py:437
  40.8 1.8 %pre.1 = (bf16[1024,256]{1,0:T(8,128)(2,1)S(1)}, f32[2,1024,128]{2,1,0:T(8,128)S(1)}, f32[80,128]{1,0:T(8,128)S(1)}) custom-call(s32[2]{0:T(128)S(1)} %pad_add_fusion.idx, f32[2,512,128]{2,1,0:T(8,128)S(1)} %get-tuple-element.71.o0, f32[2,512,128]{2,1,0:T(8,128)S(1)} %get-tuple-element.72.lse0, f32[2,512,128]{2,1,0:T(8,128)S(1)} %get-tuple-element.73.o1, ...), custom_call_target="tpu_custom_call" | custom-call | flops 10000000 | bytes 4000000 | tf_op jit(solution)/shard_map/pre/pallas_call | solution.py:524
  42.6 1.6 %collective-permute-done.6 = bf16[256,384]{1,0:T(8,128)(2,1)S(1)} collective-permute-done((bf16[256,384]{1,0:T(8,128)(2,1)S(1)}, bf16[256,384]{1,0:T(8,128)(2,1)S(1)}, u32[]{:S(2)}, u32[]{:S(2)}) %collective-permute-start.6) | collective-permute-done | bytes 196640 | tf_op jit(solution)/shard_map/ppermute | solution.py:437
  44.2 2.1 %collective-permute-start.7 = (bf16[512,384]{1,0:T(8,128)(2,1)S(1)}, bf16[512,384]{1,0:T(8,128)(2,1)S(1)}, u32[]{:S(2)}, u32[]{:S(2)}) collective-permute-start(bf16[512,384]{1,0:T(8,128)(2,1)S(1)} %pad_maximum_fusion.3), channel_id=1, source_target_pairs={{8,24},{24,8},{40,56},{56,40},{72,88},{88,72},{104,120},{120,104},... | collective-permute-start | bytes 1179656 | tf_op jit(solution)/shard_map/ppermute | solution.py:437
  47.6 5.1 %collective-permute-done.7 = bf16[512,384]{1,0:T(8,128)(2,1)S(1)} collective-permute-done((bf16[512,384]{1,0:T(8,128)(2,1)S(1)}, bf16[512,384]{1,0:T(8,128)(2,1)S(1)}, u32[]{:S(2)}, u32[]{:S(2)}) %collective-permute-start.7) | collective-permute-done | bytes 393248 | tf_op jit(solution)/shard_map/ppermute | solution.py:437
  53.9 4.7 %collective-permute-start.9 = (f32[64,128]{1,0:T(8,128)S(1)}, f32[64,128]{1,0:T(8,128)S(1)}, u32[]{:S(2)}, u32[]{:S(2)}) collective-permute-start(f32[64,128]{1,0:T(8,128)S(1)} %get-tuple-element.80), channel_id=1, source_target_pairs={{8,10},{9,11},{10,8},{11,9},{12,14},{13,15},{14,12},{15,13},{24,26... | collective-permute-start | bytes 98312 | tf_op jit(solution)/shard_map/ppermute | solution.py:442
  60.0 3.1 %collective-permute-start.10 = (f32[64,128]{1,0:T(8,128)S(1)}, f32[64,128]{1,0:T(8,128)S(1)}, u32[]{:S(2)}, u32[]{:S(2)}) collective-permute-start(f32[64,128]{1,0:T(8,128)S(1)} %add.9), channel_id=1, source_target_pairs={{8,9},{9,8},{10,11},{11,10},{12,13},{13,12},{14,15},{15,14},{24,25... | collective-permute-start | bytes 98312 | tf_op jit(solution)/shard_map/ppermute | solution.py:442
  63.2 1.5 %collective-permute-done.10 = f32[64,128]{1,0:T(8,128)S(1)} collective-permute-done((f32[64,128]{1,0:T(8,128)S(1)}, f32[64,128]{1,0:T(8,128)S(1)}, u32[]{:S(2)}, u32[]{:S(2)}) %collective-permute-start.10) | collective-permute-done | bytes 32800 | tf_op jit(solution)/shard_map/ppermute | solution.py:442
  64.7 11.3 %collective-permute-start.11 = (f32[64,128]{1,0:T(8,128)S(1)}, f32[64,128]{1,0:T(8,128)S(1)}, u32[]{:S(2)}, u32[]{:S(2)}) collective-permute-start(f32[64,128]{1,0:T(8,128)S(1)} %add.10), channel_id=1, source_target_pairs={{8,12},{9,13},{10,14},{11,15},{12,8},{13,9},{14,10},{15,11},{24,28... | collective-permute-start | bytes 98312 | tf_op jit(solution)/shard_map/ppermute | solution.py:442
  76.0 2.1 %collective-permute-done.11 = f32[64,128]{1,0:T(8,128)S(1)} collective-permute-done((f32[64,128]{1,0:T(8,128)S(1)}, f32[64,128]{1,0:T(8,128)S(1)}, u32[]{:S(2)}, u32[]{:S(2)}) %collective-permute-start.11) | collective-permute-done | bytes 32800 | tf_op jit(solution)/shard_map/ppermute | solution.py:442
  78.9 6.8 %collective-permute-start.13 = (bf16[32,256]{1,0:T(8,128)(2,1)S(1)}, bf16[32,256]{1,0:T(8,128)(2,1)S(1)}, u32[]{:S(2)}, u32[]{:S(2)}) collective-permute-start(bf16[32,256]{1,0:T(8,128)(2,1)S(1)} %far_grad.1.pack_ref), channel_id=1, source_target_pairs={{8,264},{24,280},{40,296},{56,312},{72,328},{88,344},{104,360},{12... | collective-permute-start | bytes 49160 | tf_op jit(solution)/shard_map/ppermute | solution.py:437
  88.7 3.2 %norm.1 = (bf16[1024,256]{1,0:T(8,128)(2,1)}, bf16[1024,256]{1,0:T(8,128)(2,1)S(1)}, f32[2,1024,128]{2,1,0:T(8,128)S(1)}, f32[2,1024,128]{2,1,0:T(8,128)S(1)}, bf16[256,256]{1,0:T(8,128)(2,1)S(1)}) custom-call(s32[2]{0:T(128)S(1)} %pad_add_fusion.idx, f32[80,128]{1,0:T(8,128)S(1)} %get-tuple-element.82.keep_in, ...), custom_call_target="tpu_custom_call" | custom-call | flops 10000000 | bytes 4000000 | tf_op jit(solution)/shard_map/norm/pallas_call | solution.py:574
  91.9 2.1 %collective-permute-start.16 = (bf16[256,256]{1,0:T(8,128)(2,1)S(1)}, bf16[256,256]{1,0:T(8,128)(2,1)S(1)}, u32[]{:S(2)}, u32[]{:S(2)}) collective-permute-start(bf16[256,256]{1,0:T(8,128)(2,1)S(1)} %get-tuple-element.94.mid_g), channel_id=1, source_target_pairs={{0,16},{8,24},{16,0},{24,8},{32,48},{40,56},{48,32},{56,40},{64,80... | collective-permute-start | bytes 393224 | tf_op jit(solution)/shard_map/ppermute | solution.py:433
  94.0 2.0 %collective-permute-start.14 = (bf16[64,256]{1,0:T(8,128)(2,1)S(1)}, bf16[64,256]{1,0:T(8,128)(2,1)S(1)}, u32[]{:S(2)}, u32[]{:S(2)}) collective-permute-start(bf16[64,256]{1,0:T(8,128)(2,1)S(1)} %pad_maximum_fusion.11), channel_id=1, source_target_pairs={{8,136},{24,152},{40,168},{56,184},{72,200},{88,216},{104,232},{12... | collective-permute-start | bytes 98312 | tf_op jit(solution)/shard_map/ppermute | solution.py:437
  96.0 2.1 %near_backward_0.1 = (f32[2,512,128]{2,1,0:T(8,128)S(1)}, f32[2,512,128]{2,1,0:T(8,128)S(1)}, f32[2,512,128]{2,1,0:T(8,128)S(1)}) custom-call(bf16[1024,256]{1,0:T(8,128)(2,1)S(1)} %copy-done.1, bf16[1024,256]{1,0:T(8,128)(2,1)S(1)} %copy-done.3, bf16[1024,256]{1,0:T(8,128)(2,1)S(1)} %copy-done.5, bf16[1024,256]{1,0:T(8,128)(2,1)S(1)} %get-tuple-element.89.g_ref, ...), custom_call_target="tpu_custom_call" | custom-call | flops 1000000000 | bytes 4000000 | tf_op jit(solution)/shard_map/near_backward_0/pallas_call | solution.py:594
  99.6 3.5 %collective-permute-start.15 = (bf16[128,256]{1,0:T(8,128)(2,1)S(1)}, bf16[128,256]{1,0:T(8,128)(2,1)S(1)}, u32[]{:S(2)}, u32[]{:S(2)}) collective-permute-start(bf16[128,256]{1,0:T(8,128)(2,1)S(1)} %pad_maximum_fusion.9), channel_id=1, source_target_pairs={{8,72},{24,88},{40,104},{56,120},{72,8},{88,24},{104,40},{120,56},... | collective-permute-start | bytes 196616 | tf_op jit(solution)/shard_map/ppermute | solution.py:437
  103.1 2.1 %near_backward_1.1 = (f32[2,512,128]{2,1,0:T(8,128)S(1)}, f32[2,512,128]{2,1,0:T(8,128)S(1)}, f32[2,512,128]{2,1,0:T(8,128)S(1)}) custom-call(bf16[1024,256]{1,0:T(8,128)(2,1)S(1)} %copy-done.1, bf16[1024,256]{1,0:T(8,128)(2,1)S(1)} %copy-done.3, bf16[1024,256]{1,0:T(8,128)(2,1)S(1)} %copy-done.5, bf16[1024,256]{1,0:T(8,128)(2,1)S(1)} %get-tuple-element.89.g_ref, ...), custom_call_target="tpu_custom_call" | custom-call | flops 1000000000 | bytes 4000000 | tf_op jit(solution)/shard_map/near_backward_1/pallas_call | solution.py:594
  105.3 4.8 %collective-permute-start.17 = (bf16[256,256]{1,0:T(8,128)(2,1)S(1)}, bf16[256,256]{1,0:T(8,128)(2,1)S(1)}, u32[]{:S(2)}, u32[]{:S(2)}) collective-permute-start(bf16[256,256]{1,0:T(8,128)(2,1)S(1)} %pad_maximum_fusion.7), channel_id=1, source_target_pairs={{8,40},{24,56},{40,8},{56,24},{72,104},{88,120},{104,72},{120,88},... | collective-permute-start | bytes 393224 | tf_op jit(solution)/shard_map/ppermute | solution.py:437
  110.2 1.9 %collective-permute-start.19 = (bf16[512,256]{1,0:T(8,128)(2,1)S(1)}, bf16[512,256]{1,0:T(8,128)(2,1)S(1)}, u32[]{:S(2)}, u32[]{:S(2)}) collective-permute-start(bf16[512,256]{1,0:T(8,128)(2,1)S(1)} %pad_maximum_fusion.4), channel_id=1, source_target_pairs={{0,8},{8,0},{16,24},{24,16},{32,40},{40,32},{48,56},{56,48},{64,72... | collective-permute-start | bytes 786440 | tf_op jit(solution)/shard_map/ppermute | solution.py:433
  112.1 2.1 %query_grad.1 = bf16[1024,256]{1,0:T(8,128)(2,1)} custom-call(s32[2]{0:T(128)S(1)} %pad_add_fusion.idx, f32[2,512,128]{2,1,0:T(8,128)S(1)} %get-tuple-element.97.dq0, f32[2,512,128]{2,1,0:T(8,128)S(1)} %get-tuple-element.98.dq1, bf16[1024,384]{1,0:T(8,128)(2,1)S(1)} %constant_dynamic-update-slice_fusion.mid_ref, ...), custom_call_target="tpu_custom_call" | custom-call | flops 200000000 | bytes 3000000 | tf_op jit(solution)/shard_map/query_grad/pallas_call | solution.py:616
  114.2 2.3 %collective-permute-start.18 = (bf16[512,256]{1,0:T(8,128)(2,1)S(1)}, bf16[512,256]{1,0:T(8,128)(2,1)S(1)}, u32[]{:S(2)}, u32[]{:S(2)}) collective-permute-start(bf16[512,256]{1,0:T(8,128)(2,1)S(1)} %pad_maximum_fusion.5), channel_id=1, source_target_pairs={{8,24},{24,8},{40,56},{56,40},{72,88},{88,72},{104,120},{120,104},... | collective-permute-start | bytes 786440 | tf_op jit(solution)/shard_map/ppermute | solution.py:437
  118.0 3.3 %collective-permute-done.18 = bf16[512,256]{1,0:T(8,128)(2,1)S(1)} collective-permute-done((bf16[512,256]{1,0:T(8,128)(2,1)S(1)}, bf16[512,256]{1,0:T(8,128)(2,1)S(1)}, u32[]{:S(2)}, u32[]{:S(2)}) %collective-permute-start.18) | collective-permute-done | bytes 262176 | tf_op jit(solution)/shard_map/ppermute | solution.py:437
  124.5 1.8 %key_grad.1 = (bf16[1024,256]{1,0:T(8,128)(2,1)}, bf16[1024,256]{1,0:T(8,128)(2,1)}, f32[2,8,256]{2,1,0:T(8,128)}) custom-call(s32[2]{0:T(128)S(1)} %pad_add_fusion.idx, f32[2,1024,128]{2,1,0:T(8,128)S(1)} %get-tuple-element.107.dk_in, f32[2,1024,128]{2,1,0:T(8,128)S(1)} %get-tuple-element.108.dv_in, f32[32,128]{1,0:T(8,128)S(1)} %get-tuple-element.110.keep_in, ...), custom_call_target="tpu_custom_call" | custom-call | flops 1000000 | bytes 4000000 | tf_op jit(solution)/shard_map/key_grad/pallas_call | solution.py:650
  (60 shorter events, 22.1 us)
Async XLA Ops:
  0.7 1.0 copy-start
  1.8 1.0 copy-start.2
  2.8 1.0 copy-start.4
  3.8 15.1 %copy-start.1 = (bf16[1024,256]{1,0:T(8,128)(2,1)S(1)}, bf16[1024,256]{1,0:T(8,128)(2,1)}, u32[]{:S(2)}) copy-start(bf16[1024,256]{1,0:T(8,128)(2,1)} %q_ref.9) | copy-start | bytes 1572868
  3.8 15.1 %copy-start.3 = (bf16[1024,256]{1,0:T(8,128)(2,1)S(1)}, bf16[1024,256]{1,0:T(8,128)(2,1)}, u32[]{:S(2)}) copy-start(bf16[1024,256]{1,0:T(8,128)(2,1)} %k_ref.9) | copy-start | bytes 1572868
  3.8 15.1 %copy-start.5 = (bf16[1024,256]{1,0:T(8,128)(2,1)S(1)}, bf16[1024,256]{1,0:T(8,128)(2,1)}, u32[]{:S(2)}) copy-start(bf16[1024,256]{1,0:T(8,128)(2,1)} %v_ref.9) | copy-start | bytes 1572868
  4.7 8.8 %collective-permute-start.1 = (bf16[16,384]{1,0:T(8,128)(2,1)S(1)}, bf16[16,384]{1,0:T(8,128)(2,1)S(1)}, u32[]{:S(2)}, u32[]{:S(2)}) collective-permute-start(bf16[16,384]{1,0:T(8,128)(2,1)S(1)} %get-tuple-element.61), channel_id=1, source_target_pairs={{0,8},{16,24},{32,40},{48,56},{64,72},{80,88},{96,104},{112,120},{... | collective-permute-start | bytes 36872 | tf_op jit(solution)/shard_map/ppermute | solution.py:446
  6.0 16.0 %collective-permute-start = (bf16[256,384]{1,0:T(8,128)(2,1)S(1)}, bf16[256,384]{1,0:T(8,128)(2,1)S(1)}, u32[]{:S(2)}, u32[]{:S(2)}) collective-permute-start(bf16[256,384]{1,0:T(8,128)(2,1)S(1)} %get-tuple-element.60), channel_id=1, source_target_pairs={{0,16},{8,24},{16,0},{24,8},{32,48},{40,56},{48,32},{56,40},{64,80... | collective-permute-start | bytes 589832 | tf_op jit(solution)/shard_map/ppermute | solution.py:433
  13.6 8.5 %collective-permute-start.2 = (bf16[32,384]{1,0:T(8,128)(2,1)S(1)}, bf16[32,384]{1,0:T(8,128)(2,1)S(1)}, u32[]{:S(2)}, u32[]{:S(2)}) collective-permute-start(bf16[32,384]{1,0:T(8,128)(2,1)S(1)} %pad_maximum_fusion.12), channel_id=1, source_target_pairs={{8,264},{24,280},{40,296},{56,312},{72,328},{88,344},{104,360},{12... | collective-permute-start | bytes 73736 | tf_op jit(solution)/shard_map/ppermute | solution.py:437
  22.1 7.2 %collective-permute-start.3 = (bf16[64,384]{1,0:T(8,128)(2,1)S(1)}, bf16[64,384]{1,0:T(8,128)(2,1)S(1)}, u32[]{:S(2)}, u32[]{:S(2)}) collective-permute-start(bf16[64,384]{1,0:T(8,128)(2,1)S(1)} %pad_maximum_fusion.10), channel_id=1, source_target_pairs={{8,136},{24,152},{40,168},{56,184},{72,200},{88,216},{104,232},{12... | collective-permute-start | bytes 147464 | tf_op jit(solution)/shard_map/ppermute | solution.py:437
  25.7 9.2 %collective-permute-start.5 = (bf16[512,384]{1,0:T(8,128)(2,1)S(1)}, bf16[512,384]{1,0:T(8,128)(2,1)S(1)}, u32[]{:S(2)}, u32[]{:S(2)}) collective-permute-start(bf16[512,384]{1,0:T(8,128)(2,1)S(1)} %pad_maximum_fusion.2), channel_id=1, source_target_pairs={{0,8},{8,0},{16,24},{24,16},{32,40},{40,32},{48,56},{56,48},{64,72... | collective-permute-start | bytes 1179656 | tf_op jit(solution)/shard_map/ppermute | solution.py:433
  29.4 5.5 %collective-permute-start.4 = (bf16[128,384]{1,0:T(8,128)(2,1)S(1)}, bf16[128,384]{1,0:T(8,128)(2,1)S(1)}, u32[]{:S(2)}, u32[]{:S(2)}) collective-permute-start(bf16[128,384]{1,0:T(8,128)(2,1)S(1)} %pad_maximum_fusion.8), channel_id=1, source_target_pairs={{8,72},{24,88},{40,104},{56,120},{72,8},{88,24},{104,40},{120,56},... | collective-permute-start | bytes 294920 | tf_op jit(solution)/shard_map/ppermute | solution.py:437
  35.0 5.8 %copy-start.6 = (bf16[1024,256]{1,0:T(8,128)(2,1)S(1)}, bf16[1024,256]{1,0:T(8,128)(2,1)}, u32[]{:S(2)}) copy-start(bf16[1024,256]{1,0:T(8,128)(2,1)} %g_ref.3) | copy-start | bytes 1572868
  36.2 7.9 %collective-permute-start.6 = (bf16[256,384]{1,0:T(8,128)(2,1)S(1)}, bf16[256,384]{1,0:T(8,128)(2,1)S(1)}, u32[]{:S(2)}, u32[]{:S(2)}) collective-permute-start(bf16[256,384]{1,0:T(8,128)(2,1)S(1)} %pad_maximum_fusion.6), channel_id=1, source_target_pairs={{8,40},{24,56},{40,8},{56,24},{72,104},{88,120},{104,72},{120,88},... | collective-permute-start | bytes 589832 | tf_op jit(solution)/shard_map/ppermute | solution.py:437
  44.2 8.5 %collective-permute-start.7 = (bf16[512,384]{1,0:T(8,128)(2,1)S(1)}, bf16[512,384]{1,0:T(8,128)(2,1)S(1)}, u32[]{:S(2)}, u32[]{:S(2)}) collective-permute-start(bf16[512,384]{1,0:T(8,128)(2,1)S(1)} %pad_maximum_fusion.3), channel_id=1, source_target_pairs={{8,24},{24,8},{40,56},{56,40},{72,88},{88,72},{104,120},{120,104},... | collective-permute-start | bytes 1179656 | tf_op jit(solution)/shard_map/ppermute | solution.py:437
  46.3 6.5 %collective-permute-start.8 = (f32[80,128]{1,0:T(8,128)S(1)}, f32[80,128]{1,0:T(8,128)S(1)}, u32[]{:S(2)}, u32[]{:S(2)}) collective-permute-start(f32[80,128]{1,0:T(8,128)S(1)} %get-tuple-element.79.own_ref), channel_id=1, source_target_pairs={{0,8},{16,24},{32,40},{48,56},{64,72},{80,88},{96,104},{112,120},{... | collective-permute-start | bytes 122888 | tf_op jit(solution)/shard_map/ppermute | solution.py:446
  53.9 6.2 %collective-permute-start.9 = (f32[64,128]{1,0:T(8,128)S(1)}, f32[64,128]{1,0:T(8,128)S(1)}, u32[]{:S(2)}, u32[]{:S(2)}) collective-permute-start(f32[64,128]{1,0:T(8,128)S(1)} %get-tuple-element.80), channel_id=1, source_target_pairs={{8,10},{9,11},{10,8},{11,9},{12,14},{13,15},{14,12},{15,13},{24,26... | collective-permute-start | bytes 98312 | tf_op jit(solution)/shard_map/ppermute | solution.py:442
  60.0 4.6 %collective-permute-start.10 = (f32[64,128]{1,0:T(8,128)S(1)}, f32[64,128]{1,0:T(8,128)S(1)}, u32[]{:S(2)}, u32[]{:S(2)}) collective-permute-start(f32[64,128]{1,0:T(8,128)S(1)} %add.9), channel_id=1, source_target_pairs={{8,9},{9,8},{10,11},{11,10},{12,13},{13,12},{14,15},{15,14},{24,25... | collective-permute-start | bytes 98312 | tf_op jit(solution)/shard_map/ppermute | solution.py:442
  64.7 13.4 %collective-permute-start.11 = (f32[64,128]{1,0:T(8,128)S(1)}, f32[64,128]{1,0:T(8,128)S(1)}, u32[]{:S(2)}, u32[]{:S(2)}) collective-permute-start(f32[64,128]{1,0:T(8,128)S(1)} %add.10), channel_id=1, source_target_pairs={{8,12},{9,13},{10,14},{11,15},{12,8},{13,9},{14,10},{15,11},{24,28... | collective-permute-start | bytes 98312 | tf_op jit(solution)/shard_map/ppermute | solution.py:442
  78.9 9.0 %collective-permute-start.13 = (bf16[32,256]{1,0:T(8,128)(2,1)S(1)}, bf16[32,256]{1,0:T(8,128)(2,1)S(1)}, u32[]{:S(2)}, u32[]{:S(2)}) collective-permute-start(bf16[32,256]{1,0:T(8,128)(2,1)S(1)} %far_grad.1.pack_ref), channel_id=1, source_target_pairs={{8,264},{24,280},{40,296},{56,312},{72,328},{88,344},{104,360},{12... | collective-permute-start | bytes 49160 | tf_op jit(solution)/shard_map/ppermute | solution.py:437
  86.6 2.1 %collective-permute-start.12 = (f32[80,128]{1,0:T(8,128)S(1)}, f32[80,128]{1,0:T(8,128)S(1)}, u32[]{:S(2)}, u32[]{:S(2)}) collective-permute-start(f32[80,128]{1,0:T(8,128)S(1)} %get-tuple-element.83), channel_id=1, source_target_pairs={{8,0},{24,16},{40,32},{56,48},{72,64},{88,80},{104,96},{120,112},{... | collective-permute-start | bytes 122888 | tf_op jit(solution)/shard_map/ppermute | solution.py:450
  91.9 13.4 %collective-permute-start.16 = (bf16[256,256]{1,0:T(8,128)(2,1)S(1)}, bf16[256,256]{1,0:T(8,128)(2,1)S(1)}, u32[]{:S(2)}, u32[]{:S(2)}) collective-permute-start(bf16[256,256]{1,0:T(8,128)(2,1)S(1)} %get-tuple-element.94.mid_g), channel_id=1, source_target_pairs={{0,16},{8,24},{16,0},{24,8},{32,48},{40,56},{48,32},{56,40},{64,80... | collective-permute-start | bytes 393224 | tf_op jit(solution)/shard_map/ppermute | solution.py:433
  94.0 5.6 %collective-permute-start.14 = (bf16[64,256]{1,0:T(8,128)(2,1)S(1)}, bf16[64,256]{1,0:T(8,128)(2,1)S(1)}, u32[]{:S(2)}, u32[]{:S(2)}) collective-permute-start(bf16[64,256]{1,0:T(8,128)(2,1)S(1)} %pad_maximum_fusion.11), channel_id=1, source_target_pairs={{8,136},{24,152},{40,168},{56,184},{72,200},{88,216},{104,232},{12... | collective-permute-start | bytes 98312 | tf_op jit(solution)/shard_map/ppermute | solution.py:437
  99.6 5.7 %collective-permute-start.15 = (bf16[128,256]{1,0:T(8,128)(2,1)S(1)}, bf16[128,256]{1,0:T(8,128)(2,1)S(1)}, u32[]{:S(2)}, u32[]{:S(2)}) collective-permute-start(bf16[128,256]{1,0:T(8,128)(2,1)S(1)} %pad_maximum_fusion.9), channel_id=1, source_target_pairs={{8,72},{24,88},{40,104},{56,120},{72,8},{88,24},{104,40},{120,56},... | collective-permute-start | bytes 196616 | tf_op jit(solution)/shard_map/ppermute | solution.py:437
  105.3 8.8 %collective-permute-start.17 = (bf16[256,256]{1,0:T(8,128)(2,1)S(1)}, bf16[256,256]{1,0:T(8,128)(2,1)S(1)}, u32[]{:S(2)}, u32[]{:S(2)}) collective-permute-start(bf16[256,256]{1,0:T(8,128)(2,1)S(1)} %pad_maximum_fusion.7), channel_id=1, source_target_pairs={{8,40},{24,56},{40,8},{56,24},{72,104},{88,120},{104,72},{120,88},... | collective-permute-start | bytes 393224 | tf_op jit(solution)/shard_map/ppermute | solution.py:437
  110.2 6.4 %collective-permute-start.19 = (bf16[512,256]{1,0:T(8,128)(2,1)S(1)}, bf16[512,256]{1,0:T(8,128)(2,1)S(1)}, u32[]{:S(2)}, u32[]{:S(2)}) collective-permute-start(bf16[512,256]{1,0:T(8,128)(2,1)S(1)} %pad_maximum_fusion.4), channel_id=1, source_target_pairs={{0,8},{8,0},{16,24},{24,16},{32,40},{40,32},{48,56},{56,48},{64,72... | collective-permute-start | bytes 786440 | tf_op jit(solution)/shard_map/ppermute | solution.py:433
  114.2 7.1 %collective-permute-start.18 = (bf16[512,256]{1,0:T(8,128)(2,1)S(1)}, bf16[512,256]{1,0:T(8,128)(2,1)S(1)}, u32[]{:S(2)}, u32[]{:S(2)}) collective-permute-start(bf16[512,256]{1,0:T(8,128)(2,1)S(1)} %pad_maximum_fusion.5), channel_id=1, source_target_pairs={{8,24},{24,8},{40,56},{56,40},{72,88},{88,72},{104,120},{120,104},... | collective-permute-start | bytes 786440 | tf_op jit(solution)/shard_map/ppermute | solution.py:437
  122.4 2.1 %collective-permute-start.20 = (f32[32,128]{1,0:T(8,128)S(1)}, f32[32,128]{1,0:T(8,128)S(1)}, u32[]{:S(2)}, u32[]{:S(2)}) collective-permute-start(f32[32,128]{1,0:T(8,128)S(1)} %get-tuple-element.111), channel_id=1, source_target_pairs={{8,0},{24,16},{40,32},{56,48},{72,64},{88,80},{104,96},{120,112},{... | collective-permute-start | bytes 49160 | tf_op jit(solution)/shard_map/ppermute | solution.py:450

commit v3 on v2

--- a/solution.py
+++ b/solution.py
@@ -113,14 +113,14 @@
     n, row = iota((32, 1024), 1), iota((32, 1024), 0)
     pos = n // 32
     flips = (pos & 1) * 32 + (pos & 2) * 8 + (pos & 4) * 2 + ((pos & 8) >> 1) + ((pos & 16) >> 3)
-    place = (s ^ flips ^ ((n >> 4) & 1)) * 8 + (n & 7)
-    mine = (s ^ (row >> 4)) * 8 + (row & 7)
+    place = (((s | 1) ^ flips) - ((n >> 4) & 1)) * 8 + (n & 7)
+    mine = ((s | 1) - (row >> 4)) * 8 + (row & 7)
     return ((n >> 3) & 1) == ((row >> 3) & 1), place, mine
 
 
-def own_share(idx, keep_ref, reply_ref):
-    odd = (iota(keep_ref.shape, 0) * 0 + (idx[0] & 1)) == 1
-    return jnp.where(odd, keep_ref[...], reply_ref[...])
+def by_parity(idx, if_odd, if_even):
+    odd = (iota(if_odd.shape, 0) * 0 + (idx[0] & 1)) == 1
+    return jnp.where(odd, if_odd, if_even)
 
 
 def far_keep_forward(s):
@@ -191,7 +191,7 @@
     return pack
 
 
-def far_forward_kernel(idx, far_all, own_ref, mate_ref, patch_ref, stat_ref):
+def far_kernel(idx, far_all, own_ref, mate_ref, packs_ref, fix_ref, col_scr):
     q = far_all[:32, 2 * HD :]
     s = jnp.where(far_keep_forward(idx[0]), dot_nt(q, far_all[:, :HD]) * SCALE, NEG)
     top = jnp.max(s, axis=1, keepdims=True)
@@ -205,40 +205,40 @@
     peak = jnp.maximum(l12, l3)
     e12, e3 = jnp.exp(l12 - peak), jnp.exp(l3 - peak)
     den = e12 + e3
-    at = ((e12 * o12 + e3 * o3) / den).astype(BF).astype(F32)
-    patch_ref[:32] = at
-    patch_ref[32:] = peak + jnp.log(den)
-    stat_ref[:32, :] = own_ref[48:]
-    stat_ref[32:, :] = mate_ref[48:]
-    lane, row = iota((32, HD), 1), iota((32, HD), 0)
-    here = lane == idx[1] * 2 + ((row >> 3) & 1)
-    for k, term in enumerate((at, at * at, g * at)):
-        mine = jnp.where(here, jnp.sum(term, axis=1, keepdims=True), 0.0)
-        for half in range(2):
-            both = mine[half * 16 : half * 16 + 8] + mine[half * 16 + 8 : half * 16 + 16]
-            rows = pl.ds(half * 32 + k, 8, stride=4)
-            stat_ref[rows, :] = stat_ref[rows, :] + both
-
-
-def far_grad_kernel(idx, stat_ref, own_ref, mate_ref, patch_ref, pack_ref, col_scr):
+    at16 = ((e12 * o12 + e3 * o3) / den).astype(BF)
+    at = at16.astype(F32)
+    lse = peak + jnp.log(den)
+
+    others = [[], [], [], []]
     lane64 = iota((64, HD), 1)
-    sums = [[], [], [], []]
     for half in range(2):
         for j in range(2):
             cs = col_scr.at[half * 2 + j]
-            chosen = jnp.where(lane64 == idx[1] * 2 + j, stat_ref[...], 0.0)
+            chosen = jnp.where(lane64 == idx[1] * 2 + j, mate_ref[48:], 0.0)
             cs[...] = jnp.broadcast_to(jnp.sum(chosen, axis=1, keepdims=True), (64, HD))
             for k in range(4):
-                sums[k].append(cs[pl.ds(half * 32 + k, 8, stride=4), :])
-    mean, rstd, sg, sgx = norm_terms(*(jnp.concatenate(part, 0) for part in sums))
-    at = patch_ref[:32]
-    g = jnp.concatenate([own_ref[32:48], mate_ref[32:48]], 0)
+                others[k].append(cs[pl.ds(half * 32 + k, 8, stride=4), :])
+    others = [jnp.concatenate(part, 0) for part in others]
+    lane, row = iota((32, HD), 1), iota((32, HD), 0)
+    here = lane == (row & 7) * 16 + idx[1] * 2 + ((row >> 3) & 1)
+    sums = []
+    fix_ref[...] = jnp.zeros((8, HD), F32)
+    for k, term in enumerate((at, at * at, g * at)):
+        mine = jnp.sum(term, axis=1, keepdims=True)
+        sums.append(others[k] + mine)
+        placed = jnp.where(here, mine, 0.0)
+        for half in range(2):
+            own = placed[half * 16 : half * 16 + 16]
+            fix_ref[half * 4 + k : half * 4 + k + 1, :] = jnp.sum(own, axis=0, keepdims=True)
+    mean, rstd, sg, sgx = norm_terms(sums[0], sums[1], sums[2], others[3])
     x = (at - mean) * rstd
     grad = (rstd * (g - sg - x * sgx)).astype(BF)
     delta = jnp.sum(grad.astype(F32) * at, axis=1, keepdims=True)
-    pack_ref[:, :HD] = grad
+    packs_ref[:32, :HD] = grad
     delta = jnp.broadcast_to(delta, (32, HD))
-    pack_ref[:, HD:] = stat_pack(patch_ref[32:], delta, iota((32, HD), 1)).astype(BF)
+    packs_ref[:32, HD:] = stat_pack(lse, delta, lane).astype(BF)
+    packs_ref[32:, :HD] = at16
+    packs_ref[32:, HD:] = at16
 
 
 def stat_cols(pack):
@@ -248,25 +248,26 @@
     return lse, delta
 
 
-def far_query_kernel(idx, far_all, pack_ref, stat_ref, patch_ref, keep_ref, reply_ref):
-    k_all, v_all = far_all[:, :HD], far_all[:, HD : 2 * HD]
-    lse, delta = stat_cols(pack_ref[:, HD:])
-    keep = far_keep_forward(idx[0])
-    s = jnp.where(keep, dot_nt(far_all[:32, 2 * HD :], k_all) * SCALE, NEG)
-    p = jnp.exp(s - lse)
-    ds = (p * (dot_nt(pack_ref[:, :HD], v_all) - delta)).astype(BF)
-    dq = dot_nn(ds, k_all) * SCALE
-    for half, out in enumerate((keep_ref, reply_ref)):
-        out[:32, :] = stat_ref[half * 32 : half * 32 + 32, :]
-        out[32:48, :] = patch_ref[half * 16 : half * 16 + 16, :]
-        out[48:64, :] = patch_ref[32 + half * 16 : 48 + half * 16, :]
-        out[64:80, :] = dq[half * 16 : half * 16 + 16]
+def far_query_kernel(idx, far_all, packs, dq_ref):
+    @pl.when((idx[0] & 1) == 0)
+    def _():
+        k_all, v_all = far_all[:, :HD], far_all[:, HD : 2 * HD]
+        lse, delta = stat_cols(packs[:32, HD:])
+        keep = far_keep_forward(idx[0])
+        s = jnp.where(keep, dot_nt(far_all[:32, 2 * HD :], k_all) * SCALE, NEG)
+        p = jnp.exp(s - lse)
+        ds = (p * (dot_nt(packs[:32, :HD], v_all) - delta)).astype(BF)
+        dq_ref[...] = dot_nn(ds, k_all) * SCALE
 
 
 def norm_kernel(
     idx,
-    keep_in,
-    reply_in,
+    mate_ref,
+    stat_ref,
+    fix_own,
+    fix_got,
+    packs_own,
+    packs_got,
     att_ref,
     g_ref,
     lse_in,
@@ -276,23 +277,34 @@
     lse_ref,
     mid_ref,
     att_scr,
-    pack_scr,
+    sum_scr,
 ):
-    share = own_share(idx, keep_in, reply_in)
+    sums = by_parity(idx, mate_ref[48:80], stat_ref[32:])
+    fixes = by_parity(idx, fix_own[:4], fix_got[4:])
+    far_at = by_parity(
+        idx, packs_own[32:48, :HD].astype(F32), packs_got[48:, :HD].astype(F32)
+    )
+    far_stat = by_parity(
+        idx, packs_own[:16, HD:].astype(F32), packs_got[16:32, HD:].astype(F32)
+    )
+    far_lse = jnp.broadcast_to(stat_cols(far_stat)[0], (16, HD))
     for j in range(2):
         distant = pl.ds(idx[1] * 2 + j, 8, stride=128)
         at, lse = att_scr.at[j], lse_ref.at[j]
         at[...] = att_ref[:, j * HD : (j + 1) * HD].astype(F32)
-        at[distant, :] = share[32 + j * 8 : 40 + j * 8]
+        at[distant, :] = far_at[j * 8 : j * 8 + 8]
         lse[...] = lse_in[j]
-        lse[distant, :] = share[48 + j * 8 : 56 + j * 8]
-    lane = iota((128, HD), 1)
+        lse[distant, :] = far_lse[j * 8 : j * 8 + 8]
+    for b in range(8):
+        fix = jnp.concatenate(
+            [fixes[:, b * 16 : (b + 1) * 16], jnp.zeros((4, HD - 16), F32)], 1
+        )
+        sum_scr[b * 4 : b * 4 + 4, :] = sums[b * 4 : b * 4 + 4] + fix
+    terms = norm_terms(*(sum_scr[pl.ds(k, 8, stride=4), :] for k in range(4)))
+    cols = jnp.concatenate(list(terms) + [jnp.zeros((96, HD), F32)], 0).T
     for b in range(8):
         rows = slice(b * 128, (b + 1) * 128)
-        stats = share[b * 4 : b * 4 + 4]
-        terms = norm_terms(stats[0:1], stats[1:2], stats[2:3], stats[3:4])
-        cols = jnp.concatenate(list(terms) + [jnp.zeros((124, HD), F32)], 0).T
-        mean, rstd, sg, sgx = (cols[:, i : i + 1] for i in range(4))
+        mean, rstd, sg, sgx = (cols[:, i * 8 + b : i * 8 + b + 1] for i in range(4))
         for j in range(2):
             at = att_scr[j, rows, :]
             x = (at - mean) * rstd
@@ -301,14 +313,16 @@
             grad = (rstd * (g - sg - x * sgx)).astype(BF)
             grad_ref[rows, j * HD : (j + 1) * HD] = grad
             grad = grad.astype(F32)
-            delta = jnp.broadcast_to(jnp.sum(grad * at, axis=1, keepdims=True), (128, HD))
-            delta_ref[j, rows, :] = delta
+            delta = jnp.sum(grad * at, axis=1, keepdims=True)
+            delta_ref[j, rows, :] = jnp.broadcast_to(delta, (128, HD))
             att_scr[j, rows, :] = grad
-            pack_scr[j, rows, :] = stat_pack(lse_ref[j, rows, :], delta, lane)
+    lane = iota((128, HD), 1)
     for j in range(2):
         picked = pl.ds(lax.rem(idx[1] * 2 + j, 8), 128, stride=8)
-        mid_ref[j * 128 : (j + 1) * 128, :HD] = att_scr.at[j][picked, :].astype(BF)
-        mid_ref[j * 128 : (j + 1) * 128, HD:] = pack_scr.at[j][picked, :].astype(BF)
+        own = slice(j * 128, (j + 1) * 128)
+        mid_ref[own, :HD] = att_scr.at[j][picked, :].astype(BF)
+        pack = stat_pack(lse_ref.at[j][picked, :], delta_ref.at[j][picked, :], lane)
+        mid_ref[own, HD:] = pack.astype(BF)
 
 
 def near_backward_kernel(
@@ -336,9 +350,9 @@
             dq_ref[0, rows, :] += dq
 
 
-def query_grad_kernel(idx, dq0, dq1, mid_ref, mid_g, keep_in, reply_in, out_ref, scr, far_scr):
+def query_grad_kernel(idx, dq0, dq1, mid_ref, mid_g, dq_got, dq_own, out_ref, scr, far_scr):
     s_idx = idx[0]
-    far_dq = own_share(idx, keep_in, reply_in)[64:80]
+    far_dq = by_parity(idx, dq_got[:16], dq_own[16:])
     key_slot = mid_slots(s_idx, (128, SEG), 1)
     query_slot = (s_idx & 3) * 128 + iota((128, SEG), 0)
     keep = key_slot <= query_slot
@@ -375,18 +389,17 @@
     return stats[0:1], stats[1:2]
 
 
-def far_key_kernel(idx, far_all, grads, keep_ref, reply_ref):
-    lse, delta = stat_rows(grads[:, HD:])
-    k, v = far_all[:32, :HD], far_all[:32, HD : 2 * HD]
-    q_all, g_all = far_all[:, 2 * HD :], grads[:, :HD]
-    s = jnp.where(far_keep_backward(idx[0]), dot_nt(k, q_all) * SCALE, NEG)
-    p = jnp.exp(s - lse)
-    ds = (p * (dot_nt(v, g_all) - delta)).astype(BF)
-    dk = dot_nn(ds, q_all) * SCALE
-    dv = dot_nn(p.astype(BF), g_all)
-    for half, out in enumerate((keep_ref, reply_ref)):
-        out[:16, :] = dk[half * 16 : half * 16 + 16]
-        out[16:, :] = dv[half * 16 : half * 16 + 16]
+def far_key_kernel(idx, far_all, grads, out_ref):
+    @pl.when((idx[0] & 1) == 0)
+    def _():
+        lse, delta = stat_rows(grads[:, HD:])
+        k, v = far_all[:32, :HD], far_all[:32, HD : 2 * HD]
+        q_all, g_all = far_all[:, 2 * HD :], grads[:, :HD]
+        s = jnp.where(far_keep_backward(idx[0]), dot_nt(k, q_all) * SCALE, NEG)
+        p = jnp.exp(s - lse)
+        ds = (p * (dot_nt(v, g_all) - delta)).astype(BF)
+        out_ref[:32, :] = dot_nn(ds, q_all) * SCALE
+        out_ref[32:, :] = dot_nn(p.astype(BF), g_all)
 
 
 def mid_key_kernel(idx, dk0, dk1, dv0, dv1, mid_ref, grads, dk_ref, dv_ref):
@@ -416,12 +429,12 @@
             out[picked, :] = out[picked, :] + mid
 
 
-def key_grad_kernel(idx, dk_in, dv_in, keep_in, reply_in, dk_out, dv_out, whole_ref, scr):
-    share = own_share(idx, keep_in, reply_in)
+def key_grad_kernel(idx, dk_in, dv_in, far_got, far_own, dk_out, dv_out, whole_ref, scr):
     for j in range(2):
         distant = pl.ds(idx[1] * 2 + j, 8, stride=128)
         for a, (near, out) in enumerate(((dk_in, dk_out), (dv_in, dv_out))):
-            far = share[a * 16 + j * 8 : a * 16 + j * 8 + 8]
+            row = a * 32 + j * 8
+            far = by_parity(idx, far_got[row : row + 8], far_own[row + 16 : row + 24])
             whole_ref[a, :, j * HD : (j + 1) * HD] = far
             sc = scr.at[j * 2 + a]
             sc[...] = near[j]
@@ -433,12 +446,12 @@
     return lax.ppermute(x, "seq", [(i, i ^ bit) for i in range(64)])
 
 
-def odd_exchange(x, bit):
-    return lax.ppermute(x, "seq", [(i, i ^ bit) for i in range(1, 64, 2)])
-
-
-def odd_head_exchange(x, bit):
-    pairs = [(s * 8 + h, s * 8 + (h ^ bit)) for s in range(1, 64, 2) for h in range(8)]
+def chip_exchange(x, bit, parity):
+    return lax.ppermute(x, "seq", [(i, i ^ bit) for i in range(parity, 64, 2)])
+
+
+def head_exchange(x, bit, parity):
+    pairs = [(s * 8 + h, s * 8 + (h ^ bit)) for s in range(parity, 64, 2) for h in range(8)]
     return lax.ppermute(x, ("seq", "head"), pairs)
 
 
@@ -497,17 +510,13 @@
             name=f"near_forward_{block}",
         )(queries, keys, values)
 
+    mid1 = exchange(mid0, 2)
     mate_far = to_odd(far0)
-    mid1 = exchange(mid0, 2)
-    far1 = joined(far0, mate_far)
-    from1 = odd_exchange(far1, 32)
-    near0 = near_forward(0)
-    mid_two, far2, near0 = after((joined(mid0, mid1), joined(far1, from1), near0))
+    near0, near1 = near_forward(0), near_forward(1)
+    mid_two, far1, near0, near1 = after(
+        (joined(mid0, mid1), joined(far0, mate_far), near0, near1)
+    )
     mid2 = exchange(mid_two, 1)
-    from2 = odd_exchange(far2, 16)
-    near1 = near_forward(1)
-    far4, near1 = after((joined(far2, from2), near1))
-    from4 = odd_exchange(far4, 8)
     mid_all = joined(mid_two, mid2)
     mid_o, mid_lse = pl.pallas_call(
         mid_forward_kernel,
@@ -519,8 +528,6 @@
         name="mid_forward",
     )(idx, mid_all)
 
-    far8, mid_o = after((joined(far4, from4), mid_o))
-    from8 = odd_exchange(far8, 4)
     att, lse12, bundle = pl.pallas_call(
         pre_kernel,
         out_shape=(sds((TOK, 256), BF), by_head_shape, sds((80, HD), F32)),
@@ -531,46 +538,61 @@
         cost_estimate=cost(10**7, 4 * 10**6, 10**5),
         name="pre",
     )(idx, *near0, *near1, mid_o, mid_lse, out_grad)
-    far16, bundle = after((joined(far8, from8), bundle))
-    from16 = odd_exchange(far16, 2)
-    mate_bundle = to_odd(bundle)
+    far1, bundle = after((far1, bundle))
+    mate_stats = to_even(bundle[48:])
+    from1 = chip_exchange(far1, 32, 1)
+    stats = joined(mate_stats, bundle[48:])
+    sums1 = head_exchange(stats, 2, 0)
+    far2, stats = after((joined(far1, from1), stats + sums1))
+    from2 = chip_exchange(far2, 16, 1)
+    sums2 = head_exchange(stats, 1, 0)
+    far4, stats = after((joined(far2, from2), stats + sums2))
+    from4 = chip_exchange(far4, 8, 1)
+    sums3 = head_exchange(stats, 4, 0)
+    far8 = joined(far4, from4)
+    from8 = chip_exchange(far8, 4, 1)
+    far16 = joined(far8, from8)
+    from16 = chip_exchange(far16, 2, 1)
+    stats = stats + sums3
+    mate = to_odd(joined(bundle[:48], stats))
     far_all = joined(far16, from16)
-
-    patch, stats = pl.pallas_call(
-        far_forward_kernel,
-        out_shape=(sds((64, HD), F32), sds((64, HD), F32)),
+    far_all, mate = after((far_all, mate))
+    far_even = to_even(far_all)
+
+    packs, fix = pl.pallas_call(
+        far_kernel,
+        out_shape=(sds((64, 256), BF), sds((8, HD), F32)),
         in_specs=[SMEM] + [VMEM] * 3,
         out_specs=(VMEM,) * 2,
+        scratch_shapes=[pltpu.VMEM((4, 64, HD), F32)],
         compiler_params=PARAMS,
         cost_estimate=cost(10**7, 10**6, 10**5),
-        name="far_forward",
-    )(idx, far_all, bundle, mate_bundle)
-
-    for bit in (2, 1, 4):
-        stats = stats + odd_head_exchange(stats, bit)
-
-    far_g = pl.pallas_call(
-        far_grad_kernel,
-        out_shape=sds((32, 256), BF),
-        in_specs=[SMEM] + [VMEM] * 4,
+        name="far",
+    )(idx, far_all, bundle, mate)
+
+    packs_even = to_even(packs)
+    fix1 = head_exchange(fix, 2, 1)
+    part0 = packs_even[:32]
+    part1 = chip_exchange(part0, 32, 0)
+    part_a, fix = after((joined(part0, part1), fix + fix1))
+    fix2 = head_exchange(fix, 1, 1)
+    part2 = chip_exchange(part_a, 16, 0)
+    far_dq = pl.pallas_call(
+        far_query_kernel,
+        out_shape=sds((32, HD), F32),
+        in_specs=[SMEM] + [VMEM] * 2,
         out_specs=VMEM,
-        scratch_shapes=[pltpu.VMEM((4, 64, HD), F32)],
-        compiler_params=PARAMS,
-        cost_estimate=cost(10**6, 10**5),
-        name="far_grad",
-    )(idx, stats, bundle, mate_bundle, patch)
-
-    part1 = odd_exchange(far_g, 32)
-    keep, reply = pl.pallas_call(
-        far_query_kernel,
-        out_shape=(sds((80, HD), F32), sds((80, HD), F32)),
-        in_specs=[SMEM] + [VMEM] * 4,
-        out_specs=(VMEM,) * 2,
         compiler_params=PARAMS,
         cost_estimate=cost(10**7, 10**6, 10**5),
         name="far_query",
-    )(idx, far_all, far_g, stats, patch)
-    reply = to_even(reply)
+    )(idx, far_even, packs_even)
+    part_b, fix, far_dq = after((joined(part_a, part2), fix + fix2, far_dq))
+    mate_dq = to_odd(far_dq)
+    fix3 = head_exchange(fix, 4, 1)
+    part3 = chip_exchange(part_b, 8, 0)
+    part_c, fix = after((joined(part_b, part3), fix + fix3))
+    part4 = chip_exchange(part_c, 4, 0)
+    fix_even = to_even(fix)
     normed, grad, delta, lse, mid_g = pl.pallas_call(
         norm_kernel,
         out_shape=(
@@ -580,13 +602,13 @@
             by_head_shape,
             sds((256, 256), BF),
         ),
-        in_specs=[SMEM] + [VMEM] * 5,
+        in_specs=[SMEM] + [VMEM] * 9,
         out_specs=(VMEM,) * 5,
-        scratch_shapes=[pltpu.VMEM((2, TOK, HD), F32), pltpu.VMEM((2, TOK, HD), F32)],
+        scratch_shapes=[pltpu.VMEM((2, TOK, HD), F32), pltpu.VMEM((32, HD), F32)],
         compiler_params=PARAMS,
         cost_estimate=cost(10**7, 4 * 10**6),
         name="norm",
-    )(idx, keep, reply, att, out_grad, lse12)
+    )(idx, mate, stats, fix, fix_even, packs, packs_even, att, out_grad, lse12)
 
     def near_backward(block):
         part = pl.BlockSpec((SEG, HD), lambda j: (block, j))
@@ -602,16 +624,26 @@
             name=f"near_backward_{block}",
         )(queries, keys, values, grad, lse, delta)
 
-    part_a, mid_g = after((joined(far_g, part1), mid_g))
-    part2 = odd_exchange(part_a, 16)
+    part_d, mid_g = after((joined(part_c, part4), mid_g))
     mid_g1 = exchange(mid_g, 2)
+    part5 = chip_exchange(part_d, 2, 0)
     dq0, dk0, dv0 = near_backward(0)
-    part_b, dq0 = after((joined(part_a, part2), dq0))
-    part3 = odd_exchange(part_b, 8)
     dq1, dk1, dv1 = near_backward(1)
-    part_c, mid_gs, dq1 = after((joined(part_b, part3), joined(mid_g, mid_g1), dq1))
-    part4 = odd_exchange(part_c, 4)
+    mid_gs, far_gs, dq0, dq1 = after(
+        (joined(mid_g, mid_g1), joined(part_d, part5), dq0, dq1)
+    )
     mid_g2 = exchange(mid_gs, 1)
+
+    far_kv = pl.pallas_call(
+        far_key_kernel,
+        out_shape=sds((64, HD), F32),
+        in_specs=[SMEM] + [VMEM] * 2,
+        out_specs=VMEM,
+        compiler_params=PARAMS,
+        cost_estimate=cost(10**7, 10**6, 10**5),
+        name="far_key",
+    )(idx, far_even, far_gs)
+    mate_kv = to_odd(far_kv)
 
     grad_queries = pl.pallas_call(
         query_grad_kernel,
@@ -622,10 +654,9 @@
         compiler_params=PARAMS,
         cost_estimate=cost(2 * 10**8, 3 * 10**6, 10**5),
         name="query_grad",
-    )(idx, dq0, dq1, mid_all, mid_g, keep, reply)
-
-    part_d, grad_queries = after((joined(part_c, part4), grad_queries))
-    part5 = odd_exchange(part_d, 2)
+    )(idx, dq0, dq1, mid_all, mid_g, mate_dq, far_dq)
+
+    mid_gall, grad_queries = after((joined(mid_gs, mid_g2), grad_queries))
     dk, dv = pl.pallas_call(
         mid_key_kernel,
         out_shape=(by_head_shape, by_head_shape),
@@ -634,18 +665,7 @@
         compiler_params=PARAMS,
         cost_estimate=cost(2 * 10**8, 4 * 10**6, 10**5),
         name="mid_key",
-    )(idx, dk0, dk1, dv0, dv1, mid_all, joined(mid_gs, mid_g2))
-    far_gs, dk = after((joined(part_d, part5), dk))
-
-    keep, reply = pl.pallas_call(
-        far_key_kernel,
-        out_shape=(sds((32, HD), F32), sds((32, HD), F32)),
-        in_specs=[SMEM] + [VMEM] * 2,
-        out_specs=(VMEM,) * 2,
-        compiler_params=PARAMS,
-        cost_estimate=cost(10**7, 10**6, 10**5),
-        name="far_key",
-    )(idx, far_all, far_gs)
+    )(idx, dk0, dk1, dv0, dv1, mid_all, mid_gall)
 
     grad_keys, grad_values, whole = pl.pallas_call(
         key_grad_kernel,
@@ -656,7 +676,7 @@
         compiler_params=PARAMS,
         cost_estimate=cost(10**6, 4 * 10**6),
         name="key_grad",
-    )(idx, dk, dv, keep, to_even(reply))
+    )(idx, dk, dv, mate_kv, far_kv)
 
     return normed, grad_queries, grad_keys, grad_values, whole
 

time: 127 us -> 124 us (0.976)
  starting transfers between devices: 72.7 us -> 63.1 us
  waiting for transfers between devices: 24.9 us -> 33.2 us
  Pallas kernels: 23.9 us -> 22.2 us
    ppermute x13 -> x16, starting transfers between devices: 57.6 us -> 34 us  [the longest x10 17 us: chip_exchange(): return lax.ppermute(x, 'seq', [(i, i ^ bit) for i in range(parity, 64, 2)])]
    ppermute x13 -> x16, waiting for transfers between devices: 19.8 us -> 27.6 us  [the longest x10 19.3 us: chip_exchange(): return lax.ppermute(x, 'seq', [(i, i ^ bit) for i in range(parity, 64, 2)])]
    ppermute x4, starting transfers between devices: 9.95 us -> 17.3 us  [exchange(): return lax.ppermute(x, 'seq', [(i, i ^ bit) for i in range(64)])]
    ppermute x2 -> x4, starting transfers between devices: 2.58 us -> 6.7 us  [to_even(): return lax.ppermute(x, 'seq', [(i + 1, i) for i in range(0, 64, 2)])]
    ppermute x2 -> x4, starting transfers between devices: 2.58 us -> 5.17 us  [to_odd(): return lax.ppermute(x, 'seq', [(i, i + 1) for i in range(0, 64, 2)])]
    ppermute x4, waiting for transfers between devices: 0.01 us -> 1.95 us  [exchange(): return lax.ppermute(x, 'seq', [(i, i ^ bit) for i in range(64)])]
    pallas_call x4 -> x3, Pallas kernels: 3.8 us -> 2.26 us  [the longest x1 1.16 us: local(): pl.pallas_call(far_kernel, out_shape=(sds((64, 256), BF), sds((8, HD), F3...]
    ppermute x2 -> x4, waiting for transfers between devices: 3.49 us -> 1.97 us  [to_odd(): return lax.ppermute(x, 'seq', [(i, i + 1) for i in range(0, 64, 2)])]
  transfers between devices with their start and end apart: 21 -> 28, of which waited for: 12 -> 13; matrix products, arithmetic and copies ran while one was open for 0% -> 0% of each run, Pallas kernels for 11% -> 13%
where the time goes in v3:
time: 124 us; the launch traced here: 123 us
  starting transfers between devices  63.1 us (51%)
  waiting for transfers between devices  33.2 us (27%)
  Pallas kernels  22.2 us (18%)
  local copies, waits for them, and re-layouts  3.26 us (3%)
    ppermute x10, waiting for transfers between devices, chip_exchange(): return lax.ppermute(x, 'seq', [(i, i ^ bit) for i in range(parity, 64, 2)])  19.3 us
    ppermute x4, starting transfers between devices, exchange(): return lax.ppermute(x, 'seq', [(i, i ^ bit) for i in range(64)])  17.3 us
    ppermute x10, starting transfers between devices, chip_exchange(): return lax.ppermute(x, 'seq', [(i, i ^ bit) for i in range(parity, 64, 2)])  17 us
    ppermute x6, starting transfers between devices, head_exchange(): return lax.ppermute(x, ('seq', 'head'), pairs)  16.9 us
    ppermute x6, waiting for transfers between devices, head_exchange(): return lax.ppermute(x, ('seq', 'head'), pairs)  8.32 us
    ppermute x4, starting transfers between devices, to_even(): return lax.ppermute(x, 'seq', [(i + 1, i) for i in range(0, 64, 2)])  6.7 us
    ppermute x4, starting transfers between devices, to_odd(): return lax.ppermute(x, 'seq', [(i, i + 1) for i in range(0, 64, 2)])  5.17 us
    pallas_call x2, Pallas kernels, near_backward(): pl.pallas_call(near_backward_kernel, grid=(2,), out_shape=(half_shape,) *...  4.26 us
  transfers between devices with their start and end apart: 28, of which 13 were waited for; matrix products, arithmetic and copies ran while one was open for 0% of the time, Pallas kernels for 13%

profile of v3, /device:TPU:1, one launch (start us, length us, event | category | flops | bytes accessed | tf_op | source)
XLA Modules:
  0.0 123.3 jit_solution(9002864758401890650)
XLA Ops:
  4.7 4.0 %collective-permute-start = (bf16[256,384]{1,0:T(8,128)(2,1)S(1)}, bf16[256,384]{1,0:T(8,128)(2,1)S(1)}, u32[]{:S(2)}, u32[]{:S(2)}) collective-permute-start(bf16[256,384]{1,0:T(8,128)(2,1)S(1)} %get-tuple-element.63), channel_id=1, source_target_pairs={{0,16},{8,24},{16,0},{24,8},{32,48},{40,56},{48,32},{56,40},{64,80... | collective-permute-start | bytes 589832 | tf_op jit(solution)/shard_map/ppermute | solution.py:446
  10.1 1.7 %near_forward_0.1 = (f32[2,512,128]{2,1,0:T(8,128)S(1)}, f32[2,512,128]{2,1,0:T(8,128)S(1)}) custom-call(bf16[1024,256]{1,0:T(8,128)(2,1)S(1)} %copy-done, bf16[1024,256]{1,0:T(8,128)(2,1)S(1)} %copy-done.2, bf16[1024,256]{1,0:T(8,128)(2,1)S(1)} %copy-done.4), custom_call_target="tpu_custom_call" | custom-call | flops 400000000 | bytes 2000000 | tf_op jit(solution)/shard_map/near_forward_0/pallas_call | solution.py:502
  11.8 1.7 %near_forward_1.1 = (f32[2,512,128]{2,1,0:T(8,128)S(1)}, f32[2,512,128]{2,1,0:T(8,128)S(1)}) custom-call(bf16[1024,256]{1,0:T(8,128)(2,1)S(1)} %copy-done, bf16[1024,256]{1,0:T(8,128)(2,1)S(1)} %copy-done.2, bf16[1024,256]{1,0:T(8,128)(2,1)S(1)} %copy-done.4), custom_call_target="tpu_custom_call" | custom-call | flops 400000000 | bytes 2000000 | tf_op jit(solution)/shard_map/near_forward_1/pallas_call | solution.py:502
  13.5 2.0 %collective-permute-done.1 = bf16[16,384]{1,0:T(8,128)(2,1)S(1)} collective-permute-done((bf16[16,384]{1,0:T(8,128)(2,1)S(1)}, bf16[16,384]{1,0:T(8,128)(2,1)S(1)}, u32[]{:S(2)}, u32[]{:S(2)}) %collective-permute-start.1) | collective-permute-done | bytes 12320 | tf_op jit(solution)/shard_map/ppermute | solution.py:459
  15.5 5.7 %collective-permute-start.2 = (bf16[512,384]{1,0:T(8,128)(2,1)S(1)}, bf16[512,384]{1,0:T(8,128)(2,1)S(1)}, u32[]{:S(2)}, u32[]{:S(2)}) collective-permute-start(bf16[512,384]{1,0:T(8,128)(2,1)S(1)} %pad_maximum_fusion.3), channel_id=1, source_target_pairs={{0,8},{8,0},{16,24},{24,16},{32,40},{40,32},{48,56},{56,48},{64,72... | collective-permute-start | bytes 1179656 | tf_op jit(solution)/shard_map/ppermute | solution.py:446
  23.9 1.8 %pre.1 = (bf16[1024,256]{1,0:T(8,128)(2,1)S(1)}, f32[2,1024,128]{2,1,0:T(8,128)S(1)}, f32[80,128]{1,0:T(8,128)S(1)}) custom-call(s32[2]{0:T(128)S(1)} %pad_add_fusion.idx, f32[2,512,128]{2,1,0:T(8,128)S(1)} %get-tuple-element.70.o0, f32[2,512,128]{2,1,0:T(8,128)S(1)} %get-tuple-element.71.lse0, f32[2,512,128]{2,1,0:T(8,128)S(1)} %get-tuple-element.72.o1, ...), custom_call_target="tpu_custom_call" | custom-call | flops 10000000 | bytes 4000000 | tf_op jit(solution)/shard_map/pre/pallas_call | solution.py:531
  25.7 2.3 %collective-permute-start.4 = (f32[32,128]{1,0:T(8,128)S(1)}, f32[32,128]{1,0:T(8,128)S(1)}, u32[]{:S(2)}, u32[]{:S(2)}) collective-permute-start(f32[32,128]{1,0:T(8,128)S(1)} %slice.10), channel_id=1, source_target_pairs={{8,0},{24,16},{40,32},{56,48},{72,64},{88,80},{104,96},{120,112},{... | collective-permute-start | bytes 49160 | tf_op jit(solution)/shard_map/ppermute | solution.py:463
  28.0 4.4 %collective-permute-start.3 = (bf16[32,384]{1,0:T(8,128)(2,1)S(1)}, bf16[32,384]{1,0:T(8,128)(2,1)S(1)}, u32[]{:S(2)}, u32[]{:S(2)}) collective-permute-start(bf16[32,384]{1,0:T(8,128)(2,1)S(1)} %pad_maximum_fusion.15), channel_id=1, source_target_pairs={{8,264},{24,280},{40,296},{56,312},{72,328},{88,344},{104,360},{12... | collective-permute-start | bytes 73736 | tf_op jit(solution)/shard_map/ppermute | solution.py:450
  33.1 3.5 %collective-permute-done.3 = bf16[32,384]{1,0:T(8,128)(2,1)S(1)} collective-permute-done((bf16[32,384]{1,0:T(8,128)(2,1)S(1)}, bf16[32,384]{1,0:T(8,128)(2,1)S(1)}, u32[]{:S(2)}, u32[]{:S(2)}) %collective-permute-start.3) | collective-permute-done | bytes 24608 | tf_op jit(solution)/shard_map/ppermute | solution.py:450
  36.6 1.9 %collective-permute-start.6 = (bf16[64,384]{1,0:T(8,128)(2,1)S(1)}, bf16[64,384]{1,0:T(8,128)(2,1)S(1)}, u32[]{:S(2)}, u32[]{:S(2)}) collective-permute-start(bf16[64,384]{1,0:T(8,128)(2,1)S(1)} %pad_maximum_fusion.12), channel_id=1, source_target_pairs={{8,136},{24,152},{40,168},{56,184},{72,200},{88,216},{104,232},{12... | collective-permute-start | bytes 147464 | tf_op jit(solution)/shard_map/ppermute | solution.py:450
  39.2 3.1 %collective-permute-done.6 = bf16[64,384]{1,0:T(8,128)(2,1)S(1)} collective-permute-done((bf16[64,384]{1,0:T(8,128)(2,1)S(1)}, bf16[64,384]{1,0:T(8,128)(2,1)S(1)}, u32[]{:S(2)}, u32[]{:S(2)}) %collective-permute-start.6) | collective-permute-done | bytes 49184 | tf_op jit(solution)/shard_map/ppermute | solution.py:450
  42.3 1.9 %collective-permute-start.8 = (bf16[128,384]{1,0:T(8,128)(2,1)S(1)}, bf16[128,384]{1,0:T(8,128)(2,1)S(1)}, u32[]{:S(2)}, u32[]{:S(2)}) collective-permute-start(bf16[128,384]{1,0:T(8,128)(2,1)S(1)} %pad_maximum_fusion.9), channel_id=1, source_target_pairs={{8,72},{24,88},{40,104},{56,120},{72,8},{88,24},{104,40},{120,56},... | collective-permute-start | bytes 294920 | tf_op jit(solution)/shard_map/ppermute | solution.py:450
  44.3 3.4 %collective-permute-done.8 = bf16[128,384]{1,0:T(8,128)(2,1)S(1)} collective-permute-done((bf16[128,384]{1,0:T(8,128)(2,1)S(1)}, bf16[128,384]{1,0:T(8,128)(2,1)S(1)}, u32[]{:S(2)}, u32[]{:S(2)}) %collective-permute-start.8) | collective-permute-done | bytes 98336 | tf_op jit(solution)/shard_map/ppermute | solution.py:450
  47.7 2.7 %collective-permute-start.9 = (bf16[256,384]{1,0:T(8,128)(2,1)S(1)}, bf16[256,384]{1,0:T(8,128)(2,1)S(1)}, u32[]{:S(2)}, u32[]{:S(2)}) collective-permute-start(bf16[256,384]{1,0:T(8,128)(2,1)S(1)} %pad_maximum_fusion.7), channel_id=1, source_target_pairs={{8,40},{24,56},{40,8},{56,24},{72,104},{88,120},{104,72},{120,88},... | collective-permute-start | bytes 589832 | tf_op jit(solution)/shard_map/ppermute | solution.py:450
  50.4 5.5 %collective-permute-done.9 = bf16[256,384]{1,0:T(8,128)(2,1)S(1)} collective-permute-done((bf16[256,384]{1,0:T(8,128)(2,1)S(1)}, bf16[256,384]{1,0:T(8,128)(2,1)S(1)}, u32[]{:S(2)}, u32[]{:S(2)}) %collective-permute-start.9) | collective-permute-done | bytes 196640 | tf_op jit(solution)/shard_map/ppermute | solution.py:450
  56.0 2.8 %collective-permute-start.10 = (bf16[512,384]{1,0:T(8,128)(2,1)S(1)}, bf16[512,384]{1,0:T(8,128)(2,1)S(1)}, u32[]{:S(2)}, u32[]{:S(2)}) collective-permute-start(bf16[512,384]{1,0:T(8,128)(2,1)S(1)} %pad_maximum_fusion.4), channel_id=1, source_target_pairs={{8,24},{24,8},{40,56},{56,40},{72,88},{88,72},{104,120},{120,104},... | collective-permute-start | bytes 1179656 | tf_op jit(solution)/shard_map/ppermute | solution.py:450
  60.8 3.7 %collective-permute-done.10 = bf16[512,384]{1,0:T(8,128)(2,1)S(1)} collective-permute-done((bf16[512,384]{1,0:T(8,128)(2,1)S(1)}, bf16[512,384]{1,0:T(8,128)(2,1)S(1)}, u32[]{:S(2)}, u32[]{:S(2)}) %collective-permute-start.10) | collective-permute-done | bytes 393248 | tf_op jit(solution)/shard_map/ppermute | solution.py:450
  69.9 2.2 %collective-permute-start.15 = (f32[8,128]{1,0:T(8,128)S(1)}, f32[8,128]{1,0:T(8,128)S(1)}, u32[]{:S(2)}, u32[]{:S(2)}) collective-permute-start(f32[8,128]{1,0:T(8,128)S(1)} %get-tuple-element.87), channel_id=1, source_target_pairs={{8,10},{9,11},{10,8},{11,9},{12,14},{13,15},{14,12},{15,13},{24,26... | collective-permute-start | bytes 12296 | tf_op jit(solution)/shard_map/ppermute | solution.py:455
  72.1 3.6 %collective-permute-done.15 = f32[8,128]{1,0:T(8,128)S(1)} collective-permute-done((f32[8,128]{1,0:T(8,128)S(1)}, f32[8,128]{1,0:T(8,128)S(1)}, u32[]{:S(2)}, u32[]{:S(2)}) %collective-permute-start.15) | collective-permute-done | bytes 4128 | tf_op jit(solution)/shard_map/ppermute | solution.py:455
  76.4 1.9 %collective-permute-start.17 = (f32[8,128]{1,0:T(8,128)S(1)}, f32[8,128]{1,0:T(8,128)S(1)}, u32[]{:S(2)}, u32[]{:S(2)}) collective-permute-start(f32[8,128]{1,0:T(8,128)S(1)} %add.21), channel_id=1, source_target_pairs={{8,9},{9,8},{10,11},{11,10},{12,13},{13,12},{14,15},{15,14},{24,25... | collective-permute-start | bytes 12296 | tf_op jit(solution)/shard_map/ppermute | solution.py:455
  78.4 2.4 %collective-permute-done.17 = f32[8,128]{1,0:T(8,128)S(1)} collective-permute-done((f32[8,128]{1,0:T(8,128)S(1)}, f32[8,128]{1,0:T(8,128)S(1)}, u32[]{:S(2)}, u32[]{:S(2)}) %collective-permute-start.17) | collective-permute-done | bytes 4128 | tf_op jit(solution)/shard_map/ppermute | solution.py:455
  82.1 10.8 %collective-permute-start.20 = (f32[8,128]{1,0:T(8,128)S(1)}, f32[8,128]{1,0:T(8,128)S(1)}, u32[]{:S(2)}, u32[]{:S(2)}) collective-permute-start(f32[8,128]{1,0:T(8,128)S(1)} %add.22), channel_id=1, source_target_pairs={{8,12},{9,13},{10,14},{11,15},{12,8},{13,9},{14,10},{15,11},{24,28... | collective-permute-start | bytes 12296 | tf_op jit(solution)/shard_map/ppermute | solution.py:455
  92.8 2.3 %collective-permute-done.20 = f32[8,128]{1,0:T(8,128)S(1)} collective-permute-done((f32[8,128]{1,0:T(8,128)S(1)}, f32[8,128]{1,0:T(8,128)S(1)}, u32[]{:S(2)}, u32[]{:S(2)}) %collective-permute-start.20) | collective-permute-done | bytes 4128 | tf_op jit(solution)/shard_map/ppermute | solution.py:455
  95.8 1.8 %collective-permute-start.21 = (f32[8,128]{1,0:T(8,128)S(1)}, f32[8,128]{1,0:T(8,128)S(1)}, u32[]{:S(2)}, u32[]{:S(2)}) collective-permute-start(f32[8,128]{1,0:T(8,128)S(1)} %add.23.fix_own), channel_id=1, source_target_pairs={{8,0},{24,16},{40,32},{56,48},{72,64},{88,80},{104,96},{120,112},{... | collective-permute-start | bytes 12296 | tf_op jit(solution)/shard_map/ppermute | solution.py:463
  98.4 3.0 %norm.1 = (bf16[1024,256]{1,0:T(8,128)(2,1)}, bf16[1024,256]{1,0:T(8,128)(2,1)S(1)}, f32[2,1024,128]{2,1,0:T(8,128)S(1)}, f32[2,1024,128]{2,1,0:T(8,128)S(1)}, bf16[256,256]{1,0:T(8,128)(2,1)S(1)}) custom-call(s32[2]{0:T(128)S(1)} %pad_add_fusion.idx, f32[112,128]{1,0:T(8,128)S(1)} %collective-permute-done.12.mate_ref, f32[64,128]{1,0:T(8,128)S(1)} %add.20.stat_ref, ...), custom_call_target="tpu_custom_call" | custom-call | flops 10000000 | bytes 4000000 | tf_op jit(solution)/shard_map/norm/pallas_call | solution.py:596
  102.2 2.3 %collective-permute-start.23 = (bf16[256,256]{1,0:T(8,128)(2,1)S(1)}, bf16[256,256]{1,0:T(8,128)(2,1)S(1)}, u32[]{:S(2)}, u32[]{:S(2)}) collective-permute-start(bf16[256,256]{1,0:T(8,128)(2,1)S(1)} %get-tuple-element.98.mid_g), channel_id=1, source_target_pairs={{0,16},{8,24},{16,0},{24,8},{32,48},{40,56},{48,32},{56,40},{64,80... | collective-permute-start | bytes 393224 | tf_op jit(solution)/shard_map/ppermute | solution.py:446
  104.5 2.1 %near_backward_1.1 = (f32[2,512,128]{2,1,0:T(8,128)S(1)}, f32[2,512,128]{2,1,0:T(8,128)S(1)}, f32[2,512,128]{2,1,0:T(8,128)S(1)}) custom-call(bf16[1024,256]{1,0:T(8,128)(2,1)S(1)} %copy-done.1, bf16[1024,256]{1,0:T(8,128)(2,1)S(1)} %copy-done.3, bf16[1024,256]{1,0:T(8,128)(2,1)S(1)} %copy-done.5, bf16[1024,256]{1,0:T(8,128)(2,1)S(1)} %get-tuple-element.100.g_ref, ...), custom_call_target="tpu_custom_call" | custom-call | flops 1000000000 | bytes 4000000 | tf_op jit(solution)/shard_map/near_backward_1/pallas_call | solution.py:616
  106.7 2.1 %near_backward_0.1 = (f32[2,512,128]{2,1,0:T(8,128)S(1)}, f32[2,512,128]{2,1,0:T(8,128)S(1)}, f32[2,512,128]{2,1,0:T(8,128)S(1)}) custom-call(bf16[1024,256]{1,0:T(8,128)(2,1)S(1)} %copy-done.1, bf16[1024,256]{1,0:T(8,128)(2,1)S(1)} %copy-done.3, bf16[1024,256]{1,0:T(8,128)(2,1)S(1)} %copy-done.5, bf16[1024,256]{1,0:T(8,128)(2,1)S(1)} %get-tuple-element.100.g_ref, ...), custom_call_target="tpu_custom_call" | custom-call | flops 1000000000 | bytes 4000000 | tf_op jit(solution)/shard_map/near_backward_0/pallas_call | solution.py:616
  109.5 5.2 %collective-permute-start.25 = (bf16[512,256]{1,0:T(8,128)(2,1)S(1)}, bf16[512,256]{1,0:T(8,128)(2,1)S(1)}, u32[]{:S(2)}, u32[]{:S(2)}) collective-permute-start(bf16[512,256]{1,0:T(8,128)(2,1)S(1)} %pad_maximum_fusion.6), channel_id=1, source_target_pairs={{0,8},{8,0},{16,24},{24,16},{32,40},{40,32},{48,56},{56,48},{64,72... | collective-permute-start | bytes 786440 | tf_op jit(solution)/shard_map/ppermute | solution.py:446
  118.0 2.1 %query_grad.1 = bf16[1024,256]{1,0:T(8,128)(2,1)} custom-call(s32[2]{0:T(128)S(1)} %pad_add_fusion.idx, f32[2,512,128]{2,1,0:T(8,128)S(1)} %get-tuple-element.106.dq0, f32[2,512,128]{2,1,0:T(8,128)S(1)} %get-tuple-element.107.dq1, bf16[1024,384]{1,0:T(8,128)(2,1)S(1)} %constant_dynamic-update-slice_fusion.mid_ref, ...), custom_call_target="tpu_custom_call" | custom-call | flops 200000000 | bytes 3000000 | tf_op jit(solution)/shard_map/query_grad/pallas_call | solution.py:648
  120.1 1.4 %mid_key.1 = (f32[2,1024,128]{2,1,0:T(8,128)S(1)}, f32[2,1024,128]{2,1,0:T(8,128)S(1)}) custom-call(s32[2]{0:T(128)S(1)} %pad_add_fusion.idx, f32[2,512,128]{2,1,0:T(8,128)S(1)} %get-tuple-element.110.dk0, f32[2,512,128]{2,1,0:T(8,128)S(1)} %get-tuple-element.111.dk1, f32[2,512,128]{2,1,0:T(8,128)S(1)} %get-tuple-element.112.dv0, ...), custom_call_target="tpu_custom_call" | custom-call | flops 200000000 | bytes 4000000 | tf_op jit(solution)/shard_map/mid_key/pallas_call | solution.py:660
  121.5 1.8 %key_grad.1 = (bf16[1024,256]{1,0:T(8,128)(2,1)}, bf16[1024,256]{1,0:T(8,128)(2,1)}, f32[2,8,256]{2,1,0:T(8,128)}) custom-call(s32[2]{0:T(128)S(1)} %pad_add_fusion.idx, f32[2,1024,128]{2,1,0:T(8,128)S(1)} %get-tuple-element.115.dk_in, f32[2,1024,128]{2,1,0:T(8,128)S(1)} %get-tuple-element.116.dv_in, f32[64,128]{1,0:T(8,128)S(1)} %collective-permute-done.27.far_got, ...), custom_call_target="tpu_custom_call" | custom-call | flops 1000000 | bytes 4000000 | tf_op jit(solution)/shard_map/key_grad/pallas_call | solution.py:670
  (80 shorter events, 24.8 us)
Async XLA Ops:
  4.7 10.8 %collective-permute-start = (bf16[256,384]{1,0:T(8,128)(2,1)S(1)}, bf16[256,384]{1,0:T(8,128)(2,1)S(1)}, u32[]{:S(2)}, u32[]{:S(2)}) collective-permute-start(bf16[256,384]{1,0:T(8,128)(2,1)S(1)} %get-tuple-element.63), channel_id=1, source_target_pairs={{0,16},{8,24},{16,0},{24,8},{32,48},{40,56},{48,32},{56,40},{64,80... | collective-permute-start | bytes 589832 | tf_op jit(solution)/shard_map/ppermute | solution.py:446
  8.8 6.7 %collective-permute-start.1 = (bf16[16,384]{1,0:T(8,128)(2,1)S(1)}, bf16[16,384]{1,0:T(8,128)(2,1)S(1)}, u32[]{:S(2)}, u32[]{:S(2)}) collective-permute-start(bf16[16,384]{1,0:T(8,128)(2,1)S(1)} %get-tuple-element.64), channel_id=1, source_target_pairs={{0,8},{16,24},{32,40},{48,56},{64,72},{80,88},{96,104},{112,120},{... | collective-permute-start | bytes 36872 | tf_op jit(solution)/shard_map/ppermute | solution.py:459
  15.5 8.4 %copy-start.6 = (bf16[1024,256]{1,0:T(8,128)(2,1)S(1)}, bf16[1024,256]{1,0:T(8,128)(2,1)}, u32[]{:S(2)}) copy-start(bf16[1024,256]{1,0:T(8,128)(2,1)} %g_ref.3) | copy-start | bytes 1572868
  15.5 7.1 %collective-permute-start.2 = (bf16[512,384]{1,0:T(8,128)(2,1)S(1)}, bf16[512,384]{1,0:T(8,128)(2,1)S(1)}, u32[]{:S(2)}, u32[]{:S(2)}) collective-permute-start(bf16[512,384]{1,0:T(8,128)(2,1)S(1)} %pad_maximum_fusion.3), channel_id=1, source_target_pairs={{0,8},{8,0},{16,24},{24,16},{32,40},{40,32},{48,56},{56,48},{64,72... | collective-permute-start | bytes 1179656 | tf_op jit(solution)/shard_map/ppermute | solution.py:446
  25.7 6.7 %collective-permute-start.4 = (f32[32,128]{1,0:T(8,128)S(1)}, f32[32,128]{1,0:T(8,128)S(1)}, u32[]{:S(2)}, u32[]{:S(2)}) collective-permute-start(f32[32,128]{1,0:T(8,128)S(1)} %slice.10), channel_id=1, source_target_pairs={{8,0},{24,16},{40,32},{56,48},{72,64},{88,80},{104,96},{120,112},{... | collective-permute-start | bytes 49160 | tf_op jit(solution)/shard_map/ppermute | solution.py:463
  28.0 8.6 %collective-permute-start.3 = (bf16[32,384]{1,0:T(8,128)(2,1)S(1)}, bf16[32,384]{1,0:T(8,128)(2,1)S(1)}, u32[]{:S(2)}, u32[]{:S(2)}) collective-permute-start(bf16[32,384]{1,0:T(8,128)(2,1)S(1)} %pad_maximum_fusion.15), channel_id=1, source_target_pairs={{8,264},{24,280},{40,296},{56,312},{72,328},{88,344},{104,360},{12... | collective-permute-start | bytes 73736 | tf_op jit(solution)/shard_map/ppermute | solution.py:450
  32.4 4.2 %collective-permute-start.5 = (f32[64,128]{1,0:T(8,128)S(1)}, f32[64,128]{1,0:T(8,128)S(1)}, u32[]{:S(2)}, u32[]{:S(2)}) collective-permute-start(f32[64,128]{1,0:T(8,128)S(1)} %pad_maximum_fusion.13), channel_id=1, source_target_pairs={{0,2},{1,3},{2,0},{3,1},{4,6},{5,7},{6,4},{7,5},{16,18},{17,19},{1... | collective-permute-start | bytes 98312 | tf_op jit(solution)/shard_map/ppermute | solution.py:455
  36.6 5.7 %collective-permute-start.6 = (bf16[64,384]{1,0:T(8,128)(2,1)S(1)}, bf16[64,384]{1,0:T(8,128)(2,1)S(1)}, u32[]{:S(2)}, u32[]{:S(2)}) collective-permute-start(bf16[64,384]{1,0:T(8,128)(2,1)S(1)} %pad_maximum_fusion.12), channel_id=1, source_target_pairs={{8,136},{24,152},{40,168},{56,184},{72,200},{88,216},{104,232},{12... | collective-permute-start | bytes 147464 | tf_op jit(solution)/shard_map/ppermute | solution.py:450
  38.5 0.7 collective-permute-start.7
  42.3 5.4 %collective-permute-start.8 = (bf16[128,384]{1,0:T(8,128)(2,1)S(1)}, bf16[128,384]{1,0:T(8,128)(2,1)S(1)}, u32[]{:S(2)}, u32[]{:S(2)}) collective-permute-start(bf16[128,384]{1,0:T(8,128)(2,1)S(1)} %pad_maximum_fusion.9), channel_id=1, source_target_pairs={{8,72},{24,88},{40,104},{56,120},{72,8},{88,24},{104,40},{120,56},... | collective-permute-start | bytes 294920 | tf_op jit(solution)/shard_map/ppermute | solution.py:450
  47.7 8.2 %collective-permute-start.9 = (bf16[256,384]{1,0:T(8,128)(2,1)S(1)}, bf16[256,384]{1,0:T(8,128)(2,1)S(1)}, u32[]{:S(2)}, u32[]{:S(2)}) collective-permute-start(bf16[256,384]{1,0:T(8,128)(2,1)S(1)} %pad_maximum_fusion.7), channel_id=1, source_target_pairs={{8,40},{24,56},{40,8},{56,24},{72,104},{88,120},{104,72},{120,88},... | collective-permute-start | bytes 589832 | tf_op jit(solution)/shard_map/ppermute | solution.py:450
  56.0 8.5 %collective-permute-start.10 = (bf16[512,384]{1,0:T(8,128)(2,1)S(1)}, bf16[512,384]{1,0:T(8,128)(2,1)S(1)}, u32[]{:S(2)}, u32[]{:S(2)}) collective-permute-start(bf16[512,384]{1,0:T(8,128)(2,1)S(1)} %pad_maximum_fusion.4), channel_id=1, source_target_pairs={{8,24},{24,8},{40,56},{56,40},{72,88},{88,72},{104,120},{120,104},... | collective-permute-start | bytes 1179656 | tf_op jit(solution)/shard_map/ppermute | solution.py:450
  58.7 0.7 collective-permute-start.11
  59.5 5.1 %collective-permute-start.12 = (f32[112,128]{1,0:T(8,128)S(1)}, f32[112,128]{1,0:T(8,128)S(1)}, u32[]{:S(2)}, u32[]{:S(2)}) collective-permute-start(f32[112,128]{1,0:T(8,128)S(1)} %pad_maximum_fusion.11), channel_id=1, source_target_pairs={{0,8},{16,24},{32,40},{48,56},{64,72},{80,88},{96,104},{112,120},{... | collective-permute-start | bytes 172040 | tf_op jit(solution)/shard_map/ppermute | solution.py:459
  64.6 16.2 %collective-permute-start.18 = (bf16[1024,384]{1,0:T(8,128)(2,1)S(1)}, bf16[1024,384]{1,0:T(8,128)(2,1)S(1)}, u32[]{:S(2)}, u32[]{:S(2)}) collective-permute-start(bf16[1024,384]{1,0:T(8,128)(2,1)S(1)} %pad_maximum_fusion.far_all), channel_id=1, source_target_pairs={{8,0},{24,16},{40,32},{56,48},{72,64},{88,80},{104,96},{120,112},{... | collective-permute-start | bytes 2359304 | tf_op jit(solution)/shard_map/ppermute | solution.py:463
  67.1 2.1 %collective-permute-start.13 = (bf16[64,256]{1,0:T(8,128)(2,1)S(1)}, bf16[64,256]{1,0:T(8,128)(2,1)S(1)}, u32[]{:S(2)}, u32[]{:S(2)}) collective-permute-start(bf16[64,256]{1,0:T(8,128)(2,1)S(1)} %get-tuple-element.86.packs_own), channel_id=1, source_target_pairs={{8,0},{24,16},{40,32},{56,48},{72,64},{88,80},{104,96},{120,112},{... | collective-permute-start | bytes 98312 | tf_op jit(solution)/shard_map/ppermute | solution.py:463
  69.2 6.5 %collective-permute-start.14 = (bf16[32,256]{1,0:T(8,128)(2,1)S(1)}, bf16[32,256]{1,0:T(8,128)(2,1)S(1)}, u32[]{:S(2)}, u32[]{:S(2)}) collective-permute-start(bf16[32,256]{1,0:T(8,128)(2,1)S(1)} %slice.13), channel_id=1, source_target_pairs={{0,256},{16,272},{32,288},{48,304},{64,320},{80,336},{96,352},{112... | collective-permute-start | bytes 49160 | tf_op jit(solution)/shard_map/ppermute | solution.py:450
  69.9 5.9 %collective-permute-start.15 = (f32[8,128]{1,0:T(8,128)S(1)}, f32[8,128]{1,0:T(8,128)S(1)}, u32[]{:S(2)}, u32[]{:S(2)}) collective-permute-start(f32[8,128]{1,0:T(8,128)S(1)} %get-tuple-element.87), channel_id=1, source_target_pairs={{8,10},{9,11},{10,8},{11,9},{12,14},{13,15},{14,12},{15,13},{24,26... | collective-permute-start | bytes 12296 | tf_op jit(solution)/shard_map/ppermute | solution.py:455
  75.8 5.0 %collective-permute-start.16 = (bf16[64,256]{1,0:T(8,128)(2,1)S(1)}, bf16[64,256]{1,0:T(8,128)(2,1)S(1)}, u32[]{:S(2)}, u32[]{:S(2)}) collective-permute-start(bf16[64,256]{1,0:T(8,128)(2,1)S(1)} %pad_maximum_fusion.14), channel_id=1, source_target_pairs={{0,128},{16,144},{32,160},{48,176},{64,192},{80,208},{96,224},{112... | collective-permute-start | bytes 98312 | tf_op jit(solution)/shard_map/ppermute | solution.py:450
  76.4 4.4 %collective-permute-start.17 = (f32[8,128]{1,0:T(8,128)S(1)}, f32[8,128]{1,0:T(8,128)S(1)}, u32[]{:S(2)}, u32[]{:S(2)}) collective-permute-start(f32[8,128]{1,0:T(8,128)S(1)} %add.21), channel_id=1, source_target_pairs={{8,9},{9,8},{10,11},{11,10},{12,13},{13,12},{14,15},{15,14},{24,25... | collective-permute-start | bytes 12296 | tf_op jit(solution)/shard_map/ppermute | solution.py:455
  81.4 13.7 %collective-permute-start.19 = (bf16[128,256]{1,0:T(8,128)(2,1)S(1)}, bf16[128,256]{1,0:T(8,128)(2,1)S(1)}, u32[]{:S(2)}, u32[]{:S(2)}) collective-permute-start(bf16[128,256]{1,0:T(8,128)(2,1)S(1)} %pad_maximum_fusion.10), channel_id=1, source_target_pairs={{0,64},{16,80},{32,96},{48,112},{64,0},{80,16},{96,32},{112,48},{1... | collective-permute-start | bytes 196616 | tf_op jit(solution)/shard_map/ppermute | solution.py:450
  82.1 13.1 %collective-permute-start.20 = (f32[8,128]{1,0:T(8,128)S(1)}, f32[8,128]{1,0:T(8,128)S(1)}, u32[]{:S(2)}, u32[]{:S(2)}) collective-permute-start(f32[8,128]{1,0:T(8,128)S(1)} %add.22), channel_id=1, source_target_pairs={{8,12},{9,13},{10,14},{11,15},{12,8},{13,9},{14,10},{15,11},{24,28... | collective-permute-start | bytes 12296 | tf_op jit(solution)/shard_map/ppermute | solution.py:455
  95.1 6.3 %collective-permute-start.22 = (bf16[256,256]{1,0:T(8,128)(2,1)S(1)}, bf16[256,256]{1,0:T(8,128)(2,1)S(1)}, u32[]{:S(2)}, u32[]{:S(2)}) collective-permute-start(bf16[256,256]{1,0:T(8,128)(2,1)S(1)} %pad_maximum_fusion.8), channel_id=1, source_target_pairs={{0,32},{16,48},{32,0},{48,16},{64,96},{80,112},{96,64},{112,80},{1... | collective-permute-start | bytes 393224 | tf_op jit(solution)/shard_map/ppermute | solution.py:450
  95.8 2.6 %collective-permute-start.21 = (f32[8,128]{1,0:T(8,128)S(1)}, f32[8,128]{1,0:T(8,128)S(1)}, u32[]{:S(2)}, u32[]{:S(2)}) collective-permute-start(f32[8,128]{1,0:T(8,128)S(1)} %add.23.fix_own), channel_id=1, source_target_pairs={{8,0},{24,16},{40,32},{56,48},{72,64},{88,80},{104,96},{120,112},{... | collective-permute-start | bytes 12296 | tf_op jit(solution)/shard_map/ppermute | solution.py:463
  98.4 6.1 %copy-start.1 = (bf16[1024,256]{1,0:T(8,128)(2,1)S(1)}, bf16[1024,256]{1,0:T(8,128)(2,1)}, u32[]{:S(2)}) copy-start(bf16[1024,256]{1,0:T(8,128)(2,1)} %q_ref.9) | copy-start | bytes 1572868
  98.4 6.1 %copy-start.3 = (bf16[1024,256]{1,0:T(8,128)(2,1)S(1)}, bf16[1024,256]{1,0:T(8,128)(2,1)}, u32[]{:S(2)}) copy-start(bf16[1024,256]{1,0:T(8,128)(2,1)} %k_ref.9) | copy-start | bytes 1572868
  98.4 6.1 %copy-start.5 = (bf16[1024,256]{1,0:T(8,128)(2,1)S(1)}, bf16[1024,256]{1,0:T(8,128)(2,1)}, u32[]{:S(2)}) copy-start(bf16[1024,256]{1,0:T(8,128)(2,1)} %v_ref.9) | copy-start | bytes 1572868
  101.5 8.0 %collective-permute-start.24 = (bf16[512,256]{1,0:T(8,128)(2,1)S(1)}, bf16[512,256]{1,0:T(8,128)(2,1)S(1)}, u32[]{:S(2)}, u32[]{:S(2)}) collective-permute-start(bf16[512,256]{1,0:T(8,128)(2,1)S(1)} %pad_maximum_fusion.5), channel_id=1, source_target_pairs={{0,16},{16,0},{32,48},{48,32},{64,80},{80,64},{96,112},{112,96},{1... | collective-permute-start | bytes 786440 | tf_op jit(solution)/shard_map/ppermute | solution.py:450
  102.2 7.3 %collective-permute-start.23 = (bf16[256,256]{1,0:T(8,128)(2,1)S(1)}, bf16[256,256]{1,0:T(8,128)(2,1)S(1)}, u32[]{:S(2)}, u32[]{:S(2)}) collective-permute-start(bf16[256,256]{1,0:T(8,128)(2,1)S(1)} %get-tuple-element.98.mid_g), channel_id=1, source_target_pairs={{0,16},{8,24},{16,0},{24,8},{32,48},{40,56},{48,32},{56,40},{64,80... | collective-permute-start | bytes 393224 | tf_op jit(solution)/shard_map/ppermute | solution.py:446
  109.5 10.5 %collective-permute-start.25 = (bf16[512,256]{1,0:T(8,128)(2,1)S(1)}, bf16[512,256]{1,0:T(8,128)(2,1)S(1)}, u32[]{:S(2)}, u32[]{:S(2)}) collective-permute-start(bf16[512,256]{1,0:T(8,128)(2,1)S(1)} %pad_maximum_fusion.6), channel_id=1, source_target_pairs={{0,8},{8,0},{16,24},{24,16},{32,40},{40,32},{48,56},{56,48},{64,72... | collective-permute-start | bytes 786440 | tf_op jit(solution)/shard_map/ppermute | solution.py:446
  114.8 3.2 %collective-permute-start.26 = (f32[32,128]{1,0:T(8,128)S(1)}, f32[32,128]{1,0:T(8,128)S(1)}, u32[]{:S(2)}, u32[]{:S(2)}) collective-permute-start(f32[32,128]{1,0:T(8,128)S(1)} %far_query.1.dq_own), channel_id=1, source_target_pairs={{0,8},{16,24},{32,40},{48,56},{64,72},{80,88},{96,104},{112,120},{... | collective-permute-start | bytes 49160 | tf_op jit(solution)/shard_map/ppermute | solution.py:459
  116.6 4.9 %collective-permute-start.27 = (f32[64,128]{1,0:T(8,128)S(1)}, f32[64,128]{1,0:T(8,128)S(1)}, u32[]{:S(2)}, u32[]{:S(2)}) collective-permute-start(f32[64,128]{1,0:T(8,128)S(1)} %far_key.1.far_own), channel_id=1, source_target_pairs={{0,8},{16,24},{32,40},{48,56},{64,72},{80,88},{96,104},{112,120},{... | collective-permute-start | bytes 98312 | tf_op jit(solution)/shard_map/ppermute | solution.py:459
  (3 other events, 3.1 us)

commit v4 on v3

--- a/solution.py
+++ b/solution.py
@@ -154,6 +154,7 @@
         far_ref[16 + j * 8 : 24 + j * 8, :] = sl[distant, :]
     lane = iota((128, HD), 1)
     row = iota((128, HD), 0)
+    table = jnp.zeros((128, HD), F32)
     for b in range(8):
         rows = slice(b * 128, (b + 1) * 128)
         at, g = [], []
@@ -169,10 +170,9 @@
             g[0] * at[0] + g[1] * at[1],
             g[0] + g[1],
         )
-        block = jnp.zeros((128, HD), F32)
         for i, term in enumerate(sums):
-            block = jnp.where(lane == i, jnp.sum(term, axis=1, keepdims=True), block)
-        far_ref[48 + b * 4 : 52 + b * 4, :] = block.T[:4, :]
+            table = jnp.where(lane == b * 4 + i, jnp.sum(term, axis=1, keepdims=True), table)
+    far_ref[48:, :] = table.T[:32, :]
     for j in range(2):
         distant = pl.ds(idx[1] * 2 + j, 8, stride=128)
         far_ref[32 + j * 8 : 40 + j * 8, :] = out_scr.at[j][distant, :]
@@ -191,8 +191,8 @@
     return pack
 
 
-def far_kernel(idx, far_all, own_ref, mate_ref, packs_ref, fix_ref, col_scr):
-    q = far_all[:32, 2 * HD :]
+def far_kernel(idx, far_all, rows_ref, own_ref, mate_ref, packs_ref, fix_ref, col_scr):
+    q = rows_ref[:, 2 * HD :]
     s = jnp.where(far_keep_forward(idx[0]), dot_nt(q, far_all[:, :HD]) * SCALE, NEG)
     top = jnp.max(s, axis=1, keepdims=True)
     p = jnp.exp(s - top)
@@ -236,9 +236,11 @@
     delta = jnp.sum(grad.astype(F32) * at, axis=1, keepdims=True)
     packs_ref[:32, :HD] = grad
     delta = jnp.broadcast_to(delta, (32, HD))
-    packs_ref[:32, HD:] = stat_pack(lse, delta, lane).astype(BF)
+    packs_ref[:32, HD : 2 * HD] = stat_pack(lse, delta, lane).astype(BF)
+    packs_ref[:32, 2 * HD :] = q
     packs_ref[32:, :HD] = at16
-    packs_ref[32:, HD:] = at16
+    packs_ref[32:, HD : 2 * HD] = at16
+    packs_ref[32:, 2 * HD :] = at16
 
 
 def stat_cols(pack):
@@ -252,9 +254,9 @@
     @pl.when((idx[0] & 1) == 0)
     def _():
         k_all, v_all = far_all[:, :HD], far_all[:, HD : 2 * HD]
-        lse, delta = stat_cols(packs[:32, HD:])
+        lse, delta = stat_cols(packs[:32, HD : 2 * HD])
         keep = far_keep_forward(idx[0])
-        s = jnp.where(keep, dot_nt(far_all[:32, 2 * HD :], k_all) * SCALE, NEG)
+        s = jnp.where(keep, dot_nt(packs[:32, 2 * HD :], k_all) * SCALE, NEG)
         p = jnp.exp(s - lse)
         ds = (p * (dot_nt(packs[:32, :HD], v_all) - delta)).astype(BF)
         dq_ref[...] = dot_nn(ds, k_all) * SCALE
@@ -285,7 +287,9 @@
         idx, packs_own[32:48, :HD].astype(F32), packs_got[48:, :HD].astype(F32)
     )
     far_stat = by_parity(
-        idx, packs_own[:16, HD:].astype(F32), packs_got[16:32, HD:].astype(F32)
+        idx,
+        packs_own[:16, HD : 2 * HD].astype(F32),
+        packs_got[16:32, HD : 2 * HD].astype(F32),
     )
     far_lse = jnp.broadcast_to(stat_cols(far_stat)[0], (16, HD))
     for j in range(2):
@@ -350,9 +354,9 @@
             dq_ref[0, rows, :] += dq
 
 
-def query_grad_kernel(idx, dq0, dq1, mid_ref, mid_g, dq_got, dq_own, out_ref, scr, far_scr):
+def query_grad_kernel(idx, dq0, dq1, mid_ref, mid_g, far_got, far_own, out_ref, scr, far_scr):
     s_idx = idx[0]
-    far_dq = by_parity(idx, dq_got[:16], dq_own[16:])
+    far_dq = by_parity(idx, far_got[64:80], far_own[80:])
     key_slot = mid_slots(s_idx, (128, SEG), 1)
     query_slot = (s_idx & 3) * 128 + iota((128, SEG), 0)
     keep = key_slot <= query_slot
@@ -389,17 +393,18 @@
     return stats[0:1], stats[1:2]
 
 
-def far_key_kernel(idx, far_all, grads, out_ref):
+def far_key_kernel(idx, far_all, grads, dq_ref, out_ref):
     @pl.when((idx[0] & 1) == 0)
     def _():
-        lse, delta = stat_rows(grads[:, HD:])
+        lse, delta = stat_rows(grads[:, HD : 2 * HD])
         k, v = far_all[:32, :HD], far_all[:32, HD : 2 * HD]
-        q_all, g_all = far_all[:, 2 * HD :], grads[:, :HD]
+        q_all, g_all = grads[:, 2 * HD :], grads[:, :HD]
         s = jnp.where(far_keep_backward(idx[0]), dot_nt(k, q_all) * SCALE, NEG)
         p = jnp.exp(s - lse)
         ds = (p * (dot_nt(v, g_all) - delta)).astype(BF)
         out_ref[:32, :] = dot_nn(ds, q_all) * SCALE
-        out_ref[32:, :] = dot_nn(p.astype(BF), g_all)
+        out_ref[32:64, :] = dot_nn(p.astype(BF), g_all)
+        out_ref[64:, :] = dq_ref[...]
 
 
 def mid_key_kernel(idx, dk0, dk1, dv0, dv1, mid_ref, grads, dk_ref, dv_ref):
@@ -429,17 +434,19 @@
             out[picked, :] = out[picked, :] + mid
 
 
-def key_grad_kernel(idx, dk_in, dv_in, far_got, far_own, dk_out, dv_out, whole_ref, scr):
-    for j in range(2):
-        distant = pl.ds(idx[1] * 2 + j, 8, stride=128)
+def key_grad_kernel(idx, dk_in, dv_in, far_got, far_own, dk_out, dv_out, whole_ref):
+    row = iota((128, HD), 0)
+    for j in range(2):
+        here = row == idx[1] * 2 + j
+        cols = slice(j * HD, (j + 1) * HD)
         for a, (near, out) in enumerate(((dk_in, dk_out), (dv_in, dv_out))):
-            row = a * 32 + j * 8
-            far = by_parity(idx, far_got[row : row + 8], far_own[row + 16 : row + 24])
-            whole_ref[a, :, j * HD : (j + 1) * HD] = far
-            sc = scr.at[j * 2 + a]
-            sc[...] = near[j]
-            sc[distant, :] = sc[distant, :] + far
-            out[:, j * HD : (j + 1) * HD] = sc[...].astype(BF)
+            first = a * 32 + j * 8
+            far = by_parity(idx, far_got[first : first + 8], far_own[first + 16 : first + 24])
+            whole_ref[a, :, cols] = far
+            for b in range(8):
+                rows = slice(b * 128, (b + 1) * 128)
+                total = near[j, rows, :] + jnp.where(here, far[b : b + 1], 0.0)
+                out[rows, cols] = total.astype(BF)
 
 
 def exchange(x, bit):
@@ -538,7 +545,8 @@
         cost_estimate=cost(10**7, 4 * 10**6, 10**5),
         name="pre",
     )(idx, *near0, *near1, mid_o, mid_lse, out_grad)
-    far1, bundle = after((far1, bundle))
+    rows, bundle = after((far1, bundle))
+    far1 = rows[:, : 2 * HD]
     mate_stats = to_even(bundle[48:])
     from1 = chip_exchange(far1, 32, 1)
     stats = joined(mate_stats, bundle[48:])
@@ -561,14 +569,14 @@
 
     packs, fix = pl.pallas_call(
         far_kernel,
-        out_shape=(sds((64, 256), BF), sds((8, HD), F32)),
-        in_specs=[SMEM] + [VMEM] * 3,
+        out_shape=(sds((64, 384), BF), sds((8, HD), F32)),
+        in_specs=[SMEM] + [VMEM] * 4,
         out_specs=(VMEM,) * 2,
         scratch_shapes=[pltpu.VMEM((4, 64, HD), F32)],
         compiler_params=PARAMS,
         cost_estimate=cost(10**7, 10**6, 10**5),
         name="far",
-    )(idx, far_all, bundle, mate)
+    )(idx, far_all, rows, bundle, mate)
 
     packs_even = to_even(packs)
     fix1 = head_exchange(fix, 2, 1)
@@ -587,7 +595,6 @@
         name="far_query",
     )(idx, far_even, packs_even)
     part_b, fix, far_dq = after((joined(part_a, part2), fix + fix2, far_dq))
-    mate_dq = to_odd(far_dq)
     fix3 = head_exchange(fix, 4, 1)
     part3 = chip_exchange(part_b, 8, 0)
     part_c, fix = after((joined(part_b, part3), fix + fix3))
@@ -636,14 +643,27 @@
 
     far_kv = pl.pallas_call(
         far_key_kernel,
-        out_shape=sds((64, HD), F32),
-        in_specs=[SMEM] + [VMEM] * 2,
+        out_shape=sds((96, HD), F32),
+        in_specs=[SMEM] + [VMEM] * 3,
         out_specs=VMEM,
         compiler_params=PARAMS,
         cost_estimate=cost(10**7, 10**6, 10**5),
         name="far_key",
-    )(idx, far_even, far_gs)
+    )(idx, far_even, far_gs, far_dq)
     mate_kv = to_odd(far_kv)
+
+    mid_gall = joined(mid_gs, mid_g2)
+    dk, dv = pl.pallas_call(
+        mid_key_kernel,
+        out_shape=(by_head_shape, by_head_shape),
+        in_specs=[SMEM] + [VMEM] * 6,
+        out_specs=(VMEM,) * 2,
+        compiler_params=PARAMS,
+        cost_estimate=cost(2 * 10**8, 4 * 10**6, 10**5),
+        name="mid_key",
+    )(idx, dk0, dk1, dv0, dv1, mid_all, mid_gall)
+
+    mate_kv, dk = after((mate_kv, dk))
 
     grad_queries = pl.pallas_call(
         query_grad_kernel,
@@ -654,25 +674,13 @@
         compiler_params=PARAMS,
         cost_estimate=cost(2 * 10**8, 3 * 10**6, 10**5),
         name="query_grad",
-    )(idx, dq0, dq1, mid_all, mid_g, mate_dq, far_dq)
-
-    mid_gall, grad_queries = after((joined(mid_gs, mid_g2), grad_queries))
-    dk, dv = pl.pallas_call(
-        mid_key_kernel,
-        out_shape=(by_head_shape, by_head_shape),
-        in_specs=[SMEM] + [VMEM] * 6,
-        out_specs=(VMEM,) * 2,
-        compiler_params=PARAMS,
-        cost_estimate=cost(2 * 10**8, 4 * 10**6, 10**5),
-        name="mid_key",
-    )(idx, dk0, dk1, dv0, dv1, mid_all, mid_gall)
+    )(idx, dq0, dq1, mid_all, mid_g, mate_kv, far_kv)
 
     grad_keys, grad_values, whole = pl.pallas_call(
         key_grad_kernel,
         out_shape=(sds((TOK, 256), BF), sds((TOK, 256), BF), sds((2, 8, 256), F32)),
         in_specs=[SMEM] + [VMEM] * 4,
         out_specs=(VMEM,) * 3,
-        scratch_shapes=[pltpu.VMEM((4, TOK, HD), F32)],
         compiler_params=PARAMS,
         cost_estimate=cost(10**6, 4 * 10**6),
         name="key_grad",

time: 124 us -> 123 us (level)
  waiting for transfers between devices: 33.2 us -> 29.3 us
  starting transfers between devices: 63.1 us -> 66.4 us
    ppermute x10, waiting for transfers between devices: 19.3 us -> 16.4 us  [chip_exchange(): return lax.ppermute(x, 'seq', [(i, i ^ bit) for i in range(parity, 64, 2)])]
    ppermute x4, starting transfers between devices: 17.3 us -> 18.9 us  [exchange(): return lax.ppermute(x, 'seq', [(i, i ^ bit) for i in range(64)])]
    ppermute x4 -> x3, starting transfers between devices: 5.17 us -> 3.88 us  [to_odd(): return lax.ppermute(x, 'seq', [(i, i + 1) for i in range(0, 64, 2)])]
    ppermute x4, starting transfers between devices: 6.7 us -> 7.98 us  [to_even(): return lax.ppermute(x, 'seq', [(i + 1, i) for i in range(0, 64, 2)])]
  transfers between devices with their start and end apart: 28 -> 27, of which waited for: 13 -> 14; matrix products, arithmetic and copies ran while one was open for 0% -> 0% of each run, Pallas kernels for 13% -> 11%
where the time goes in v4:
time: 123 us; the launch traced here: 122 us
  starting transfers between devices  66.4 us (54%)
  waiting for transfers between devices  29.3 us (24%)
  Pallas kernels  21.8 us (18%)
  local copies, waits for them, and re-layouts  3.26 us (3%)
    ppermute x4, starting transfers between devices, exchange(): return lax.ppermute(x, 'seq', [(i, i ^ bit) for i in range(64)])  18.9 us
    ppermute x6, starting transfers between devices, head_exchange(): return lax.ppermute(x, ('seq', 'head'), pairs)  18.1 us
    ppermute x10, starting transfers between devices, chip_exchange(): return lax.ppermute(x, 'seq', [(i, i ^ bit) for i in range(parity, 64, 2)])  17.5 us
    ppermute x10, waiting for transfers between devices, chip_exchange(): return lax.ppermute(x, 'seq', [(i, i ^ bit) for i in range(parity, 64, 2)])  16.4 us
    ppermute x4, starting transfers between devices, to_even(): return lax.ppermute(x, 'seq', [(i + 1, i) for i in range(0, 64, 2)])  7.98 us
    ppermute x6, waiting for transfers between devices, head_exchange(): return lax.ppermute(x, ('seq', 'head'), pairs)  7.12 us
    pallas_call x2, Pallas kernels, near_backward(): pl.pallas_call(near_backward_kernel, grid=(2,), out_shape=(half_shape,) *...  4.26 us
    ppermute x3, starting transfers between devices, to_odd(): return lax.ppermute(x, 'seq', [(i, i + 1) for i in range(0, 64, 2)])  3.88 us
  transfers between devices with their start and end apart: 27, of which 14 were waited for; matrix products, arithmetic and copies ran while one was open for 0% of the time, Pallas kernels for 11%

profile of v4, /device:TPU:1, one launch (start us, length us, event | category | flops | bytes accessed | tf_op | source)
XLA Modules:
  0.0 122.3 jit_solution(10024464363016046853)
XLA Ops:
  4.7 4.0 %collective-permute-start = (bf16[256,384]{1,0:T(8,128)(2,1)S(1)}, bf16[256,384]{1,0:T(8,128)(2,1)S(1)}, u32[]{:S(2)}, u32[]{:S(2)}) collective-permute-start(bf16[256,384]{1,0:T(8,128)(2,1)S(1)} %get-tuple-element.63), channel_id=1, source_target_pairs={{0,16},{8,24},{16,0},{24,8},{32,48},{40,56},{48,32},{56,40},{64,80... | collective-permute-start | bytes 589832 | tf_op jit(solution)/shard_map/ppermute | solution.py:453
  10.1 1.7 %near_forward_0.1 = (f32[2,512,128]{2,1,0:T(8,128)S(1)}, f32[2,512,128]{2,1,0:T(8,128)S(1)}) custom-call(bf16[1024,256]{1,0:T(8,128)(2,1)S(1)} %copy-done, bf16[1024,256]{1,0:T(8,128)(2,1)S(1)} %copy-done.2, bf16[1024,256]{1,0:T(8,128)(2,1)S(1)} %copy-done.4), custom_call_target="tpu_custom_call" | custom-call | flops 400000000 | bytes 2000000 | tf_op jit(solution)/shard_map/near_forward_0/pallas_call | solution.py:509
  11.8 1.7 %near_forward_1.1 = (f32[2,512,128]{2,1,0:T(8,128)S(1)}, f32[2,512,128]{2,1,0:T(8,128)S(1)}) custom-call(bf16[1024,256]{1,0:T(8,128)(2,1)S(1)} %copy-done, bf16[1024,256]{1,0:T(8,128)(2,1)S(1)} %copy-done.2, bf16[1024,256]{1,0:T(8,128)(2,1)S(1)} %copy-done.4), custom_call_target="tpu_custom_call" | custom-call | flops 400000000 | bytes 2000000 | tf_op jit(solution)/shard_map/near_forward_1/pallas_call | solution.py:509
  13.5 2.0 %collective-permute-done.1 = bf16[16,384]{1,0:T(8,128)(2,1)S(1)} collective-permute-done((bf16[16,384]{1,0:T(8,128)(2,1)S(1)}, bf16[16,384]{1,0:T(8,128)(2,1)S(1)}, u32[]{:S(2)}, u32[]{:S(2)}) %collective-permute-start.1) | collective-permute-done | bytes 12320 | tf_op jit(solution)/shard_map/ppermute | solution.py:466
  15.5 5.7 %collective-permute-start.2 = (bf16[512,384]{1,0:T(8,128)(2,1)S(1)}, bf16[512,384]{1,0:T(8,128)(2,1)S(1)}, u32[]{:S(2)}, u32[]{:S(2)}) collective-permute-start(bf16[512,384]{1,0:T(8,128)(2,1)S(1)} %pad_maximum_fusion.3), channel_id=1, source_target_pairs={{0,8},{8,0},{16,24},{24,16},{32,40},{40,32},{48,56},{56,48},{64,72... | collective-permute-start | bytes 1179656 | tf_op jit(solution)/shard_map/ppermute | solution.py:453
  23.9 1.6 %pre.1 = (bf16[1024,256]{1,0:T(8,128)(2,1)S(1)}, f32[2,1024,128]{2,1,0:T(8,128)S(1)}, f32[80,128]{1,0:T(8,128)S(1)}) custom-call(s32[2]{0:T(128)S(1)} %pad_add_fusion.idx, f32[2,512,128]{2,1,0:T(8,128)S(1)} %get-tuple-element.70.o0, f32[2,512,128]{2,1,0:T(8,128)S(1)} %get-tuple-element.71.lse0, f32[2,512,128]{2,1,0:T(8,128)S(1)} %get-tuple-element.72.o1, ...), custom_call_target="tpu_custom_call" | custom-call | flops 10000000 | bytes 4000000 | tf_op jit(solution)/shard_map/pre/pallas_call | solution.py:538
  25.5 2.3 %collective-permute-start.4 = (f32[32,128]{1,0:T(8,128)S(1)}, f32[32,128]{1,0:T(8,128)S(1)}, u32[]{:S(2)}, u32[]{:S(2)}) collective-permute-start(f32[32,128]{1,0:T(8,128)S(1)} %slice.14), channel_id=1, source_target_pairs={{8,0},{24,16},{40,32},{56,48},{72,64},{88,80},{104,96},{120,112},{... | collective-permute-start | bytes 49160 | tf_op jit(solution)/shard_map/ppermute | solution.py:470
  27.8 4.4 %collective-permute-start.3 = (bf16[32,256]{1,0:T(8,128)(2,1)S(1)}, bf16[32,256]{1,0:T(8,128)(2,1)S(1)}, u32[]{:S(2)}, u32[]{:S(2)}) collective-permute-start(bf16[32,256]{1,0:T(8,128)(2,1)S(1)} %slice.13), channel_id=1, source_target_pairs={{8,264},{24,280},{40,296},{56,312},{72,328},{88,344},{104,360},{12... | collective-permute-start | bytes 49160 | tf_op jit(solution)/shard_map/ppermute | solution.py:457
  32.9 3.3 %collective-permute-done.3 = bf16[32,256]{1,0:T(8,128)(2,1)S(1)} collective-permute-done((bf16[32,256]{1,0:T(8,128)(2,1)S(1)}, bf16[32,256]{1,0:T(8,128)(2,1)S(1)}, u32[]{:S(2)}, u32[]{:S(2)}) %collective-permute-start.3) | collective-permute-done | bytes 16416 | tf_op jit(solution)/shard_map/ppermute | solution.py:457
  36.9 2.0 %collective-permute-start.6 = (bf16[64,256]{1,0:T(8,128)(2,1)S(1)}, bf16[64,256]{1,0:T(8,128)(2,1)S(1)}, u32[]{:S(2)}, u32[]{:S(2)}) collective-permute-start(bf16[64,256]{1,0:T(8,128)(2,1)S(1)} %pad_maximum_fusion.13), channel_id=1, source_target_pairs={{8,136},{24,152},{40,168},{56,184},{72,200},{88,216},{104,232},{12... | collective-permute-start | bytes 98312 | tf_op jit(solution)/shard_map/ppermute | solution.py:457
  39.0 3.5 %collective-permute-done.6 = bf16[64,256]{1,0:T(8,128)(2,1)S(1)} collective-permute-done((bf16[64,256]{1,0:T(8,128)(2,1)S(1)}, bf16[64,256]{1,0:T(8,128)(2,1)S(1)}, u32[]{:S(2)}, u32[]{:S(2)}) %collective-permute-start.6) | collective-permute-done | bytes 32800 | tf_op jit(solution)/shard_map/ppermute | solution.py:457
  42.5 1.9 %collective-permute-start.8 = (bf16[128,256]{1,0:T(8,128)(2,1)S(1)}, bf16[128,256]{1,0:T(8,128)(2,1)S(1)}, u32[]{:S(2)}, u32[]{:S(2)}) collective-permute-start(bf16[128,256]{1,0:T(8,128)(2,1)S(1)} %pad_maximum_fusion.10), channel_id=1, source_target_pairs={{8,72},{24,88},{40,104},{56,120},{72,8},{88,24},{104,40},{120,56},... | collective-permute-start | bytes 196616 | tf_op jit(solution)/shard_map/ppermute | solution.py:457
  44.4 3.1 %collective-permute-done.8 = bf16[128,256]{1,0:T(8,128)(2,1)S(1)} collective-permute-done((bf16[128,256]{1,0:T(8,128)(2,1)S(1)}, bf16[128,256]{1,0:T(8,128)(2,1)S(1)}, u32[]{:S(2)}, u32[]{:S(2)}) %collective-permute-start.8) | collective-permute-done | bytes 65568 | tf_op jit(solution)/shard_map/ppermute | solution.py:457
  47.5 2.8 %collective-permute-start.9 = (bf16[256,256]{1,0:T(8,128)(2,1)S(1)}, bf16[256,256]{1,0:T(8,128)(2,1)S(1)}, u32[]{:S(2)}, u32[]{:S(2)}) collective-permute-start(bf16[256,256]{1,0:T(8,128)(2,1)S(1)} %pad_maximum_fusion.8), channel_id=1, source_target_pairs={{8,40},{24,56},{40,8},{56,24},{72,104},{88,120},{104,72},{120,88},... | collective-permute-start | bytes 393224 | tf_op jit(solution)/shard_map/ppermute | solution.py:457
  50.3 4.4 %collective-permute-done.9 = bf16[256,256]{1,0:T(8,128)(2,1)S(1)} collective-permute-done((bf16[256,256]{1,0:T(8,128)(2,1)S(1)}, bf16[256,256]{1,0:T(8,128)(2,1)S(1)}, u32[]{:S(2)}, u32[]{:S(2)}) %collective-permute-start.9) | collective-permute-done | bytes 131104 | tf_op jit(solution)/shard_map/ppermute | solution.py:457
  54.8 3.1 %collective-permute-start.10 = (bf16[512,256]{1,0:T(8,128)(2,1)S(1)}, bf16[512,256]{1,0:T(8,128)(2,1)S(1)}, u32[]{:S(2)}, u32[]{:S(2)}) collective-permute-start(bf16[512,256]{1,0:T(8,128)(2,1)S(1)} %pad_maximum_fusion.5), channel_id=1, source_target_pairs={{8,24},{24,8},{40,56},{56,40},{72,88},{88,72},{104,120},{120,104},... | collective-permute-start | bytes 786440 | tf_op jit(solution)/shard_map/ppermute | solution.py:457
  59.8 2.0 %collective-permute-done.10 = bf16[512,256]{1,0:T(8,128)(2,1)S(1)} collective-permute-done((bf16[512,256]{1,0:T(8,128)(2,1)S(1)}, bf16[512,256]{1,0:T(8,128)(2,1)S(1)}, u32[]{:S(2)}, u32[]{:S(2)}) %collective-permute-start.10) | collective-permute-done | bytes 262176 | tf_op jit(solution)/shard_map/ppermute | solution.py:457
  61.9 1.8 %collective-permute-start.18 = (bf16[1024,256]{1,0:T(8,128)(2,1)S(1)}, bf16[1024,256]{1,0:T(8,128)(2,1)S(1)}, u32[]{:S(2)}, u32[]{:S(2)}) collective-permute-start(bf16[1024,256]{1,0:T(8,128)(2,1)S(1)} %pad_maximum_fusion.1.far_all), channel_id=1, source_target_pairs={{8,0},{24,16},{40,32},{56,48},{72,64},{88,80},{104,96},{120,112},{... | collective-permute-start | bytes 1572872 | tf_op jit(solution)/shard_map/ppermute | solution.py:470
  67.8 2.8 %collective-permute-start.15 = (f32[8,128]{1,0:T(8,128)S(1)}, f32[8,128]{1,0:T(8,128)S(1)}, u32[]{:S(2)}, u32[]{:S(2)}) collective-permute-start(f32[8,128]{1,0:T(8,128)S(1)} %get-tuple-element.87), channel_id=1, source_target_pairs={{8,10},{9,11},{10,8},{11,9},{12,14},{13,15},{14,12},{15,13},{24,26... | collective-permute-start | bytes 12296 | tf_op jit(solution)/shard_map/ppermute | solution.py:462
  70.5 3.1 %collective-permute-done.15 = f32[8,128]{1,0:T(8,128)S(1)} collective-permute-done((f32[8,128]{1,0:T(8,128)S(1)}, f32[8,128]{1,0:T(8,128)S(1)}, u32[]{:S(2)}, u32[]{:S(2)}) %collective-permute-start.15) | collective-permute-done | bytes 4128 | tf_op jit(solution)/shard_map/ppermute | solution.py:462
  74.3 1.9 %collective-permute-start.17 = (f32[8,128]{1,0:T(8,128)S(1)}, f32[8,128]{1,0:T(8,128)S(1)}, u32[]{:S(2)}, u32[]{:S(2)}) collective-permute-start(f32[8,128]{1,0:T(8,128)S(1)} %add.21), channel_id=1, source_target_pairs={{8,9},{9,8},{10,11},{11,10},{12,13},{13,12},{14,15},{15,14},{24,25... | collective-permute-start | bytes 12296 | tf_op jit(solution)/shard_map/ppermute | solution.py:462
  76.2 2.4 %collective-permute-done.17 = f32[8,128]{1,0:T(8,128)S(1)} collective-permute-done((f32[8,128]{1,0:T(8,128)S(1)}, f32[8,128]{1,0:T(8,128)S(1)}, u32[]{:S(2)}, u32[]{:S(2)}) %collective-permute-start.17) | collective-permute-done | bytes 4128 | tf_op jit(solution)/shard_map/ppermute | solution.py:462
  79.9 11.5 %collective-permute-start.20 = (f32[8,128]{1,0:T(8,128)S(1)}, f32[8,128]{1,0:T(8,128)S(1)}, u32[]{:S(2)}, u32[]{:S(2)}) collective-permute-start(f32[8,128]{1,0:T(8,128)S(1)} %add.22), channel_id=1, source_target_pairs={{8,12},{9,13},{10,14},{11,15},{12,8},{13,9},{14,10},{15,11},{24,28... | collective-permute-start | bytes 12296 | tf_op jit(solution)/shard_map/ppermute | solution.py:462
  91.4 1.6 %collective-permute-done.20 = f32[8,128]{1,0:T(8,128)S(1)} collective-permute-done((f32[8,128]{1,0:T(8,128)S(1)}, f32[8,128]{1,0:T(8,128)S(1)}, u32[]{:S(2)}, u32[]{:S(2)}) %collective-permute-start.20) | collective-permute-done | bytes 4128 | tf_op jit(solution)/shard_map/ppermute | solution.py:462
  93.7 2.6 %collective-permute-start.21 = (f32[8,128]{1,0:T(8,128)S(1)}, f32[8,128]{1,0:T(8,128)S(1)}, u32[]{:S(2)}, u32[]{:S(2)}) collective-permute-start(f32[8,128]{1,0:T(8,128)S(1)} %add.23.fix_own), channel_id=1, source_target_pairs={{8,0},{24,16},{40,32},{56,48},{72,64},{88,80},{104,96},{120,112},{... | collective-permute-start | bytes 12296 | tf_op jit(solution)/shard_map/ppermute | solution.py:470
  97.1 3.0 %norm.1 = (bf16[1024,256]{1,0:T(8,128)(2,1)}, bf16[1024,256]{1,0:T(8,128)(2,1)S(1)}, f32[2,1024,128]{2,1,0:T(8,128)S(1)}, f32[2,1024,128]{2,1,0:T(8,128)S(1)}, bf16[256,256]{1,0:T(8,128)(2,1)S(1)}) custom-call(s32[2]{0:T(128)S(1)} %pad_add_fusion.idx, f32[112,128]{1,0:T(8,128)S(1)} %collective-permute-done.12.mate_ref, f32[64,128]{1,0:T(8,128)S(1)} %add.20.stat_ref, ...), custom_call_target="tpu_custom_call" | custom-call | flops 10000000 | bytes 4000000 | tf_op jit(solution)/shard_map/norm/pallas_call | solution.py:603
  100.9 2.3 %collective-permute-start.23 = (bf16[256,256]{1,0:T(8,128)(2,1)S(1)}, bf16[256,256]{1,0:T(8,128)(2,1)S(1)}, u32[]{:S(2)}, u32[]{:S(2)}) collective-permute-start(bf16[256,256]{1,0:T(8,128)(2,1)S(1)} %get-tuple-element.98.mid_g), channel_id=1, source_target_pairs={{0,16},{8,24},{16,0},{24,8},{32,48},{40,56},{48,32},{56,40},{64,80... | collective-permute-start | bytes 393224 | tf_op jit(solution)/shard_map/ppermute | solution.py:453
  103.2 2.1 %near_backward_1.1 = (f32[2,512,128]{2,1,0:T(8,128)S(1)}, f32[2,512,128]{2,1,0:T(8,128)S(1)}, f32[2,512,128]{2,1,0:T(8,128)S(1)}) custom-call(bf16[1024,256]{1,0:T(8,128)(2,1)S(1)} %copy-done.1, bf16[1024,256]{1,0:T(8,128)(2,1)S(1)} %copy-done.3, bf16[1024,256]{1,0:T(8,128)(2,1)S(1)} %copy-done.5, bf16[1024,256]{1,0:T(8,128)(2,1)S(1)} %get-tuple-element.100.g_ref, ...), custom_call_target="tpu_custom_call" | custom-call | flops 1000000000 | bytes 4000000 | tf_op jit(solution)/shard_map/near_backward_1/pallas_call | solution.py:623
  105.3 2.1 %near_backward_0.1 = (f32[2,512,128]{2,1,0:T(8,128)S(1)}, f32[2,512,128]{2,1,0:T(8,128)S(1)}, f32[2,512,128]{2,1,0:T(8,128)S(1)}) custom-call(bf16[1024,256]{1,0:T(8,128)(2,1)S(1)} %copy-done.1, bf16[1024,256]{1,0:T(8,128)(2,1)S(1)} %copy-done.3, bf16[1024,256]{1,0:T(8,128)(2,1)S(1)} %copy-done.5, bf16[1024,256]{1,0:T(8,128)(2,1)S(1)} %get-tuple-element.100.g_ref, ...), custom_call_target="tpu_custom_call" | custom-call | flops 1000000000 | bytes 4000000 | tf_op jit(solution)/shard_map/near_backward_0/pallas_call | solution.py:623
  108.1 6.9 %collective-permute-start.26 = (bf16[512,256]{1,0:T(8,128)(2,1)S(1)}, bf16[512,256]{1,0:T(8,128)(2,1)S(1)}, u32[]{:S(2)}, u32[]{:S(2)}) collective-permute-start(bf16[512,256]{1,0:T(8,128)(2,1)S(1)} %pad_maximum_fusion.6), channel_id=1, source_target_pairs={{0,8},{8,0},{16,24},{24,16},{32,40},{40,32},{48,56},{56,48},{64,72... | collective-permute-start | bytes 786440 | tf_op jit(solution)/shard_map/ppermute | solution.py:453
  118.6 1.6 %key_grad.1 = (bf16[1024,256]{1,0:T(8,128)(2,1)}, bf16[1024,256]{1,0:T(8,128)(2,1)}, f32[2,8,256]{2,1,0:T(8,128)}) custom-call(s32[2]{0:T(128)S(1)} %pad_add_fusion.idx, f32[2,1024,128]{2,1,0:T(8,128)S(1)} %get-tuple-element.116.dk_in, f32[2,1024,128]{2,1,0:T(8,128)S(1)} %get-tuple-element.117.dv_in, f32[96,128]{1,0:T(8,128)S(1)} %collective-permute-done.25.far_got, ...), custom_call_target="tpu_custom_call" | custom-call | flops 1000000 | bytes 4000000 | tf_op jit(solution)/shard_map/key_grad/pallas_call | solution.py:679
  120.2 2.1 %query_grad.1 = bf16[1024,256]{1,0:T(8,128)(2,1)} custom-call(s32[2]{0:T(128)S(1)} %pad_add_fusion.idx, f32[2,512,128]{2,1,0:T(8,128)S(1)} %get-tuple-element.105.dq0, f32[2,512,128]{2,1,0:T(8,128)S(1)} %get-tuple-element.106.dq1, bf16[1024,384]{1,0:T(8,128)(2,1)S(1)} %constant_dynamic-update-slice_fusion.mid_ref, ...), custom_call_target="tpu_custom_call" | custom-call | flops 200000000 | bytes 3000000 | tf_op jit(solution)/shard_map/query_grad/pallas_call | solution.py:668
  (79 shorter events, 23.8 us)
Async XLA Ops:
  0.7 1.0 copy-start
  4.7 10.8 %collective-permute-start = (bf16[256,384]{1,0:T(8,128)(2,1)S(1)}, bf16[256,384]{1,0:T(8,128)(2,1)S(1)}, u32[]{:S(2)}, u32[]{:S(2)}) collective-permute-start(bf16[256,384]{1,0:T(8,128)(2,1)S(1)} %get-tuple-element.63), channel_id=1, source_target_pairs={{0,16},{8,24},{16,0},{24,8},{32,48},{40,56},{48,32},{56,40},{64,80... | collective-permute-start | bytes 589832 | tf_op jit(solution)/shard_map/ppermute | solution.py:453
  8.8 6.7 %collective-permute-start.1 = (bf16[16,384]{1,0:T(8,128)(2,1)S(1)}, bf16[16,384]{1,0:T(8,128)(2,1)S(1)}, u32[]{:S(2)}, u32[]{:S(2)}) collective-permute-start(bf16[16,384]{1,0:T(8,128)(2,1)S(1)} %get-tuple-element.64), channel_id=1, source_target_pairs={{0,8},{16,24},{32,40},{48,56},{64,72},{80,88},{96,104},{112,120},{... | collective-permute-start | bytes 36872 | tf_op jit(solution)/shard_map/ppermute | solution.py:466
  15.5 8.4 %copy-start.6 = (bf16[1024,256]{1,0:T(8,128)(2,1)S(1)}, bf16[1024,256]{1,0:T(8,128)(2,1)}, u32[]{:S(2)}) copy-start(bf16[1024,256]{1,0:T(8,128)(2,1)} %g_ref.3) | copy-start | bytes 1572868
  15.5 7.1 %collective-permute-start.2 = (bf16[512,384]{1,0:T(8,128)(2,1)S(1)}, bf16[512,384]{1,0:T(8,128)(2,1)S(1)}, u32[]{:S(2)}, u32[]{:S(2)}) collective-permute-start(bf16[512,384]{1,0:T(8,128)(2,1)S(1)} %pad_maximum_fusion.3), channel_id=1, source_target_pairs={{0,8},{8,0},{16,24},{24,16},{32,40},{40,32},{48,56},{56,48},{64,72... | collective-permute-start | bytes 1179656 | tf_op jit(solution)/shard_map/ppermute | solution.py:453
  25.5 6.7 %collective-permute-start.4 = (f32[32,128]{1,0:T(8,128)S(1)}, f32[32,128]{1,0:T(8,128)S(1)}, u32[]{:S(2)}, u32[]{:S(2)}) collective-permute-start(f32[32,128]{1,0:T(8,128)S(1)} %slice.14), channel_id=1, source_target_pairs={{8,0},{24,16},{40,32},{56,48},{72,64},{88,80},{104,96},{120,112},{... | collective-permute-start | bytes 49160 | tf_op jit(solution)/shard_map/ppermute | solution.py:470
  27.8 8.4 %collective-permute-start.3 = (bf16[32,256]{1,0:T(8,128)(2,1)S(1)}, bf16[32,256]{1,0:T(8,128)(2,1)S(1)}, u32[]{:S(2)}, u32[]{:S(2)}) collective-permute-start(bf16[32,256]{1,0:T(8,128)(2,1)S(1)} %slice.13), channel_id=1, source_target_pairs={{8,264},{24,280},{40,296},{56,312},{72,328},{88,344},{104,360},{12... | collective-permute-start | bytes 49160 | tf_op jit(solution)/shard_map/ppermute | solution.py:457
  32.3 4.0 %collective-permute-start.5 = (f32[64,128]{1,0:T(8,128)S(1)}, f32[64,128]{1,0:T(8,128)S(1)}, u32[]{:S(2)}, u32[]{:S(2)}) collective-permute-start(f32[64,128]{1,0:T(8,128)S(1)} %pad_maximum_fusion.14), channel_id=1, source_target_pairs={{0,2},{1,3},{2,0},{3,1},{4,6},{5,7},{6,4},{7,5},{16,18},{17,19},{1... | collective-permute-start | bytes 98312 | tf_op jit(solution)/shard_map/ppermute | solution.py:462
  36.3 2.7 %collective-permute-start.7 = (f32[64,128]{1,0:T(8,128)S(1)}, f32[64,128]{1,0:T(8,128)S(1)}, u32[]{:S(2)}, u32[]{:S(2)}) collective-permute-start(f32[64,128]{1,0:T(8,128)S(1)} %fusion), channel_id=1, source_target_pairs={{0,1},{1,0},{2,3},{3,2},{4,5},{5,4},{6,7},{7,6},{16,17},{17,16},{1... | collective-permute-start | bytes 98312 | tf_op jit(solution)/shard_map/ppermute | solution.py:462
  36.9 5.6 %collective-permute-start.6 = (bf16[64,256]{1,0:T(8,128)(2,1)S(1)}, bf16[64,256]{1,0:T(8,128)(2,1)S(1)}, u32[]{:S(2)}, u32[]{:S(2)}) collective-permute-start(bf16[64,256]{1,0:T(8,128)(2,1)S(1)} %pad_maximum_fusion.13), channel_id=1, source_target_pairs={{8,136},{24,152},{40,168},{56,184},{72,200},{88,216},{104,232},{12... | collective-permute-start | bytes 98312 | tf_op jit(solution)/shard_map/ppermute | solution.py:457
  42.5 5.0 %collective-permute-start.8 = (bf16[128,256]{1,0:T(8,128)(2,1)S(1)}, bf16[128,256]{1,0:T(8,128)(2,1)S(1)}, u32[]{:S(2)}, u32[]{:S(2)}) collective-permute-start(bf16[128,256]{1,0:T(8,128)(2,1)S(1)} %pad_maximum_fusion.10), channel_id=1, source_target_pairs={{8,72},{24,88},{40,104},{56,120},{72,8},{88,24},{104,40},{120,56},... | collective-permute-start | bytes 196616 | tf_op jit(solution)/shard_map/ppermute | solution.py:457
  47.5 7.2 %collective-permute-start.9 = (bf16[256,256]{1,0:T(8,128)(2,1)S(1)}, bf16[256,256]{1,0:T(8,128)(2,1)S(1)}, u32[]{:S(2)}, u32[]{:S(2)}) collective-permute-start(bf16[256,256]{1,0:T(8,128)(2,1)S(1)} %pad_maximum_fusion.8), channel_id=1, source_target_pairs={{8,40},{24,56},{40,8},{56,24},{72,104},{88,120},{104,72},{120,88},... | collective-permute-start | bytes 393224 | tf_op jit(solution)/shard_map/ppermute | solution.py:457
  54.8 7.1 %collective-permute-start.10 = (bf16[512,256]{1,0:T(8,128)(2,1)S(1)}, bf16[512,256]{1,0:T(8,128)(2,1)S(1)}, u32[]{:S(2)}, u32[]{:S(2)}) collective-permute-start(bf16[512,256]{1,0:T(8,128)(2,1)S(1)} %pad_maximum_fusion.5), channel_id=1, source_target_pairs={{8,24},{24,8},{40,56},{56,40},{72,88},{88,72},{104,120},{120,104},... | collective-permute-start | bytes 786440 | tf_op jit(solution)/shard_map/ppermute | solution.py:457
  57.8 0.7 collective-permute-start.11
  58.5 3.4 %collective-permute-start.12 = (f32[112,128]{1,0:T(8,128)S(1)}, f32[112,128]{1,0:T(8,128)S(1)}, u32[]{:S(2)}, u32[]{:S(2)}) collective-permute-start(f32[112,128]{1,0:T(8,128)S(1)} %pad_maximum_fusion.11), channel_id=1, source_target_pairs={{0,8},{16,24},{32,40},{48,56},{64,72},{80,88},{96,104},{112,120},{... | collective-permute-start | bytes 172040 | tf_op jit(solution)/shard_map/ppermute | solution.py:466
  61.9 16.8 %collective-permute-start.18 = (bf16[1024,256]{1,0:T(8,128)(2,1)S(1)}, bf16[1024,256]{1,0:T(8,128)(2,1)S(1)}, u32[]{:S(2)}, u32[]{:S(2)}) collective-permute-start(bf16[1024,256]{1,0:T(8,128)(2,1)S(1)} %pad_maximum_fusion.1.far_all), channel_id=1, source_target_pairs={{8,0},{24,16},{40,32},{56,48},{72,64},{88,80},{104,96},{120,112},{... | collective-permute-start | bytes 1572872 | tf_op jit(solution)/shard_map/ppermute | solution.py:470
  64.9 2.2 %collective-permute-start.13 = (bf16[64,384]{1,0:T(8,128)(2,1)S(1)}, bf16[64,384]{1,0:T(8,128)(2,1)S(1)}, u32[]{:S(2)}, u32[]{:S(2)}) collective-permute-start(bf16[64,384]{1,0:T(8,128)(2,1)S(1)} %get-tuple-element.86.packs_own), channel_id=1, source_target_pairs={{8,0},{24,16},{40,32},{56,48},{72,64},{88,80},{104,96},{120,112},{... | collective-permute-start | bytes 147464 | tf_op jit(solution)/shard_map/ppermute | solution.py:470
  67.1 6.5 %collective-permute-start.14 = (bf16[32,384]{1,0:T(8,128)(2,1)S(1)}, bf16[32,384]{1,0:T(8,128)(2,1)S(1)}, u32[]{:S(2)}, u32[]{:S(2)}) collective-permute-start(bf16[32,384]{1,0:T(8,128)(2,1)S(1)} %slice.17), channel_id=1, source_target_pairs={{0,256},{16,272},{32,288},{48,304},{64,320},{80,336},{96,352},{112... | collective-permute-start | bytes 73736 | tf_op jit(solution)/shard_map/ppermute | solution.py:457
  67.8 5.9 %collective-permute-start.15 = (f32[8,128]{1,0:T(8,128)S(1)}, f32[8,128]{1,0:T(8,128)S(1)}, u32[]{:S(2)}, u32[]{:S(2)}) collective-permute-start(f32[8,128]{1,0:T(8,128)S(1)} %get-tuple-element.87), channel_id=1, source_target_pairs={{8,10},{9,11},{10,8},{11,9},{12,14},{13,15},{14,12},{15,13},{24,26... | collective-permute-start | bytes 12296 | tf_op jit(solution)/shard_map/ppermute | solution.py:462
  73.6 5.0 %collective-permute-start.16 = (bf16[64,384]{1,0:T(8,128)(2,1)S(1)}, bf16[64,384]{1,0:T(8,128)(2,1)S(1)}, u32[]{:S(2)}, u32[]{:S(2)}) collective-permute-start(bf16[64,384]{1,0:T(8,128)(2,1)S(1)} %pad_maximum_fusion.12), channel_id=1, source_target_pairs={{0,128},{16,144},{32,160},{48,176},{64,192},{80,208},{96,224},{112... | collective-permute-start | bytes 147464 | tf_op jit(solution)/shard_map/ppermute | solution.py:457
  74.3 4.4 %collective-permute-start.17 = (f32[8,128]{1,0:T(8,128)S(1)}, f32[8,128]{1,0:T(8,128)S(1)}, u32[]{:S(2)}, u32[]{:S(2)}) collective-permute-start(f32[8,128]{1,0:T(8,128)S(1)} %add.21), channel_id=1, source_target_pairs={{8,9},{9,8},{10,11},{11,10},{12,13},{13,12},{14,15},{15,14},{24,25... | collective-permute-start | bytes 12296 | tf_op jit(solution)/shard_map/ppermute | solution.py:462
  79.3 13.7 %collective-permute-start.19 = (bf16[128,384]{1,0:T(8,128)(2,1)S(1)}, bf16[128,384]{1,0:T(8,128)(2,1)S(1)}, u32[]{:S(2)}, u32[]{:S(2)}) collective-permute-start(bf16[128,384]{1,0:T(8,128)(2,1)S(1)} %pad_maximum_fusion.9), channel_id=1, source_target_pairs={{0,64},{16,80},{32,96},{48,112},{64,0},{80,16},{96,32},{112,48},{1... | collective-permute-start | bytes 294920 | tf_op jit(solution)/shard_map/ppermute | solution.py:457
  79.9 13.1 %collective-permute-start.20 = (f32[8,128]{1,0:T(8,128)S(1)}, f32[8,128]{1,0:T(8,128)S(1)}, u32[]{:S(2)}, u32[]{:S(2)}) collective-permute-start(f32[8,128]{1,0:T(8,128)S(1)} %add.22), channel_id=1, source_target_pairs={{8,12},{9,13},{10,14},{11,15},{12,8},{13,9},{14,10},{15,11},{24,28... | collective-permute-start | bytes 12296 | tf_op jit(solution)/shard_map/ppermute | solution.py:462
  93.0 7.1 %collective-permute-start.22 = (bf16[256,384]{1,0:T(8,128)(2,1)S(1)}, bf16[256,384]{1,0:T(8,128)(2,1)S(1)}, u32[]{:S(2)}, u32[]{:S(2)}) collective-permute-start(bf16[256,384]{1,0:T(8,128)(2,1)S(1)} %pad_maximum_fusion.7), channel_id=1, source_target_pairs={{0,32},{16,48},{32,0},{48,16},{64,96},{80,112},{96,64},{112,80},{1... | collective-permute-start | bytes 589832 | tf_op jit(solution)/shard_map/ppermute | solution.py:457
  93.7 3.4 %collective-permute-start.21 = (f32[8,128]{1,0:T(8,128)S(1)}, f32[8,128]{1,0:T(8,128)S(1)}, u32[]{:S(2)}, u32[]{:S(2)}) collective-permute-start(f32[8,128]{1,0:T(8,128)S(1)} %add.23.fix_own), channel_id=1, source_target_pairs={{8,0},{24,16},{40,32},{56,48},{72,64},{88,80},{104,96},{120,112},{... | collective-permute-start | bytes 12296 | tf_op jit(solution)/shard_map/ppermute | solution.py:470
  97.1 6.1 %copy-start.1 = (bf16[1024,256]{1,0:T(8,128)(2,1)S(1)}, bf16[1024,256]{1,0:T(8,128)(2,1)}, u32[]{:S(2)}) copy-start(bf16[1024,256]{1,0:T(8,128)(2,1)} %q_ref.9) | copy-start | bytes 1572868
  97.1 6.1 %copy-start.3 = (bf16[1024,256]{1,0:T(8,128)(2,1)S(1)}, bf16[1024,256]{1,0:T(8,128)(2,1)}, u32[]{:S(2)}) copy-start(bf16[1024,256]{1,0:T(8,128)(2,1)} %k_ref.9) | copy-start | bytes 1572868
  97.1 6.1 %copy-start.5 = (bf16[1024,256]{1,0:T(8,128)(2,1)S(1)}, bf16[1024,256]{1,0:T(8,128)(2,1)}, u32[]{:S(2)}) copy-start(bf16[1024,256]{1,0:T(8,128)(2,1)} %v_ref.9) | copy-start | bytes 1572868
  100.2 7.8 %collective-permute-start.24 = (bf16[512,384]{1,0:T(8,128)(2,1)S(1)}, bf16[512,384]{1,0:T(8,128)(2,1)S(1)}, u32[]{:S(2)}, u32[]{:S(2)}) collective-permute-start(bf16[512,384]{1,0:T(8,128)(2,1)S(1)} %pad_maximum_fusion.4), channel_id=1, source_target_pairs={{0,16},{16,0},{32,48},{48,32},{64,80},{80,64},{96,112},{112,96},{1... | collective-permute-start | bytes 1179656 | tf_op jit(solution)/shard_map/ppermute | solution.py:457
  100.9 7.1 %collective-permute-start.23 = (bf16[256,256]{1,0:T(8,128)(2,1)S(1)}, bf16[256,256]{1,0:T(8,128)(2,1)S(1)}, u32[]{:S(2)}, u32[]{:S(2)}) collective-permute-start(bf16[256,256]{1,0:T(8,128)(2,1)S(1)} %get-tuple-element.98.mid_g), channel_id=1, source_target_pairs={{0,16},{8,24},{16,0},{24,8},{32,48},{40,56},{48,32},{56,40},{64,80... | collective-permute-start | bytes 393224 | tf_op jit(solution)/shard_map/ppermute | solution.py:453
  108.1 8.7 %collective-permute-start.26 = (bf16[512,256]{1,0:T(8,128)(2,1)S(1)}, bf16[512,256]{1,0:T(8,128)(2,1)S(1)}, u32[]{:S(2)}, u32[]{:S(2)}) collective-permute-start(bf16[512,256]{1,0:T(8,128)(2,1)S(1)} %pad_maximum_fusion.6), channel_id=1, source_target_pairs={{0,8},{8,0},{16,24},{24,16},{32,40},{40,32},{48,56},{56,48},{64,72... | collective-permute-start | bytes 786440 | tf_op jit(solution)/shard_map/ppermute | solution.py:453
  115.5 3.1 %collective-permute-start.25 = (f32[96,128]{1,0:T(8,128)S(1)}, f32[96,128]{1,0:T(8,128)S(1)}, u32[]{:S(2)}, u32[]{:S(2)}) collective-permute-start(f32[96,128]{1,0:T(8,128)S(1)} %far_key.1.far_own), channel_id=1, source_target_pairs={{0,8},{16,24},{32,40},{48,56},{64,72},{80,88},{96,104},{112,120},{... | collective-permute-start | bytes 147464 | tf_op jit(solution)/shard_map/ppermute | solution.py:466
  (2 other events, 2.1 us)

commit v5 on v4

--- a/solution.py
+++ b/solution.py
@@ -580,11 +580,12 @@
 
     packs_even = to_even(packs)
     fix1 = head_exchange(fix, 2, 1)
-    part0 = packs_even[:32]
+    part0, fix = after((packs_even[:32], fix + fix1))
     part1 = chip_exchange(part0, 32, 0)
-    part_a, fix = after((joined(part0, part1), fix + fix1))
     fix2 = head_exchange(fix, 1, 1)
+    part_a, fix = after((joined(part0, part1), fix + fix2))
     part2 = chip_exchange(part_a, 16, 0)
+    fix3 = head_exchange(fix, 4, 1)
     far_dq = pl.pallas_call(
         far_query_kernel,
         out_shape=sds((32, HD), F32),
@@ -594,12 +595,12 @@
         cost_estimate=cost(10**7, 10**6, 10**5),
         name="far_query",
     )(idx, far_even, packs_even)
-    part_b, fix, far_dq = after((joined(part_a, part2), fix + fix2, far_dq))
-    fix3 = head_exchange(fix, 4, 1)
+    part_b, fix = after((joined(part_a, part2), fix + fix3))
     part3 = chip_exchange(part_b, 8, 0)
-    part_c, fix = after((joined(part_b, part3), fix + fix3))
+    part_c, far_dq = after((joined(part_b, part3), far_dq))
     part4 = chip_exchange(part_c, 4, 0)
-    fix_even = to_even(fix)
+    part_c, fix_sent = after((part_c, fix))
+    fix_even = to_even(fix_sent)
     normed, grad, delta, lse, mid_g = pl.pallas_call(
         norm_kernel,
         out_shape=(
@@ -631,8 +632,8 @@
             name=f"near_backward_{block}",
         )(queries, keys, values, grad, lse, delta)
 
-    part_d, mid_g = after((joined(part_c, part4), mid_g))
     mid_g1 = exchange(mid_g, 2)
+    part_d, grad = after((joined(part_c, part4), grad))
     part5 = chip_exchange(part_d, 2, 0)
     dq0, dk0, dv0 = near_backward(0)
     dq1, dk1, dv1 = near_backward(1)
@@ -662,7 +663,6 @@
         cost_estimate=cost(2 * 10**8, 4 * 10**6, 10**5),
         name="mid_key",
     )(idx, dk0, dk1, dv0, dv1, mid_all, mid_gall)
-
     mate_kv, dk = after((mate_kv, dk))
 
     grad_queries = pl.pallas_call(

time: 123 us -> 122 us (level)
  starting transfers between devices: 66.4 us -> 62.9 us
  waiting for transfers between devices: 29.3 us -> 31.5 us
    ppermute x4, starting transfers between devices: 18.9 us -> 15.7 us  [exchange(): return lax.ppermute(x, 'seq', [(i, i ^ bit) for i in range(64)])]
    ppermute x4, waiting for transfers between devices: 1.77 us -> 4.87 us  [exchange(): return lax.ppermute(x, 'seq', [(i, i ^ bit) for i in range(64)])]
  transfers between devices with their start and end apart: 27 -> 27, of which waited for: 14 -> 13; matrix products, arithmetic and copies ran while one was open for 0% -> 0% of each run, Pallas kernels for 11% -> 10%
where the time goes in v5:
time: 122 us; the launch traced here: 121 us
  starting transfers between devices  62.9 us (52%)
  waiting for transfers between devices  31.5 us (26%)
  Pallas kernels  21.8 us (18%)
  local copies, waits for them, and re-layouts  3.26 us (3%)
    ppermute x6, starting transfers between devices, head_exchange(): return lax.ppermute(x, ('seq', 'head'), pairs)  18.1 us
    ppermute x10, starting transfers between devices, chip_exchange(): return lax.ppermute(x, 'seq', [(i, i ^ bit) for i in range(parity, 64, 2)])  17.5 us
    ppermute x10, waiting for transfers between devices, chip_exchange(): return lax.ppermute(x, 'seq', [(i, i ^ bit) for i in range(parity, 64, 2)])  16.4 us
    ppermute x4, starting transfers between devices, exchange(): return lax.ppermute(x, 'seq', [(i, i ^ bit) for i in range(64)])  15.7 us
    ppermute x4, starting transfers between devices, to_even(): return lax.ppermute(x, 'seq', [(i + 1, i) for i in range(0, 64, 2)])  7.69 us
    ppermute x6, waiting for transfers between devices, head_exchange(): return lax.ppermute(x, ('seq', 'head'), pairs)  7.12 us
    ppermute x4, waiting for transfers between devices, exchange(): return lax.ppermute(x, 'seq', [(i, i ^ bit) for i in range(64)])  4.87 us
    pallas_call x2, Pallas kernels, near_backward(): pl.pallas_call(near_backward_kernel, grid=(2,), out_shape=(half_shape,) *...  4.26 us
  transfers between devices with their start and end apart: 27, of which 13 were waited for; matrix products, arithmetic and copies ran while one was open for 0% of the time, Pallas kernels for 10%

profile of v5, /device:TPU:1, one launch (start us, length us, event | category | flops | bytes accessed | tf_op | source)
XLA Modules:
  0.0 121.2 jit_solution(6437855282330305189)
XLA Ops:
  4.7 4.0 %collective-permute-start = (bf16[256,384]{1,0:T(8,128)(2,1)S(1)}, bf16[256,384]{1,0:T(8,128)(2,1)S(1)}, u32[]{:S(2)}, u32[]{:S(2)}) collective-permute-start(bf16[256,384]{1,0:T(8,128)(2,1)S(1)} %get-tuple-element.66), channel_id=1, source_target_pairs={{0,16},{8,24},{16,0},{24,8},{32,48},{40,56},{48,32},{56,40},{64,80... | collective-permute-start | bytes 589832 | tf_op jit(solution)/shard_map/ppermute | solution.py:453
  10.1 1.7 %near_forward_0.1 = (f32[2,512,128]{2,1,0:T(8,128)S(1)}, f32[2,512,128]{2,1,0:T(8,128)S(1)}) custom-call(bf16[1024,256]{1,0:T(8,128)(2,1)S(1)} %copy-done, bf16[1024,256]{1,0:T(8,128)(2,1)S(1)} %copy-done.2, bf16[1024,256]{1,0:T(8,128)(2,1)S(1)} %copy-done.4), custom_call_target="tpu_custom_call" | custom-call | flops 400000000 | bytes 2000000 | tf_op jit(solution)/shard_map/near_forward_0/pallas_call | solution.py:509
  11.8 1.7 %near_forward_1.1 = (f32[2,512,128]{2,1,0:T(8,128)S(1)}, f32[2,512,128]{2,1,0:T(8,128)S(1)}) custom-call(bf16[1024,256]{1,0:T(8,128)(2,1)S(1)} %copy-done, bf16[1024,256]{1,0:T(8,128)(2,1)S(1)} %copy-done.2, bf16[1024,256]{1,0:T(8,128)(2,1)S(1)} %copy-done.4), custom_call_target="tpu_custom_call" | custom-call | flops 400000000 | bytes 2000000 | tf_op jit(solution)/shard_map/near_forward_1/pallas_call | solution.py:509
  13.5 2.0 %collective-permute-done.1 = bf16[16,384]{1,0:T(8,128)(2,1)S(1)} collective-permute-done((bf16[16,384]{1,0:T(8,128)(2,1)S(1)}, bf16[16,384]{1,0:T(8,128)(2,1)S(1)}, u32[]{:S(2)}, u32[]{:S(2)}) %collective-permute-start.1) | collective-permute-done | bytes 12320 | tf_op jit(solution)/shard_map/ppermute | solution.py:466
  15.5 5.7 %collective-permute-start.2 = (bf16[512,384]{1,0:T(8,128)(2,1)S(1)}, bf16[512,384]{1,0:T(8,128)(2,1)S(1)}, u32[]{:S(2)}, u32[]{:S(2)}) collective-permute-start(bf16[512,384]{1,0:T(8,128)(2,1)S(1)} %pad_maximum_fusion.3), channel_id=1, source_target_pairs={{0,8},{8,0},{16,24},{24,16},{32,40},{40,32},{48,56},{56,48},{64,72... | collective-permute-start | bytes 1179656 | tf_op jit(solution)/shard_map/ppermute | solution.py:453
  23.9 1.6 %pre.1 = (bf16[1024,256]{1,0:T(8,128)(2,1)S(1)}, f32[2,1024,128]{2,1,0:T(8,128)S(1)}, f32[80,128]{1,0:T(8,128)S(1)}) custom-call(s32[2]{0:T(128)S(1)} %pad_add_fusion.idx, f32[2,512,128]{2,1,0:T(8,128)S(1)} %get-tuple-element.73.o0, f32[2,512,128]{2,1,0:T(8,128)S(1)} %get-tuple-element.74.lse0, f32[2,512,128]{2,1,0:T(8,128)S(1)} %get-tuple-element.75.o1, ...), custom_call_target="tpu_custom_call" | custom-call | flops 10000000 | bytes 4000000 | tf_op jit(solution)/shard_map/pre/pallas_call | solution.py:538
  25.5 2.3 %collective-permute-start.4 = (f32[32,128]{1,0:T(8,128)S(1)}, f32[32,128]{1,0:T(8,128)S(1)}, u32[]{:S(2)}, u32[]{:S(2)}) collective-permute-start(f32[32,128]{1,0:T(8,128)S(1)} %slice.14), channel_id=1, source_target_pairs={{8,0},{24,16},{40,32},{56,48},{72,64},{88,80},{104,96},{120,112},{... | collective-permute-start | bytes 49160 | tf_op jit(solution)/shard_map/ppermute | solution.py:470
  27.8 4.4 %collective-permute-start.3 = (bf16[32,256]{1,0:T(8,128)(2,1)S(1)}, bf16[32,256]{1,0:T(8,128)(2,1)S(1)}, u32[]{:S(2)}, u32[]{:S(2)}) collective-permute-start(bf16[32,256]{1,0:T(8,128)(2,1)S(1)} %slice.13), channel_id=1, source_target_pairs={{8,264},{24,280},{40,296},{56,312},{72,328},{88,344},{104,360},{12... | collective-permute-start | bytes 49160 | tf_op jit(solution)/shard_map/ppermute | solution.py:457
  32.9 3.3 %collective-permute-done.3 = bf16[32,256]{1,0:T(8,128)(2,1)S(1)} collective-permute-done((bf16[32,256]{1,0:T(8,128)(2,1)S(1)}, bf16[32,256]{1,0:T(8,128)(2,1)S(1)}, u32[]{:S(2)}, u32[]{:S(2)}) %collective-permute-start.3) | collective-permute-done | bytes 16416 | tf_op jit(solution)/shard_map/ppermute | solution.py:457
  36.9 2.0 %collective-permute-start.6 = (bf16[64,256]{1,0:T(8,128)(2,1)S(1)}, bf16[64,256]{1,0:T(8,128)(2,1)S(1)}, u32[]{:S(2)}, u32[]{:S(2)}) collective-permute-start(bf16[64,256]{1,0:T(8,128)(2,1)S(1)} %pad_maximum_fusion.13), channel_id=1, source_target_pairs={{8,136},{24,152},{40,168},{56,184},{72,200},{88,216},{104,232},{12... | collective-permute-start | bytes 98312 | tf_op jit(solution)/shard_map/ppermute | solution.py:457
  39.0 3.5 %collective-permute-done.6 = bf16[64,256]{1,0:T(8,128)(2,1)S(1)} collective-permute-done((bf16[64,256]{1,0:T(8,128)(2,1)S(1)}, bf16[64,256]{1,0:T(8,128)(2,1)S(1)}, u32[]{:S(2)}, u32[]{:S(2)}) %collective-permute-start.6) | collective-permute-done | bytes 32800 | tf_op jit(solution)/shard_map/ppermute | solution.py:457
  42.5 1.9 %collective-permute-start.8 = (bf16[128,256]{1,0:T(8,128)(2,1)S(1)}, bf16[128,256]{1,0:T(8,128)(2,1)S(1)}, u32[]{:S(2)}, u32[]{:S(2)}) collective-permute-start(bf16[128,256]{1,0:T(8,128)(2,1)S(1)} %pad_maximum_fusion.10), channel_id=1, source_target_pairs={{8,72},{24,88},{40,104},{56,120},{72,8},{88,24},{104,40},{120,56},... | collective-permute-start | bytes 196616 | tf_op jit(solution)/shard_map/ppermute | solution.py:457
  44.4 3.1 %collective-permute-done.8 = bf16[128,256]{1,0:T(8,128)(2,1)S(1)} collective-permute-done((bf16[128,256]{1,0:T(8,128)(2,1)S(1)}, bf16[128,256]{1,0:T(8,128)(2,1)S(1)}, u32[]{:S(2)}, u32[]{:S(2)}) %collective-permute-start.8) | collective-permute-done | bytes 65568 | tf_op jit(solution)/shard_map/ppermute | solution.py:457
  47.5 2.8 %collective-permute-start.9 = (bf16[256,256]{1,0:T(8,128)(2,1)S(1)}, bf16[256,256]{1,0:T(8,128)(2,1)S(1)}, u32[]{:S(2)}, u32[]{:S(2)}) collective-permute-start(bf16[256,256]{1,0:T(8,128)(2,1)S(1)} %pad_maximum_fusion.8), channel_id=1, source_target_pairs={{8,40},{24,56},{40,8},{56,24},{72,104},{88,120},{104,72},{120,88},... | collective-permute-start | bytes 393224 | tf_op jit(solution)/shard_map/ppermute | solution.py:457
  50.3 4.4 %collective-permute-done.9 = bf16[256,256]{1,0:T(8,128)(2,1)S(1)} collective-permute-done((bf16[256,256]{1,0:T(8,128)(2,1)S(1)}, bf16[256,256]{1,0:T(8,128)(2,1)S(1)}, u32[]{:S(2)}, u32[]{:S(2)}) %collective-permute-start.9) | collective-permute-done | bytes 131104 | tf_op jit(solution)/shard_map/ppermute | solution.py:457
  54.7 3.1 %collective-permute-start.10 = (bf16[512,256]{1,0:T(8,128)(2,1)S(1)}, bf16[512,256]{1,0:T(8,128)(2,1)S(1)}, u32[]{:S(2)}, u32[]{:S(2)}) collective-permute-start(bf16[512,256]{1,0:T(8,128)(2,1)S(1)} %pad_maximum_fusion.5), channel_id=1, source_target_pairs={{8,24},{24,8},{40,56},{56,40},{72,88},{88,72},{104,120},{120,104},... | collective-permute-start | bytes 786440 | tf_op jit(solution)/shard_map/ppermute | solution.py:457
  59.8 2.0 %collective-permute-done.10 = bf16[512,256]{1,0:T(8,128)(2,1)S(1)} collective-permute-done((bf16[512,256]{1,0:T(8,128)(2,1)S(1)}, bf16[512,256]{1,0:T(8,128)(2,1)S(1)}, u32[]{:S(2)}, u32[]{:S(2)}) %collective-permute-start.10) | collective-permute-done | bytes 262176 | tf_op jit(solution)/shard_map/ppermute | solution.py:457
  63.1 1.8 %collective-permute-start.13 = (bf16[64,384]{1,0:T(8,128)(2,1)S(1)}, bf16[64,384]{1,0:T(8,128)(2,1)S(1)}, u32[]{:S(2)}, u32[]{:S(2)}) collective-permute-start(bf16[64,384]{1,0:T(8,128)(2,1)S(1)} %get-tuple-element.89.packs_own), channel_id=1, source_target_pairs={{8,0},{24,16},{40,32},{56,48},{72,64},{88,80},{104,96},{120,112},{... | collective-permute-start | bytes 147464 | tf_op jit(solution)/shard_map/ppermute | solution.py:470
  66.2 2.8 %collective-permute-start.14 = (f32[8,128]{1,0:T(8,128)S(1)}, f32[8,128]{1,0:T(8,128)S(1)}, u32[]{:S(2)}, u32[]{:S(2)}) collective-permute-start(f32[8,128]{1,0:T(8,128)S(1)} %get-tuple-element.90), channel_id=1, source_target_pairs={{8,10},{9,11},{10,8},{11,9},{12,14},{13,15},{14,12},{15,13},{24,26... | collective-permute-start | bytes 12296 | tf_op jit(solution)/shard_map/ppermute | solution.py:462
  69.0 3.1 %collective-permute-done.14 = f32[8,128]{1,0:T(8,128)S(1)} collective-permute-done((f32[8,128]{1,0:T(8,128)S(1)}, f32[8,128]{1,0:T(8,128)S(1)}, u32[]{:S(2)}, u32[]{:S(2)}) %collective-permute-start.14) | collective-permute-done | bytes 4128 | tf_op jit(solution)/shard_map/ppermute | solution.py:462
  72.8 1.9 %collective-permute-start.16 = (f32[8,128]{1,0:T(8,128)S(1)}, f32[8,128]{1,0:T(8,128)S(1)}, u32[]{:S(2)}, u32[]{:S(2)}) collective-permute-start(f32[8,128]{1,0:T(8,128)S(1)} %add.21), channel_id=1, source_target_pairs={{8,9},{9,8},{10,11},{11,10},{12,13},{13,12},{14,15},{15,14},{24,25... | collective-permute-start | bytes 12296 | tf_op jit(solution)/shard_map/ppermute | solution.py:462
  74.7 2.4 %collective-permute-done.16 = f32[8,128]{1,0:T(8,128)S(1)} collective-permute-done((f32[8,128]{1,0:T(8,128)S(1)}, f32[8,128]{1,0:T(8,128)S(1)}, u32[]{:S(2)}, u32[]{:S(2)}) %collective-permute-start.16) | collective-permute-done | bytes 4128 | tf_op jit(solution)/shard_map/ppermute | solution.py:462
  77.8 11.5 %collective-permute-start.18 = (f32[8,128]{1,0:T(8,128)S(1)}, f32[8,128]{1,0:T(8,128)S(1)}, u32[]{:S(2)}, u32[]{:S(2)}) collective-permute-start(f32[8,128]{1,0:T(8,128)S(1)} %add.22), channel_id=1, source_target_pairs={{8,12},{9,13},{10,14},{11,15},{12,8},{13,9},{14,10},{15,11},{24,28... | collective-permute-start | bytes 12296 | tf_op jit(solution)/shard_map/ppermute | solution.py:462
  92.9 2.3 %collective-permute-start.21 = (f32[8,128]{1,0:T(8,128)S(1)}, f32[8,128]{1,0:T(8,128)S(1)}, u32[]{:S(2)}, u32[]{:S(2)}) collective-permute-start(f32[8,128]{1,0:T(8,128)S(1)} %add.23.fix_own), channel_id=1, source_target_pairs={{8,0},{24,16},{40,32},{56,48},{72,64},{88,80},{104,96},{120,112},{... | collective-permute-start | bytes 12296 | tf_op jit(solution)/shard_map/ppermute | solution.py:470
  96.0 3.0 %norm.1 = (bf16[1024,256]{1,0:T(8,128)(2,1)}, bf16[1024,256]{1,0:T(8,128)(2,1)S(1)}, f32[2,1024,128]{2,1,0:T(8,128)S(1)}, f32[2,1024,128]{2,1,0:T(8,128)S(1)}, bf16[256,256]{1,0:T(8,128)(2,1)S(1)}) custom-call(s32[2]{0:T(128)S(1)} %pad_add_fusion.idx, f32[112,128]{1,0:T(8,128)S(1)} %collective-permute-done.12.mate_ref, f32[64,128]{1,0:T(8,128)S(1)} %add.20.stat_ref, ...), custom_call_target="tpu_custom_call" | custom-call | flops 10000000 | bytes 4000000 | tf_op jit(solution)/shard_map/norm/pallas_call | solution.py:604
  99.0 2.4 %collective-permute-start.22 = (bf16[256,256]{1,0:T(8,128)(2,1)S(1)}, bf16[256,256]{1,0:T(8,128)(2,1)S(1)}, u32[]{:S(2)}, u32[]{:S(2)}) collective-permute-start(bf16[256,256]{1,0:T(8,128)(2,1)S(1)} %get-tuple-element.102.mid_g), channel_id=1, source_target_pairs={{0,16},{8,24},{16,0},{24,8},{32,48},{40,56},{48,32},{56,40},{64,80... | collective-permute-start | bytes 393224 | tf_op jit(solution)/shard_map/ppermute | solution.py:453
  102.2 3.6 %collective-permute-done.22 = bf16[256,256]{1,0:T(8,128)(2,1)S(1)} collective-permute-done((bf16[256,256]{1,0:T(8,128)(2,1)S(1)}, bf16[256,256]{1,0:T(8,128)(2,1)S(1)}, u32[]{:S(2)}, u32[]{:S(2)}) %collective-permute-start.22) | collective-permute-done | bytes 131104 | tf_op jit(solution)/shard_map/ppermute | solution.py:453
  105.8 2.1 %near_backward_1.1 = (f32[2,512,128]{2,1,0:T(8,128)S(1)}, f32[2,512,128]{2,1,0:T(8,128)S(1)}, f32[2,512,128]{2,1,0:T(8,128)S(1)}) custom-call(bf16[1024,256]{1,0:T(8,128)(2,1)S(1)} %copy-done.1, bf16[1024,256]{1,0:T(8,128)(2,1)S(1)} %copy-done.3, bf16[1024,256]{1,0:T(8,128)(2,1)S(1)} %copy-done.5, bf16[1024,256]{1,0:T(8,128)(2,1)S(1)} %get-tuple-element.106.g_ref, ...), custom_call_target="tpu_custom_call" | custom-call | flops 1000000000 | bytes 4000000 | tf_op jit(solution)/shard_map/near_backward_1/pallas_call | solution.py:624
  107.9 2.1 %near_backward_0.1 = (f32[2,512,128]{2,1,0:T(8,128)S(1)}, f32[2,512,128]{2,1,0:T(8,128)S(1)}, f32[2,512,128]{2,1,0:T(8,128)S(1)}) custom-call(bf16[1024,256]{1,0:T(8,128)(2,1)S(1)} %copy-done.1, bf16[1024,256]{1,0:T(8,128)(2,1)S(1)} %copy-done.3, bf16[1024,256]{1,0:T(8,128)(2,1)S(1)} %copy-done.5, bf16[1024,256]{1,0:T(8,128)(2,1)S(1)} %get-tuple-element.106.g_ref, ...), custom_call_target="tpu_custom_call" | custom-call | flops 1000000000 | bytes 4000000 | tf_op jit(solution)/shard_map/near_backward_0/pallas_call | solution.py:624
  110.2 3.6 %collective-permute-start.26 = (bf16[512,256]{1,0:T(8,128)(2,1)S(1)}, bf16[512,256]{1,0:T(8,128)(2,1)S(1)}, u32[]{:S(2)}, u32[]{:S(2)}) collective-permute-start(bf16[512,256]{1,0:T(8,128)(2,1)S(1)} %pad_maximum_fusion.6), channel_id=1, source_target_pairs={{0,8},{8,0},{16,24},{24,16},{32,40},{40,32},{48,56},{56,48},{64,72... | collective-permute-start | bytes 786440 | tf_op jit(solution)/shard_map/ppermute | solution.py:453
  117.4 1.6 %key_grad.1 = (bf16[1024,256]{1,0:T(8,128)(2,1)}, bf16[1024,256]{1,0:T(8,128)(2,1)}, f32[2,8,256]{2,1,0:T(8,128)}) custom-call(s32[2]{0:T(128)S(1)} %pad_add_fusion.idx, f32[2,1024,128]{2,1,0:T(8,128)S(1)} %get-tuple-element.122.dk_in, f32[2,1024,128]{2,1,0:T(8,128)S(1)} %get-tuple-element.123.dv_in, f32[96,128]{1,0:T(8,128)S(1)} %collective-permute-done.25.far_got, ...), custom_call_target="tpu_custom_call" | custom-call | flops 1000000 | bytes 4000000 | tf_op jit(solution)/shard_map/key_grad/pallas_call | solution.py:679
  119.1 2.1 %query_grad.1 = bf16[1024,256]{1,0:T(8,128)(2,1)} custom-call(s32[2]{0:T(128)S(1)} %pad_add_fusion.idx, f32[2,512,128]{2,1,0:T(8,128)S(1)} %get-tuple-element.111.dq0, f32[2,512,128]{2,1,0:T(8,128)S(1)} %get-tuple-element.112.dq1, bf16[1024,384]{1,0:T(8,128)(2,1)S(1)} %constant_dynamic-update-slice_fusion.mid_ref, ...), custom_call_target="tpu_custom_call" | custom-call | flops 200000000 | bytes 3000000 | tf_op jit(solution)/shard_map/query_grad/pallas_call | solution.py:668
  (79 shorter events, 24.1 us)
Async XLA Ops:
  0.7 1.0 copy-start
  4.7 10.8 %collective-permute-start = (bf16[256,384]{1,0:T(8,128)(2,1)S(1)}, bf16[256,384]{1,0:T(8,128)(2,1)S(1)}, u32[]{:S(2)}, u32[]{:S(2)}) collective-permute-start(bf16[256,384]{1,0:T(8,128)(2,1)S(1)} %get-tuple-element.66), channel_id=1, source_target_pairs={{0,16},{8,24},{16,0},{24,8},{32,48},{40,56},{48,32},{56,40},{64,80... | collective-permute-start | bytes 589832 | tf_op jit(solution)/shard_map/ppermute | solution.py:453
  8.8 6.7 %collective-permute-start.1 = (bf16[16,384]{1,0:T(8,128)(2,1)S(1)}, bf16[16,384]{1,0:T(8,128)(2,1)S(1)}, u32[]{:S(2)}, u32[]{:S(2)}) collective-permute-start(bf16[16,384]{1,0:T(8,128)(2,1)S(1)} %get-tuple-element.67), channel_id=1, source_target_pairs={{0,8},{16,24},{32,40},{48,56},{64,72},{80,88},{96,104},{112,120},{... | collective-permute-start | bytes 36872 | tf_op jit(solution)/shard_map/ppermute | solution.py:466
  15.5 8.4 %copy-start.6 = (bf16[1024,256]{1,0:T(8,128)(2,1)S(1)}, bf16[1024,256]{1,0:T(8,128)(2,1)}, u32[]{:S(2)}) copy-start(bf16[1024,256]{1,0:T(8,128)(2,1)} %g_ref.3) | copy-start | bytes 1572868
  15.5 7.1 %collective-permute-start.2 = (bf16[512,384]{1,0:T(8,128)(2,1)S(1)}, bf16[512,384]{1,0:T(8,128)(2,1)S(1)}, u32[]{:S(2)}, u32[]{:S(2)}) collective-permute-start(bf16[512,384]{1,0:T(8,128)(2,1)S(1)} %pad_maximum_fusion.3), channel_id=1, source_target_pairs={{0,8},{8,0},{16,24},{24,16},{32,40},{40,32},{48,56},{56,48},{64,72... | collective-permute-start | bytes 1179656 | tf_op jit(solution)/shard_map/ppermute | solution.py:453
  25.5 6.7 %collective-permute-start.4 = (f32[32,128]{1,0:T(8,128)S(1)}, f32[32,128]{1,0:T(8,128)S(1)}, u32[]{:S(2)}, u32[]{:S(2)}) collective-permute-start(f32[32,128]{1,0:T(8,128)S(1)} %slice.14), channel_id=1, source_target_pairs={{8,0},{24,16},{40,32},{56,48},{72,64},{88,80},{104,96},{120,112},{... | collective-permute-start | bytes 49160 | tf_op jit(solution)/shard_map/ppermute | solution.py:470
  27.8 8.4 %collective-permute-start.3 = (bf16[32,256]{1,0:T(8,128)(2,1)S(1)}, bf16[32,256]{1,0:T(8,128)(2,1)S(1)}, u32[]{:S(2)}, u32[]{:S(2)}) collective-permute-start(bf16[32,256]{1,0:T(8,128)(2,1)S(1)} %slice.13), channel_id=1, source_target_pairs={{8,264},{24,280},{40,296},{56,312},{72,328},{88,344},{104,360},{12... | collective-permute-start | bytes 49160 | tf_op jit(solution)/shard_map/ppermute | solution.py:457
  32.3 4.0 %collective-permute-start.5 = (f32[64,128]{1,0:T(8,128)S(1)}, f32[64,128]{1,0:T(8,128)S(1)}, u32[]{:S(2)}, u32[]{:S(2)}) collective-permute-start(f32[64,128]{1,0:T(8,128)S(1)} %pad_maximum_fusion.14), channel_id=1, source_target_pairs={{0,2},{1,3},{2,0},{3,1},{4,6},{5,7},{6,4},{7,5},{16,18},{17,19},{1... | collective-permute-start | bytes 98312 | tf_op jit(solution)/shard_map/ppermute | solution.py:462
  36.3 2.7 %collective-permute-start.7 = (f32[64,128]{1,0:T(8,128)S(1)}, f32[64,128]{1,0:T(8,128)S(1)}, u32[]{:S(2)}, u32[]{:S(2)}) collective-permute-start(f32[64,128]{1,0:T(8,128)S(1)} %fusion), channel_id=1, source_target_pairs={{0,1},{1,0},{2,3},{3,2},{4,5},{5,4},{6,7},{7,6},{16,17},{17,16},{1... | collective-permute-start | bytes 98312 | tf_op jit(solution)/shard_map/ppermute | solution.py:462
  36.9 5.6 %collective-permute-start.6 = (bf16[64,256]{1,0:T(8,128)(2,1)S(1)}, bf16[64,256]{1,0:T(8,128)(2,1)S(1)}, u32[]{:S(2)}, u32[]{:S(2)}) collective-permute-start(bf16[64,256]{1,0:T(8,128)(2,1)S(1)} %pad_maximum_fusion.13), channel_id=1, source_target_pairs={{8,136},{24,152},{40,168},{56,184},{72,200},{88,216},{104,232},{12... | collective-permute-start | bytes 98312 | tf_op jit(solution)/shard_map/ppermute | solution.py:457
  42.5 5.0 %collective-permute-start.8 = (bf16[128,256]{1,0:T(8,128)(2,1)S(1)}, bf16[128,256]{1,0:T(8,128)(2,1)S(1)}, u32[]{:S(2)}, u32[]{:S(2)}) collective-permute-start(bf16[128,256]{1,0:T(8,128)(2,1)S(1)} %pad_maximum_fusion.10), channel_id=1, source_target_pairs={{8,72},{24,88},{40,104},{56,120},{72,8},{88,24},{104,40},{120,56},... | collective-permute-start | bytes 196616 | tf_op jit(solution)/shard_map/ppermute | solution.py:457
  47.5 7.2 %collective-permute-start.9 = (bf16[256,256]{1,0:T(8,128)(2,1)S(1)}, bf16[256,256]{1,0:T(8,128)(2,1)S(1)}, u32[]{:S(2)}, u32[]{:S(2)}) collective-permute-start(bf16[256,256]{1,0:T(8,128)(2,1)S(1)} %pad_maximum_fusion.8), channel_id=1, source_target_pairs={{8,40},{24,56},{40,8},{56,24},{72,104},{88,120},{104,72},{120,88},... | collective-permute-start | bytes 393224 | tf_op jit(solution)/shard_map/ppermute | solution.py:457
  54.7 7.1 %collective-permute-start.10 = (bf16[512,256]{1,0:T(8,128)(2,1)S(1)}, bf16[512,256]{1,0:T(8,128)(2,1)S(1)}, u32[]{:S(2)}, u32[]{:S(2)}) collective-permute-start(bf16[512,256]{1,0:T(8,128)(2,1)S(1)} %pad_maximum_fusion.5), channel_id=1, source_target_pairs={{8,24},{24,8},{40,56},{56,40},{72,88},{88,72},{104,120},{120,104},... | collective-permute-start | bytes 786440 | tf_op jit(solution)/shard_map/ppermute | solution.py:457
  57.8 0.7 collective-permute-start.11
  58.5 3.4 %collective-permute-start.12 = (f32[112,128]{1,0:T(8,128)S(1)}, f32[112,128]{1,0:T(8,128)S(1)}, u32[]{:S(2)}, u32[]{:S(2)}) collective-permute-start(f32[112,128]{1,0:T(8,128)S(1)} %pad_maximum_fusion.11), channel_id=1, source_target_pairs={{0,8},{16,24},{32,40},{48,56},{64,72},{80,88},{96,104},{112,120},{... | collective-permute-start | bytes 172040 | tf_op jit(solution)/shard_map/ppermute | solution.py:466
  63.1 9.0 %collective-permute-start.13 = (bf16[64,384]{1,0:T(8,128)(2,1)S(1)}, bf16[64,384]{1,0:T(8,128)(2,1)S(1)}, u32[]{:S(2)}, u32[]{:S(2)}) collective-permute-start(bf16[64,384]{1,0:T(8,128)(2,1)S(1)} %get-tuple-element.89.packs_own), channel_id=1, source_target_pairs={{8,0},{24,16},{40,32},{56,48},{72,64},{88,80},{104,96},{120,112},{... | collective-permute-start | bytes 147464 | tf_op jit(solution)/shard_map/ppermute | solution.py:470
  64.9 26.7 %collective-permute-start.20 = (bf16[1024,256]{1,0:T(8,128)(2,1)S(1)}, bf16[1024,256]{1,0:T(8,128)(2,1)S(1)}, u32[]{:S(2)}, u32[]{:S(2)}) collective-permute-start(bf16[1024,256]{1,0:T(8,128)(2,1)S(1)} %pad_maximum_fusion.1.far_all), channel_id=1, source_target_pairs={{8,0},{24,16},{40,32},{56,48},{72,64},{88,80},{104,96},{120,112},{... | collective-permute-start | bytes 1572872 | tf_op jit(solution)/shard_map/ppermute | solution.py:470
  66.2 5.9 %collective-permute-start.14 = (f32[8,128]{1,0:T(8,128)S(1)}, f32[8,128]{1,0:T(8,128)S(1)}, u32[]{:S(2)}, u32[]{:S(2)}) collective-permute-start(f32[8,128]{1,0:T(8,128)S(1)} %get-tuple-element.90), channel_id=1, source_target_pairs={{8,10},{9,11},{10,8},{11,9},{12,14},{13,15},{14,12},{15,13},{24,26... | collective-permute-start | bytes 12296 | tf_op jit(solution)/shard_map/ppermute | solution.py:462
  72.1 5.0 %collective-permute-start.15 = (bf16[32,384]{1,0:T(8,128)(2,1)S(1)}, bf16[32,384]{1,0:T(8,128)(2,1)S(1)}, u32[]{:S(2)}, u32[]{:S(2)}) collective-permute-start(bf16[32,384]{1,0:T(8,128)(2,1)S(1)} %slice.17), channel_id=1, source_target_pairs={{0,256},{16,272},{32,288},{48,304},{64,320},{80,336},{96,352},{112... | collective-permute-start | bytes 73736 | tf_op jit(solution)/shard_map/ppermute | solution.py:457
  72.8 4.4 %collective-permute-start.16 = (f32[8,128]{1,0:T(8,128)S(1)}, f32[8,128]{1,0:T(8,128)S(1)}, u32[]{:S(2)}, u32[]{:S(2)}) collective-permute-start(f32[8,128]{1,0:T(8,128)S(1)} %add.21), channel_id=1, source_target_pairs={{8,9},{9,8},{10,11},{11,10},{12,13},{13,12},{14,15},{15,14},{24,25... | collective-permute-start | bytes 12296 | tf_op jit(solution)/shard_map/ppermute | solution.py:462
  77.1 13.7 %collective-permute-start.17 = (bf16[64,384]{1,0:T(8,128)(2,1)S(1)}, bf16[64,384]{1,0:T(8,128)(2,1)S(1)}, u32[]{:S(2)}, u32[]{:S(2)}) collective-permute-start(bf16[64,384]{1,0:T(8,128)(2,1)S(1)} %pad_maximum_fusion.12), channel_id=1, source_target_pairs={{0,128},{16,144},{32,160},{48,176},{64,192},{80,208},{96,224},{112... | collective-permute-start | bytes 147464 | tf_op jit(solution)/shard_map/ppermute | solution.py:457
  77.8 13.1 %collective-permute-start.18 = (f32[8,128]{1,0:T(8,128)S(1)}, f32[8,128]{1,0:T(8,128)S(1)}, u32[]{:S(2)}, u32[]{:S(2)}) collective-permute-start(f32[8,128]{1,0:T(8,128)S(1)} %add.22), channel_id=1, source_target_pairs={{8,12},{9,13},{10,14},{11,15},{12,8},{13,9},{14,10},{15,11},{24,28... | collective-permute-start | bytes 12296 | tf_op jit(solution)/shard_map/ppermute | solution.py:462
  90.9 0.7 collective-permute-start.19
  92.2 9.2 %collective-permute-start.23 = (bf16[256,384]{1,0:T(8,128)(2,1)S(1)}, bf16[256,384]{1,0:T(8,128)(2,1)S(1)}, u32[]{:S(2)}, u32[]{:S(2)}) collective-permute-start(bf16[256,384]{1,0:T(8,128)(2,1)S(1)} %pad_maximum_fusion.7), channel_id=1, source_target_pairs={{0,32},{16,48},{32,0},{48,16},{64,96},{80,112},{96,64},{112,80},{1... | collective-permute-start | bytes 589832 | tf_op jit(solution)/shard_map/ppermute | solution.py:457
  92.9 3.1 %collective-permute-start.21 = (f32[8,128]{1,0:T(8,128)S(1)}, f32[8,128]{1,0:T(8,128)S(1)}, u32[]{:S(2)}, u32[]{:S(2)}) collective-permute-start(f32[8,128]{1,0:T(8,128)S(1)} %add.23.fix_own), channel_id=1, source_target_pairs={{8,0},{24,16},{40,32},{56,48},{72,64},{88,80},{104,96},{120,112},{... | collective-permute-start | bytes 12296 | tf_op jit(solution)/shard_map/ppermute | solution.py:470
  96.0 9.8 %copy-start.5 = (bf16[1024,256]{1,0:T(8,128)(2,1)S(1)}, bf16[1024,256]{1,0:T(8,128)(2,1)}, u32[]{:S(2)}) copy-start(bf16[1024,256]{1,0:T(8,128)(2,1)} %v_ref.9) | copy-start | bytes 1572868
  99.0 6.8 %copy-start.1 = (bf16[1024,256]{1,0:T(8,128)(2,1)S(1)}, bf16[1024,256]{1,0:T(8,128)(2,1)}, u32[]{:S(2)}) copy-start(bf16[1024,256]{1,0:T(8,128)(2,1)} %q_ref.9) | copy-start | bytes 1572868
  99.0 6.8 %copy-start.3 = (bf16[1024,256]{1,0:T(8,128)(2,1)S(1)}, bf16[1024,256]{1,0:T(8,128)(2,1)}, u32[]{:S(2)}) copy-start(bf16[1024,256]{1,0:T(8,128)(2,1)} %k_ref.9) | copy-start | bytes 1572868
  99.0 6.8 %collective-permute-start.22 = (bf16[256,256]{1,0:T(8,128)(2,1)S(1)}, bf16[256,256]{1,0:T(8,128)(2,1)S(1)}, u32[]{:S(2)}, u32[]{:S(2)}) collective-permute-start(bf16[256,256]{1,0:T(8,128)(2,1)S(1)} %get-tuple-element.102.mid_g), channel_id=1, source_target_pairs={{0,16},{8,24},{16,0},{24,8},{32,48},{40,56},{48,32},{56,40},{64,80... | collective-permute-start | bytes 393224 | tf_op jit(solution)/shard_map/ppermute | solution.py:453
  101.5 8.6 %collective-permute-start.24 = (bf16[512,384]{1,0:T(8,128)(2,1)S(1)}, bf16[512,384]{1,0:T(8,128)(2,1)S(1)}, u32[]{:S(2)}, u32[]{:S(2)}) collective-permute-start(bf16[512,384]{1,0:T(8,128)(2,1)S(1)} %pad_maximum_fusion.4), channel_id=1, source_target_pairs={{0,16},{16,0},{32,48},{48,32},{64,80},{80,64},{96,112},{112,96},{1... | collective-permute-start | bytes 1179656 | tf_op jit(solution)/shard_map/ppermute | solution.py:457
  110.2 5.4 %collective-permute-start.26 = (bf16[512,256]{1,0:T(8,128)(2,1)S(1)}, bf16[512,256]{1,0:T(8,128)(2,1)S(1)}, u32[]{:S(2)}, u32[]{:S(2)}) collective-permute-start(bf16[512,256]{1,0:T(8,128)(2,1)S(1)} %pad_maximum_fusion.6), channel_id=1, source_target_pairs={{0,8},{8,0},{16,24},{24,16},{32,40},{40,32},{48,56},{56,48},{64,72... | collective-permute-start | bytes 786440 | tf_op jit(solution)/shard_map/ppermute | solution.py:453
  114.3 3.1 %collective-permute-start.25 = (f32[96,128]{1,0:T(8,128)S(1)}, f32[96,128]{1,0:T(8,128)S(1)}, u32[]{:S(2)}, u32[]{:S(2)}) collective-permute-start(f32[96,128]{1,0:T(8,128)S(1)} %far_key.1.far_own), channel_id=1, source_target_pairs={{0,8},{16,24},{32,40},{48,56},{64,72},{80,88},{96,104},{112,120},{... | collective-permute-start | bytes 147464 | tf_op jit(solution)/shard_map/ppermute | solution.py:466
  (2 other events, 2.1 us)

commit v6 on v5

--- a/solution.py
+++ b/solution.py
@@ -597,7 +597,8 @@
     )(idx, far_even, packs_even)
     part_b, fix = after((joined(part_a, part2), fix + fix3))
     part3 = chip_exchange(part_b, 8, 0)
-    part_c, far_dq = after((joined(part_b, part3), far_dq))
+    part_b, far_dq = after((part_b, far_dq))
+    part_c = joined(part_b, part3)
     part4 = chip_exchange(part_c, 4, 0)
     part_c, fix_sent = after((part_c, fix))
     fix_even = to_even(fix_sent)

time: 122 us -> 122 us (level)
    unnamed x15 -> x16, local copies, waits for them, and re-layouts: 3.18 us -> 3.19 us
  transfers between devices with their start and end apart: 27 -> 27, of which waited for: 13 -> 13; matrix products, arithmetic and copies ran while one was open for 0% -> 0% of each run, Pallas kernels for 10% -> 12%
where the time goes in v6:
time: 122 us; the launch traced here: 121 us
  starting transfers between devices  63 us (52%)
  waiting for transfers between devices  31.6 us (26%)
  Pallas kernels  21.8 us (18%)
  local copies, waits for them, and re-layouts  3.29 us (3%)
    ppermute x6, starting transfers between devices, head_exchange(): return lax.ppermute(x, ('seq', 'head'), pairs)  18.1 us
    ppermute x10, starting transfers between devices, chip_exchange(): return lax.ppermute(x, 'seq', [(i, i ^ bit) for i in range(parity, 64, 2)])  17.5 us
    ppermute x10, waiting for transfers between devices, chip_exchange(): return lax.ppermute(x, 'seq', [(i, i ^ bit) for i in range(parity, 64, 2)])  16.4 us
    ppermute x4, starting transfers between devices, exchange(): return lax.ppermute(x, 'seq', [(i, i ^ bit) for i in range(64)])  15.7 us
    ppermute x4, starting transfers between devices, to_even(): return lax.ppermute(x, 'seq', [(i + 1, i) for i in range(0, 64, 2)])  7.73 us
    ppermute x6, waiting for transfers between devices, head_exchange(): return lax.ppermute(x, ('seq', 'head'), pairs)  7.22 us
    ppermute x4, waiting for transfers between devices, exchange(): return lax.ppermute(x, 'seq', [(i, i ^ bit) for i in range(64)])  4.87 us
    pallas_call x2, Pallas kernels, near_backward(): pl.pallas_call(near_backward_kernel, grid=(2,), out_shape=(half_shape,) *...  4.27 us
  transfers between devices with their start and end apart: 27, of which 13 were waited for; matrix products, arithmetic and copies ran while one was open for 0% of the time, Pallas kernels for 12%

profile of v6, /device:TPU:1, one launch (start us, length us, event | category | flops | bytes accessed | tf_op | source)
XLA Modules:
  0.0 121.3 jit_solution(8868320470943517447)
XLA Ops:
  4.7 4.0 %collective-permute-start = (bf16[256,384]{1,0:T(8,128)(2,1)S(1)}, bf16[256,384]{1,0:T(8,128)(2,1)S(1)}, u32[]{:S(2)}, u32[]{:S(2)}) collective-permute-start(bf16[256,384]{1,0:T(8,128)(2,1)S(1)} %get-tuple-element.66), channel_id=1, source_target_pairs={{0,16},{8,24},{16,0},{24,8},{32,48},{40,56},{48,32},{56,40},{64,80... | collective-permute-start | bytes 589832 | tf_op jit(solution)/shard_map/ppermute | solution.py:453
  10.1 1.7 %near_forward_0.1 = (f32[2,512,128]{2,1,0:T(8,128)S(1)}, f32[2,512,128]{2,1,0:T(8,128)S(1)}) custom-call(bf16[1024,256]{1,0:T(8,128)(2,1)S(1)} %copy-done, bf16[1024,256]{1,0:T(8,128)(2,1)S(1)} %copy-done.2, bf16[1024,256]{1,0:T(8,128)(2,1)S(1)} %copy-done.4), custom_call_target="tpu_custom_call" | custom-call | flops 400000000 | bytes 2000000 | tf_op jit(solution)/shard_map/near_forward_0/pallas_call | solution.py:509
  11.8 1.7 %near_forward_1.1 = (f32[2,512,128]{2,1,0:T(8,128)S(1)}, f32[2,512,128]{2,1,0:T(8,128)S(1)}) custom-call(bf16[1024,256]{1,0:T(8,128)(2,1)S(1)} %copy-done, bf16[1024,256]{1,0:T(8,128)(2,1)S(1)} %copy-done.2, bf16[1024,256]{1,0:T(8,128)(2,1)S(1)} %copy-done.4), custom_call_target="tpu_custom_call" | custom-call | flops 400000000 | bytes 2000000 | tf_op jit(solution)/shard_map/near_forward_1/pallas_call | solution.py:509
  13.5 2.0 %collective-permute-done.1 = bf16[16,384]{1,0:T(8,128)(2,1)S(1)} collective-permute-done((bf16[16,384]{1,0:T(8,128)(2,1)S(1)}, bf16[16,384]{1,0:T(8,128)(2,1)S(1)}, u32[]{:S(2)}, u32[]{:S(2)}) %collective-permute-start.1) | collective-permute-done | bytes 12320 | tf_op jit(solution)/shard_map/ppermute | solution.py:466
  15.5 5.7 %collective-permute-start.2 = (bf16[512,384]{1,0:T(8,128)(2,1)S(1)}, bf16[512,384]{1,0:T(8,128)(2,1)S(1)}, u32[]{:S(2)}, u32[]{:S(2)}) collective-permute-start(bf16[512,384]{1,0:T(8,128)(2,1)S(1)} %pad_maximum_fusion.3), channel_id=1, source_target_pairs={{0,8},{8,0},{16,24},{24,16},{32,40},{40,32},{48,56},{56,48},{64,72... | collective-permute-start | bytes 1179656 | tf_op jit(solution)/shard_map/ppermute | solution.py:453
  25.5 2.3 %collective-permute-start.4 = (f32[32,128]{1,0:T(8,128)S(1)}, f32[32,128]{1,0:T(8,128)S(1)}, u32[]{:S(2)}, u32[]{:S(2)}) collective-permute-start(f32[32,128]{1,0:T(8,128)S(1)} %slice.14), channel_id=1, source_target_pairs={{8,0},{24,16},{40,32},{56,48},{72,64},{88,80},{104,96},{120,112},{... | collective-permute-start | bytes 49160 | tf_op jit(solution)/shard_map/ppermute | solution.py:470
  27.8 4.4 %collective-permute-start.3 = (bf16[32,256]{1,0:T(8,128)(2,1)S(1)}, bf16[32,256]{1,0:T(8,128)(2,1)S(1)}, u32[]{:S(2)}, u32[]{:S(2)}) collective-permute-start(bf16[32,256]{1,0:T(8,128)(2,1)S(1)} %slice.13), channel_id=1, source_target_pairs={{8,264},{24,280},{40,296},{56,312},{72,328},{88,344},{104,360},{12... | collective-permute-start | bytes 49160 | tf_op jit(solution)/shard_map/ppermute | solution.py:457
  32.9 3.3 %collective-permute-done.3 = bf16[32,256]{1,0:T(8,128)(2,1)S(1)} collective-permute-done((bf16[32,256]{1,0:T(8,128)(2,1)S(1)}, bf16[32,256]{1,0:T(8,128)(2,1)S(1)}, u32[]{:S(2)}, u32[]{:S(2)}) %collective-permute-start.3) | collective-permute-done | bytes 16416 | tf_op jit(solution)/shard_map/ppermute | solution.py:457
  36.9 2.0 %collective-permute-start.6 = (bf16[64,256]{1,0:T(8,128)(2,1)S(1)}, bf16[64,256]{1,0:T(8,128)(2,1)S(1)}, u32[]{:S(2)}, u32[]{:S(2)}) collective-permute-start(bf16[64,256]{1,0:T(8,128)(2,1)S(1)} %pad_maximum_fusion.12), channel_id=1, source_target_pairs={{8,136},{24,152},{40,168},{56,184},{72,200},{88,216},{104,232},{12... | collective-permute-start | bytes 98312 | tf_op jit(solution)/shard_map/ppermute | solution.py:457
  39.0 3.5 %collective-permute-done.6 = bf16[64,256]{1,0:T(8,128)(2,1)S(1)} collective-permute-done((bf16[64,256]{1,0:T(8,128)(2,1)S(1)}, bf16[64,256]{1,0:T(8,128)(2,1)S(1)}, u32[]{:S(2)}, u32[]{:S(2)}) %collective-permute-start.6) | collective-permute-done | bytes 32800 | tf_op jit(solution)/shard_map/ppermute | solution.py:457
  42.5 1.9 %collective-permute-start.8 = (bf16[128,256]{1,0:T(8,128)(2,1)S(1)}, bf16[128,256]{1,0:T(8,128)(2,1)S(1)}, u32[]{:S(2)}, u32[]{:S(2)}) collective-permute-start(bf16[128,256]{1,0:T(8,128)(2,1)S(1)} %pad_maximum_fusion.9), channel_id=1, source_target_pairs={{8,72},{24,88},{40,104},{56,120},{72,8},{88,24},{104,40},{120,56},... | collective-permute-start | bytes 196616 | tf_op jit(solution)/shard_map/ppermute | solution.py:457
  44.4 3.1 %collective-permute-done.8 = bf16[128,256]{1,0:T(8,128)(2,1)S(1)} collective-permute-done((bf16[128,256]{1,0:T(8,128)(2,1)S(1)}, bf16[128,256]{1,0:T(8,128)(2,1)S(1)}, u32[]{:S(2)}, u32[]{:S(2)}) %collective-permute-start.8) | collective-permute-done | bytes 65568 | tf_op jit(solution)/shard_map/ppermute | solution.py:457
  47.5 2.8 %collective-permute-start.9 = (bf16[256,256]{1,0:T(8,128)(2,1)S(1)}, bf16[256,256]{1,0:T(8,128)(2,1)S(1)}, u32[]{:S(2)}, u32[]{:S(2)}) collective-permute-start(bf16[256,256]{1,0:T(8,128)(2,1)S(1)} %pad_maximum_fusion.7), channel_id=1, source_target_pairs={{8,40},{24,56},{40,8},{56,24},{72,104},{88,120},{104,72},{120,88},... | collective-permute-start | bytes 393224 | tf_op jit(solution)/shard_map/ppermute | solution.py:457
  50.3 4.4 %collective-permute-done.9 = bf16[256,256]{1,0:T(8,128)(2,1)S(1)} collective-permute-done((bf16[256,256]{1,0:T(8,128)(2,1)S(1)}, bf16[256,256]{1,0:T(8,128)(2,1)S(1)}, u32[]{:S(2)}, u32[]{:S(2)}) %collective-permute-start.9) | collective-permute-done | bytes 131104 | tf_op jit(solution)/shard_map/ppermute | solution.py:457
  54.7 3.1 %collective-permute-start.10 = (bf16[512,256]{1,0:T(8,128)(2,1)S(1)}, bf16[512,256]{1,0:T(8,128)(2,1)S(1)}, u32[]{:S(2)}, u32[]{:S(2)}) collective-permute-start(bf16[512,256]{1,0:T(8,128)(2,1)S(1)} %pad_maximum_fusion.5), channel_id=1, source_target_pairs={{8,24},{24,8},{40,56},{56,40},{72,88},{88,72},{104,120},{120,104},... | collective-permute-start | bytes 786440 | tf_op jit(solution)/shard_map/ppermute | solution.py:457
  59.8 2.0 %collective-permute-done.10 = bf16[512,256]{1,0:T(8,128)(2,1)S(1)} collective-permute-done((bf16[512,256]{1,0:T(8,128)(2,1)S(1)}, bf16[512,256]{1,0:T(8,128)(2,1)S(1)}, u32[]{:S(2)}, u32[]{:S(2)}) %collective-permute-start.10) | collective-permute-done | bytes 262176 | tf_op jit(solution)/shard_map/ppermute | solution.py:457
  61.9 1.8 %collective-permute-start.19 = (bf16[1024,256]{1,0:T(8,128)(2,1)S(1)}, bf16[1024,256]{1,0:T(8,128)(2,1)S(1)}, u32[]{:S(2)}, u32[]{:S(2)}) collective-permute-start(bf16[1024,256]{1,0:T(8,128)(2,1)S(1)} %pad_maximum_fusion.1.far_all), channel_id=1, source_target_pairs={{8,0},{24,16},{40,32},{56,48},{72,64},{88,80},{104,96},{120,112},{... | collective-permute-start | bytes 1572872 | tf_op jit(solution)/shard_map/ppermute | solution.py:470
  66.2 2.8 %collective-permute-start.14 = (f32[8,128]{1,0:T(8,128)S(1)}, f32[8,128]{1,0:T(8,128)S(1)}, u32[]{:S(2)}, u32[]{:S(2)}) collective-permute-start(f32[8,128]{1,0:T(8,128)S(1)} %get-tuple-element.90), channel_id=1, source_target_pairs={{8,10},{9,11},{10,8},{11,9},{12,14},{13,15},{14,12},{15,13},{24,26... | collective-permute-start | bytes 12296 | tf_op jit(solution)/shard_map/ppermute | solution.py:462
  69.0 3.1 %collective-permute-done.14 = f32[8,128]{1,0:T(8,128)S(1)} collective-permute-done((f32[8,128]{1,0:T(8,128)S(1)}, f32[8,128]{1,0:T(8,128)S(1)}, u32[]{:S(2)}, u32[]{:S(2)}) %collective-permute-start.14) | collective-permute-done | bytes 4128 | tf_op jit(solution)/shard_map/ppermute | solution.py:462
  72.8 1.9 %collective-permute-start.16 = (f32[8,128]{1,0:T(8,128)S(1)}, f32[8,128]{1,0:T(8,128)S(1)}, u32[]{:S(2)}, u32[]{:S(2)}) collective-permute-start(f32[8,128]{1,0:T(8,128)S(1)} %add.21), channel_id=1, source_target_pairs={{8,9},{9,8},{10,11},{11,10},{12,13},{13,12},{14,15},{15,14},{24,25... | collective-permute-start | bytes 12296 | tf_op jit(solution)/shard_map/ppermute | solution.py:462
  74.7 2.4 %collective-permute-done.16 = f32[8,128]{1,0:T(8,128)S(1)} collective-permute-done((f32[8,128]{1,0:T(8,128)S(1)}, f32[8,128]{1,0:T(8,128)S(1)}, u32[]{:S(2)}, u32[]{:S(2)}) %collective-permute-start.16) | collective-permute-done | bytes 4128 | tf_op jit(solution)/shard_map/ppermute | solution.py:462
  77.8 11.5 %collective-permute-start.18 = (f32[8,128]{1,0:T(8,128)S(1)}, f32[8,128]{1,0:T(8,128)S(1)}, u32[]{:S(2)}, u32[]{:S(2)}) collective-permute-start(f32[8,128]{1,0:T(8,128)S(1)} %add.22), channel_id=1, source_target_pairs={{8,12},{9,13},{10,14},{11,15},{12,8},{13,9},{14,10},{15,11},{24,28... | collective-permute-start | bytes 12296 | tf_op jit(solution)/shard_map/ppermute | solution.py:462
  89.3 1.7 %collective-permute-done.18 = f32[8,128]{1,0:T(8,128)S(1)} collective-permute-done((f32[8,128]{1,0:T(8,128)S(1)}, f32[8,128]{1,0:T(8,128)S(1)}, u32[]{:S(2)}, u32[]{:S(2)}) %collective-permute-start.18) | collective-permute-done | bytes 4128 | tf_op jit(solution)/shard_map/ppermute | solution.py:462
  93.0 2.3 %collective-permute-start.21 = (f32[8,128]{1,0:T(8,128)S(1)}, f32[8,128]{1,0:T(8,128)S(1)}, u32[]{:S(2)}, u32[]{:S(2)}) collective-permute-start(f32[8,128]{1,0:T(8,128)S(1)} %add.23.fix_own), channel_id=1, source_target_pairs={{8,0},{24,16},{40,32},{56,48},{72,64},{88,80},{104,96},{120,112},{... | collective-permute-start | bytes 12296 | tf_op jit(solution)/shard_map/ppermute | solution.py:470
  96.1 3.0 %norm.1 = (bf16[1024,256]{1,0:T(8,128)(2,1)}, bf16[1024,256]{1,0:T(8,128)(2,1)S(1)}, f32[2,1024,128]{2,1,0:T(8,128)S(1)}, f32[2,1024,128]{2,1,0:T(8,128)S(1)}, bf16[256,256]{1,0:T(8,128)(2,1)S(1)}) custom-call(s32[2]{0:T(128)S(1)} %pad_add_fusion.idx, f32[112,128]{1,0:T(8,128)S(1)} %collective-permute-done.12.mate_ref, f32[64,128]{1,0:T(8,128)S(1)} %add.20.stat_ref, ...), custom_call_target="tpu_custom_call" | custom-call | flops 10000000 | bytes 4000000 | tf_op jit(solution)/shard_map/norm/pallas_call | solution.py:605
  99.2 2.4 %collective-permute-start.22 = (bf16[256,256]{1,0:T(8,128)(2,1)S(1)}, bf16[256,256]{1,0:T(8,128)(2,1)S(1)}, u32[]{:S(2)}, u32[]{:S(2)}) collective-permute-start(bf16[256,256]{1,0:T(8,128)(2,1)S(1)} %get-tuple-element.102.mid_g), channel_id=1, source_target_pairs={{0,16},{8,24},{16,0},{24,8},{32,48},{40,56},{48,32},{56,40},{64,80... | collective-permute-start | bytes 393224 | tf_op jit(solution)/shard_map/ppermute | solution.py:453
  102.3 3.6 %collective-permute-done.22 = bf16[256,256]{1,0:T(8,128)(2,1)S(1)} collective-permute-done((bf16[256,256]{1,0:T(8,128)(2,1)S(1)}, bf16[256,256]{1,0:T(8,128)(2,1)S(1)}, u32[]{:S(2)}, u32[]{:S(2)}) %collective-permute-start.22) | collective-permute-done | bytes 131104 | tf_op jit(solution)/shard_map/ppermute | solution.py:453
  106.0 2.1 %near_backward_1.1 = (f32[2,512,128]{2,1,0:T(8,128)S(1)}, f32[2,512,128]{2,1,0:T(8,128)S(1)}, f32[2,512,128]{2,1,0:T(8,128)S(1)}) custom-call(bf16[1024,256]{1,0:T(8,128)(2,1)S(1)} %copy-done.1, bf16[1024,256]{1,0:T(8,128)(2,1)S(1)} %copy-done.3, bf16[1024,256]{1,0:T(8,128)(2,1)S(1)} %copy-done.5, bf16[1024,256]{1,0:T(8,128)(2,1)S(1)} %get-tuple-element.106.g_ref, ...), custom_call_target="tpu_custom_call" | custom-call | flops 1000000000 | bytes 4000000 | tf_op jit(solution)/shard_map/near_backward_1/pallas_call | solution.py:625
  108.1 2.1 %near_backward_0.1 = (f32[2,512,128]{2,1,0:T(8,128)S(1)}, f32[2,512,128]{2,1,0:T(8,128)S(1)}, f32[2,512,128]{2,1,0:T(8,128)S(1)}) custom-call(bf16[1024,256]{1,0:T(8,128)(2,1)S(1)} %copy-done.1, bf16[1024,256]{1,0:T(8,128)(2,1)S(1)} %copy-done.3, bf16[1024,256]{1,0:T(8,128)(2,1)S(1)} %copy-done.5, bf16[1024,256]{1,0:T(8,128)(2,1)S(1)} %get-tuple-element.106.g_ref, ...), custom_call_target="tpu_custom_call" | custom-call | flops 1000000000 | bytes 4000000 | tf_op jit(solution)/shard_map/near_backward_0/pallas_call | solution.py:625
  110.3 3.6 %collective-permute-start.26 = (bf16[512,256]{1,0:T(8,128)(2,1)S(1)}, bf16[512,256]{1,0:T(8,128)(2,1)S(1)}, u32[]{:S(2)}, u32[]{:S(2)}) collective-permute-start(bf16[512,256]{1,0:T(8,128)(2,1)S(1)} %pad_maximum_fusion.6), channel_id=1, source_target_pairs={{0,8},{8,0},{16,24},{24,16},{32,40},{40,32},{48,56},{56,48},{64,72... | collective-permute-start | bytes 786440 | tf_op jit(solution)/shard_map/ppermute | solution.py:453
  117.6 1.6 %key_grad.1 = (bf16[1024,256]{1,0:T(8,128)(2,1)}, bf16[1024,256]{1,0:T(8,128)(2,1)}, f32[2,8,256]{2,1,0:T(8,128)}) custom-call(s32[2]{0:T(128)S(1)} %pad_add_fusion.idx, f32[2,1024,128]{2,1,0:T(8,128)S(1)} %get-tuple-element.122.dk_in, f32[2,1024,128]{2,1,0:T(8,128)S(1)} %get-tuple-element.123.dv_in, f32[96,128]{1,0:T(8,128)S(1)} %collective-permute-done.25.far_got, ...), custom_call_target="tpu_custom_call" | custom-call | flops 1000000 | bytes 4000000 | tf_op jit(solution)/shard_map/key_grad/pallas_call | solution.py:680
  119.2 2.1 %query_grad.1 = bf16[1024,256]{1,0:T(8,128)(2,1)} custom-call(s32[2]{0:T(128)S(1)} %pad_add_fusion.idx, f32[2,512,128]{2,1,0:T(8,128)S(1)} %get-tuple-element.111.dq0, f32[2,512,128]{2,1,0:T(8,128)S(1)} %get-tuple-element.112.dq1, bf16[1024,384]{1,0:T(8,128)(2,1)S(1)} %constant_dynamic-update-slice_fusion.mid_ref, ...), custom_call_target="tpu_custom_call" | custom-call | flops 200000000 | bytes 3000000 | tf_op jit(solution)/shard_map/query_grad/pallas_call | solution.py:669
  (80 shorter events, 24.1 us)
Async XLA Ops:
  0.7 1.0 copy-start
  4.7 10.8 %collective-permute-start = (bf16[256,384]{1,0:T(8,128)(2,1)S(1)}, bf16[256,384]{1,0:T(8,128)(2,1)S(1)}, u32[]{:S(2)}, u32[]{:S(2)}) collective-permute-start(bf16[256,384]{1,0:T(8,128)(2,1)S(1)} %get-tuple-element.66), channel_id=1, source_target_pairs={{0,16},{8,24},{16,0},{24,8},{32,48},{40,56},{48,32},{56,40},{64,80... | collective-permute-start | bytes 589832 | tf_op jit(solution)/shard_map/ppermute | solution.py:453
  8.8 6.7 %collective-permute-start.1 = (bf16[16,384]{1,0:T(8,128)(2,1)S(1)}, bf16[16,384]{1,0:T(8,128)(2,1)S(1)}, u32[]{:S(2)}, u32[]{:S(2)}) collective-permute-start(bf16[16,384]{1,0:T(8,128)(2,1)S(1)} %get-tuple-element.67), channel_id=1, source_target_pairs={{0,8},{16,24},{32,40},{48,56},{64,72},{80,88},{96,104},{112,120},{... | collective-permute-start | bytes 36872 | tf_op jit(solution)/shard_map/ppermute | solution.py:466
  15.5 8.4 %copy-start.6 = (bf16[1024,256]{1,0:T(8,128)(2,1)S(1)}, bf16[1024,256]{1,0:T(8,128)(2,1)}, u32[]{:S(2)}) copy-start(bf16[1024,256]{1,0:T(8,128)(2,1)} %g_ref.3) | copy-start | bytes 1572868
  15.5 7.1 %collective-permute-start.2 = (bf16[512,384]{1,0:T(8,128)(2,1)S(1)}, bf16[512,384]{1,0:T(8,128)(2,1)S(1)}, u32[]{:S(2)}, u32[]{:S(2)}) collective-permute-start(bf16[512,384]{1,0:T(8,128)(2,1)S(1)} %pad_maximum_fusion.3), channel_id=1, source_target_pairs={{0,8},{8,0},{16,24},{24,16},{32,40},{40,32},{48,56},{56,48},{64,72... | collective-permute-start | bytes 1179656 | tf_op jit(solution)/shard_map/ppermute | solution.py:453
  25.5 6.7 %collective-permute-start.4 = (f32[32,128]{1,0:T(8,128)S(1)}, f32[32,128]{1,0:T(8,128)S(1)}, u32[]{:S(2)}, u32[]{:S(2)}) collective-permute-start(f32[32,128]{1,0:T(8,128)S(1)} %slice.14), channel_id=1, source_target_pairs={{8,0},{24,16},{40,32},{56,48},{72,64},{88,80},{104,96},{120,112},{... | collective-permute-start | bytes 49160 | tf_op jit(solution)/shard_map/ppermute | solution.py:470
  27.8 8.4 %collective-permute-start.3 = (bf16[32,256]{1,0:T(8,128)(2,1)S(1)}, bf16[32,256]{1,0:T(8,128)(2,1)S(1)}, u32[]{:S(2)}, u32[]{:S(2)}) collective-permute-start(bf16[32,256]{1,0:T(8,128)(2,1)S(1)} %slice.13), channel_id=1, source_target_pairs={{8,264},{24,280},{40,296},{56,312},{72,328},{88,344},{104,360},{12... | collective-permute-start | bytes 49160 | tf_op jit(solution)/shard_map/ppermute | solution.py:457
  32.3 4.0 %collective-permute-start.5 = (f32[64,128]{1,0:T(8,128)S(1)}, f32[64,128]{1,0:T(8,128)S(1)}, u32[]{:S(2)}, u32[]{:S(2)}) collective-permute-start(f32[64,128]{1,0:T(8,128)S(1)} %pad_maximum_fusion.13), channel_id=1, source_target_pairs={{0,2},{1,3},{2,0},{3,1},{4,6},{5,7},{6,4},{7,5},{16,18},{17,19},{1... | collective-permute-start | bytes 98312 | tf_op jit(solution)/shard_map/ppermute | solution.py:462
  36.3 2.7 %collective-permute-start.7 = (f32[64,128]{1,0:T(8,128)S(1)}, f32[64,128]{1,0:T(8,128)S(1)}, u32[]{:S(2)}, u32[]{:S(2)}) collective-permute-start(f32[64,128]{1,0:T(8,128)S(1)} %fusion), channel_id=1, source_target_pairs={{0,1},{1,0},{2,3},{3,2},{4,5},{5,4},{6,7},{7,6},{16,17},{17,16},{1... | collective-permute-start | bytes 98312 | tf_op jit(solution)/shard_map/ppermute | solution.py:462
  36.9 5.6 %collective-permute-start.6 = (bf16[64,256]{1,0:T(8,128)(2,1)S(1)}, bf16[64,256]{1,0:T(8,128)(2,1)S(1)}, u32[]{:S(2)}, u32[]{:S(2)}) collective-permute-start(bf16[64,256]{1,0:T(8,128)(2,1)S(1)} %pad_maximum_fusion.12), channel_id=1, source_target_pairs={{8,136},{24,152},{40,168},{56,184},{72,200},{88,216},{104,232},{12... | collective-permute-start | bytes 98312 | tf_op jit(solution)/shard_map/ppermute | solution.py:457
  42.5 5.0 %collective-permute-start.8 = (bf16[128,256]{1,0:T(8,128)(2,1)S(1)}, bf16[128,256]{1,0:T(8,128)(2,1)S(1)}, u32[]{:S(2)}, u32[]{:S(2)}) collective-permute-start(bf16[128,256]{1,0:T(8,128)(2,1)S(1)} %pad_maximum_fusion.9), channel_id=1, source_target_pairs={{8,72},{24,88},{40,104},{56,120},{72,8},{88,24},{104,40},{120,56},... | collective-permute-start | bytes 196616 | tf_op jit(solution)/shard_map/ppermute | solution.py:457
  47.5 7.2 %collective-permute-start.9 = (bf16[256,256]{1,0:T(8,128)(2,1)S(1)}, bf16[256,256]{1,0:T(8,128)(2,1)S(1)}, u32[]{:S(2)}, u32[]{:S(2)}) collective-permute-start(bf16[256,256]{1,0:T(8,128)(2,1)S(1)} %pad_maximum_fusion.7), channel_id=1, source_target_pairs={{8,40},{24,56},{40,8},{56,24},{72,104},{88,120},{104,72},{120,88},... | collective-permute-start | bytes 393224 | tf_op jit(solution)/shard_map/ppermute | solution.py:457
  54.7 7.1 %collective-permute-start.10 = (bf16[512,256]{1,0:T(8,128)(2,1)S(1)}, bf16[512,256]{1,0:T(8,128)(2,1)S(1)}, u32[]{:S(2)}, u32[]{:S(2)}) collective-permute-start(bf16[512,256]{1,0:T(8,128)(2,1)S(1)} %pad_maximum_fusion.5), channel_id=1, source_target_pairs={{8,24},{24,8},{40,56},{56,40},{72,88},{88,72},{104,120},{120,104},... | collective-permute-start | bytes 786440 | tf_op jit(solution)/shard_map/ppermute | solution.py:457
  57.8 0.7 collective-permute-start.11
  58.5 3.4 %collective-permute-start.12 = (f32[112,128]{1,0:T(8,128)S(1)}, f32[112,128]{1,0:T(8,128)S(1)}, u32[]{:S(2)}, u32[]{:S(2)}) collective-permute-start(f32[112,128]{1,0:T(8,128)S(1)} %pad_maximum_fusion.10), channel_id=1, source_target_pairs={{0,8},{16,24},{32,40},{48,56},{64,72},{80,88},{96,104},{112,120},{... | collective-permute-start | bytes 172040 | tf_op jit(solution)/shard_map/ppermute | solution.py:466
  61.9 29.8 %collective-permute-start.19 = (bf16[1024,256]{1,0:T(8,128)(2,1)S(1)}, bf16[1024,256]{1,0:T(8,128)(2,1)S(1)}, u32[]{:S(2)}, u32[]{:S(2)}) collective-permute-start(bf16[1024,256]{1,0:T(8,128)(2,1)S(1)} %pad_maximum_fusion.1.far_all), channel_id=1, source_target_pairs={{8,0},{24,16},{40,32},{56,48},{72,64},{88,80},{104,96},{120,112},{... | collective-permute-start | bytes 1572872 | tf_op jit(solution)/shard_map/ppermute | solution.py:470
  64.9 7.2 %collective-permute-start.13 = (bf16[64,384]{1,0:T(8,128)(2,1)S(1)}, bf16[64,384]{1,0:T(8,128)(2,1)S(1)}, u32[]{:S(2)}, u32[]{:S(2)}) collective-permute-start(bf16[64,384]{1,0:T(8,128)(2,1)S(1)} %get-tuple-element.89.packs_own), channel_id=1, source_target_pairs={{8,0},{24,16},{40,32},{56,48},{72,64},{88,80},{104,96},{120,112},{... | collective-permute-start | bytes 147464 | tf_op jit(solution)/shard_map/ppermute | solution.py:470
  66.2 5.9 %collective-permute-start.14 = (f32[8,128]{1,0:T(8,128)S(1)}, f32[8,128]{1,0:T(8,128)S(1)}, u32[]{:S(2)}, u32[]{:S(2)}) collective-permute-start(f32[8,128]{1,0:T(8,128)S(1)} %get-tuple-element.90), channel_id=1, source_target_pairs={{8,10},{9,11},{10,8},{11,9},{12,14},{13,15},{14,12},{15,13},{24,26... | collective-permute-start | bytes 12296 | tf_op jit(solution)/shard_map/ppermute | solution.py:462
  72.1 5.0 %collective-permute-start.15 = (bf16[32,384]{1,0:T(8,128)(2,1)S(1)}, bf16[32,384]{1,0:T(8,128)(2,1)S(1)}, u32[]{:S(2)}, u32[]{:S(2)}) collective-permute-start(bf16[32,384]{1,0:T(8,128)(2,1)S(1)} %slice.17), channel_id=1, source_target_pairs={{0,256},{16,272},{32,288},{48,304},{64,320},{80,336},{96,352},{112... | collective-permute-start | bytes 73736 | tf_op jit(solution)/shard_map/ppermute | solution.py:457
  72.8 4.4 %collective-permute-start.16 = (f32[8,128]{1,0:T(8,128)S(1)}, f32[8,128]{1,0:T(8,128)S(1)}, u32[]{:S(2)}, u32[]{:S(2)}) collective-permute-start(f32[8,128]{1,0:T(8,128)S(1)} %add.21), channel_id=1, source_target_pairs={{8,9},{9,8},{10,11},{11,10},{12,13},{13,12},{14,15},{15,14},{24,25... | collective-permute-start | bytes 12296 | tf_op jit(solution)/shard_map/ppermute | solution.py:462
  77.1 13.8 %collective-permute-start.17 = (bf16[64,384]{1,0:T(8,128)(2,1)S(1)}, bf16[64,384]{1,0:T(8,128)(2,1)S(1)}, u32[]{:S(2)}, u32[]{:S(2)}) collective-permute-start(bf16[64,384]{1,0:T(8,128)(2,1)S(1)} %pad_maximum_fusion.11), channel_id=1, source_target_pairs={{0,128},{16,144},{32,160},{48,176},{64,192},{80,208},{96,224},{112... | collective-permute-start | bytes 147464 | tf_op jit(solution)/shard_map/ppermute | solution.py:457
  77.8 13.2 %collective-permute-start.18 = (f32[8,128]{1,0:T(8,128)S(1)}, f32[8,128]{1,0:T(8,128)S(1)}, u32[]{:S(2)}, u32[]{:S(2)}) collective-permute-start(f32[8,128]{1,0:T(8,128)S(1)} %add.22), channel_id=1, source_target_pairs={{8,12},{9,13},{10,14},{11,15},{12,8},{13,9},{14,10},{15,11},{24,28... | collective-permute-start | bytes 12296 | tf_op jit(solution)/shard_map/ppermute | solution.py:462
  91.0 1.3 %collective-permute-start.20 = (bf16[128,384]{1,0:T(8,128)(2,1)S(1)}, bf16[128,384]{1,0:T(8,128)(2,1)S(1)}, u32[]{:S(2)}, u32[]{:S(2)}) collective-permute-start(bf16[128,384]{1,0:T(8,128)(2,1)S(1)} %pad_maximum_fusion.8), channel_id=1, source_target_pairs={{0,64},{16,80},{32,96},{48,112},{64,0},{80,16},{96,32},{112,48},{1... | collective-permute-start | bytes 294920 | tf_op jit(solution)/shard_map/ppermute | solution.py:457
  92.3 9.3 %collective-permute-start.23 = (bf16[256,384]{1,0:T(8,128)(2,1)S(1)}, bf16[256,384]{1,0:T(8,128)(2,1)S(1)}, u32[]{:S(2)}, u32[]{:S(2)}) collective-permute-start(bf16[256,384]{1,0:T(8,128)(2,1)S(1)} %constant_dynamic-update-slice_fusion.2), channel_id=1, source_target_pairs={{0,32},{16,48},{32,0},{48,16},{64,96},{80,112},{96,64},{112,80},{1... | collective-permute-start | bytes 589832 | tf_op jit(solution)/shard_map/ppermute | solution.py:457
  93.0 3.1 %collective-permute-start.21 = (f32[8,128]{1,0:T(8,128)S(1)}, f32[8,128]{1,0:T(8,128)S(1)}, u32[]{:S(2)}, u32[]{:S(2)}) collective-permute-start(f32[8,128]{1,0:T(8,128)S(1)} %add.23.fix_own), channel_id=1, source_target_pairs={{8,0},{24,16},{40,32},{56,48},{72,64},{88,80},{104,96},{120,112},{... | collective-permute-start | bytes 12296 | tf_op jit(solution)/shard_map/ppermute | solution.py:470
  96.1 9.8 %copy-start.5 = (bf16[1024,256]{1,0:T(8,128)(2,1)S(1)}, bf16[1024,256]{1,0:T(8,128)(2,1)}, u32[]{:S(2)}) copy-start(bf16[1024,256]{1,0:T(8,128)(2,1)} %v_ref.9) | copy-start | bytes 1572868
  99.2 6.8 %copy-start.1 = (bf16[1024,256]{1,0:T(8,128)(2,1)S(1)}, bf16[1024,256]{1,0:T(8,128)(2,1)}, u32[]{:S(2)}) copy-start(bf16[1024,256]{1,0:T(8,128)(2,1)} %q_ref.9) | copy-start | bytes 1572868
  99.2 6.8 %copy-start.3 = (bf16[1024,256]{1,0:T(8,128)(2,1)S(1)}, bf16[1024,256]{1,0:T(8,128)(2,1)}, u32[]{:S(2)}) copy-start(bf16[1024,256]{1,0:T(8,128)(2,1)} %k_ref.9) | copy-start | bytes 1572868
  99.2 6.8 %collective-permute-start.22 = (bf16[256,256]{1,0:T(8,128)(2,1)S(1)}, bf16[256,256]{1,0:T(8,128)(2,1)S(1)}, u32[]{:S(2)}, u32[]{:S(2)}) collective-permute-start(bf16[256,256]{1,0:T(8,128)(2,1)S(1)} %get-tuple-element.102.mid_g), channel_id=1, source_target_pairs={{0,16},{8,24},{16,0},{24,8},{32,48},{40,56},{48,32},{56,40},{64,80... | collective-permute-start | bytes 393224 | tf_op jit(solution)/shard_map/ppermute | solution.py:453
  101.6 8.6 %collective-permute-start.24 = (bf16[512,384]{1,0:T(8,128)(2,1)S(1)}, bf16[512,384]{1,0:T(8,128)(2,1)S(1)}, u32[]{:S(2)}, u32[]{:S(2)}) collective-permute-start(bf16[512,384]{1,0:T(8,128)(2,1)S(1)} %pad_maximum_fusion.4), channel_id=1, source_target_pairs={{0,16},{16,0},{32,48},{48,32},{64,80},{80,64},{96,112},{112,96},{1... | collective-permute-start | bytes 1179656 | tf_op jit(solution)/shard_map/ppermute | solution.py:457
  110.3 5.4 %collective-permute-start.26 = (bf16[512,256]{1,0:T(8,128)(2,1)S(1)}, bf16[512,256]{1,0:T(8,128)(2,1)S(1)}, u32[]{:S(2)}, u32[]{:S(2)}) collective-permute-start(bf16[512,256]{1,0:T(8,128)(2,1)S(1)} %pad_maximum_fusion.6), channel_id=1, source_target_pairs={{0,8},{8,0},{16,24},{24,16},{32,40},{40,32},{48,56},{56,48},{64,72... | collective-permute-start | bytes 786440 | tf_op jit(solution)/shard_map/ppermute | solution.py:453
  114.5 3.1 %collective-permute-start.25 = (f32[96,128]{1,0:T(8,128)S(1)}, f32[96,128]{1,0:T(8,128)S(1)}, u32[]{:S(2)}, u32[]{:S(2)}) collective-permute-start(f32[96,128]{1,0:T(8,128)S(1)} %far_key.1.far_own), channel_id=1, source_target_pairs={{0,8},{16,24},{32,40},{48,56},{64,72},{80,88},{96,104},{112,120},{... | collective-permute-start | bytes 147464 | tf_op jit(solution)/shard_map/ppermute | solution.py:466
  (2 other events, 2.1 us)
